TPU v7x, 32 devices: a whole 2x2x4 slice. The times are simulated.
32 devices in a mesh: cams: 32 (over z, y, x, core).
Axes of the slice: x: 2, y: 2, z: 4, core: 2. Of those that a mesh axis runs over, the one named last changes fastest.
Arguments:
- right_side: float32 [128, 288], P('cams')
- schur_tiles: float32 [128, 4, 288, 288], P('cams')
- block_cols: int32 [128, 4], P('cams'), may hold values from 0 to 127, as said below
- tile_counts: int32 [128], P('cams'), may hold values from 1 to 4, as said below
- jacobi_inverse: float32 [128, 288, 288], P('cams'), as said below
Outputs:
- camera_update: float32 [128, 288], P('cams')
- final_residual: float32 [128, 288], P('cams')
Inputs may be any that keep to these rules, and one draw needn't show every extreme that they name: block_cols[g, 0] = g; the other slots of row g hold distinct blocks (g + o) mod 128 with 1 <= o <= 8. `tile_counts`: slot 0 is always live; some block row has all 4 slots live. `jacobi_inverse`: every tile is symmetric positive definite.
All inputs are finite; a program needn't handle non-finite values.
Results may differ from a plain program's by a relative error of at most 0.00025.
Values sent between devices are 32-bit elements; how exact they have to be, the bound alone decides.
No kernel may reach another device: no remote copies, remote signals or barrier semaphores. Data moves between devices by JAX's collectives and lax.ppermute only.
A program may use at most 64 MiB of HBM per device.

v0:
```python
import jax
import jax.numpy as jnp
from jax import lax
from jax.sharding import PartitionSpec as P

BAND = 2
ITERS = 2


HIGH = lax.Precision.HIGHEST


def shifted(value, axis, steps):
    count = lax.axis_size(axis)
    pairs = [(source, (source + steps) % count) for source in range(count)]
    return lax.ppermute(value, axis, pairs)


def apply_schur(schur_tiles, block_cols, tile_counts, vector):
    blocks, slots = block_cols.shape
    slot_ids = lax.broadcasted_iota(jnp.int32, (blocks, slots), 1)
    live = slot_ids < tile_counts[:, None]
    transposed = live & (slot_ids > 0)
    offset = lax.axis_index("cams") * blocks
    total = blocks * lax.axis_size("cams")
    pieces = [vector]
    for distance in range(1, BAND + 1):
        pieces.append(shifted(vector, "cams", -distance))
    extended = jnp.concatenate(pieces, axis=0)
    local = (block_cols - offset) % total
    picked = extended[local]
    upper = jnp.einsum("bsij,bsj->bsi", schur_tiles, picked, precision=HIGH)
    result = jnp.sum(jnp.where(live[:, :, None], upper, 0.0), axis=1)
    lower = jnp.einsum("bsij,bi->bsj", schur_tiles, vector, precision=HIGH)
    lower = jnp.where(transposed[:, :, None], lower, 0.0)
    targets = extended.shape[0]
    onehot = (
        local.reshape(-1)[:, None] == lax.broadcasted_iota(jnp.int32, (1, targets), 1)
    ).astype(jnp.float32)
    spread = jnp.einsum("rt,rj->tj", onehot, lower.reshape(blocks * slots, -1), precision=HIGH)
    result = result + spread[:blocks]
    for distance in range(1, BAND + 1):
        result = result + shifted(
            spread[distance * blocks : (distance + 1) * blocks], "cams", distance
        )
    return result


def apply_precond(jacobi_inverse, vector):
    return jnp.einsum("bij,bj->bi", jacobi_inverse, vector, precision=HIGH)


def paired(residual, precond, image):
    return lax.psum((jnp.sum(residual * precond), jnp.sum(image * precond)), "cams")


def on_device(right_side, schur_tiles, block_cols, tile_counts, jacobi_inverse):
    camera_update = jnp.zeros_like(right_side)
    final_residual = right_side
    precond = apply_precond(jacobi_inverse, final_residual)
    image = apply_schur(schur_tiles, block_cols, tile_counts, precond)
    norm_now, product = paired(final_residual, precond, image)
    alpha = norm_now / product
    direction, along = (precond, image)
    for iteration in range(ITERS):
        camera_update = camera_update + alpha * direction
        final_residual = final_residual - alpha * along
        if iteration + 1 < ITERS:
            precond = apply_precond(jacobi_inverse, final_residual)
            image = apply_schur(schur_tiles, block_cols, tile_counts, precond)
            fresh, product = paired(final_residual, precond, image)
            ratio = fresh / norm_now
            alpha = fresh / (product - ratio * fresh / alpha)
            direction = precond + ratio * direction
            along = image + ratio * along
            norm_now = fresh
    return (camera_update, final_residual)


def solution(mesh):
    placed = (
        P("cams", None),
        P("cams", None, None, None),
        P("cams", None),
        P("cams"),
        P("cams", None, None),
    )
    return jax.shard_map(
        on_device,
        mesh=mesh,
        in_specs=placed,
        out_specs=(P("cams", None), P("cams", None)),
        check_vma=False,
    )
```

profile of v0, /device:TPU:0, one launch (start us, length us, event | category | flops | bytes accessed | tf_op | source)
XLA Modules:
  0.0 139.1 jit_solution(17939874473240312673)
XLA Ops:
  0.6 1.5 %copy-done = f32[4,288,288]{2,1,0:T(8,128)S(1)} copy-done((f32[4,288,288]{2,1,0:T(8,128)S(1)}, f32[4,288,288]{2,1,0:T(8,128)}, u32[]{:S(2)}) %copy-start) | copy-done | bytes 1327128
  2.1 2.3 %fusion.14 = f32[4,1,288]{2,1,0:T(1,128)S(1)} fusion(f32[4,288,288]{2,1,0:T(8,128)S(1)} %copy-done, f32[4,288,1]{1,0,2:T(4,128)} %bitcast.49), kind=kOutput, calls=%fused_computation.25 | convolution fusion | flops 3981312 | bytes 1336320 | tf_op jit(solution)/shard_map/bij,bj->bi/dot_general | solution.py:50
  4.5 6.4 %collective-permute-start = (f32[4,288]{1,0:T(4,128)S(1)}, f32[4,288]{1,0:T(4,128)S(1)}, u32[]{:S(2)}, u32[]{:S(2)}) collective-permute-start(f32[4,288]{1,0:T(4,128)S(1)} %bitcast.50), channel_id=1, source_target_pairs={{0,31},{1,0},{2,1},{3,2},{4,3},{5,4},{6,5},{7,6},{8,7},{9,8},{10,9... | collective-permute-start | bytes 13832 | tf_op jit(solution)/shard_map/ppermute | solution.py:16
  10.9 0.6 collective-permute-start.1
  11.5 0.7 compare_select_fusion
  12.3 0.7 iota_compare_fusion.3
  13.0 5.7 %fusion.12 = f32[4,1,4,288]{3,1,2,0:T(1,128)S(1)} fusion(f32[4,4,288,288]{3,2,1,0:T(8,128)} %param.6, f32[4,288,1,1]{1,0,2,3:T(4,128)S(1)} %bitcast.52), kind=kOutput, calls=%fused_computation.23 | convolution fusion | flops 15925248 | bytes 5331456 | tf_op jit(solution)/shard_map/bsij,bi->bsj/dot_general | solution.py:34
  18.8 0.3 fusion.3
  19.1 0.2 collective-permute-start.2
  19.3 1.3 collective-permute-start.3
  20.7 0.6 gather_fusion
  21.3 8.2 %fusion.24 = f32[4,4,1,288]{3,2,1,0:T(1,128)S(1)} fusion(f32[4,4,288,1]{2,3,1,0:T(1,128)S(1)} %reshape.94, f32[4,4,288,288]{3,2,1,0:T(8,128)} %param.6), kind=kOutput, calls=%fused_computation.52 | convolution fusion | flops 15925248 | bytes 5345280 | tf_op jit(solution)/shard_map/bsij,bsj->bsi/dot_general | solution.py:32
  29.7 0.6 multiply_reduce_fusion.2
  30.3 39.0 %all-reduce.1 = (f32[]{:T(128)}, f32[]{:T(128)}) all-reduce(f32[]{:T(128)} %get-tuple-element.5, f32[]{:T(128)} %get-tuple-element.4), channel_id=1, replica_groups=mesh['cams'=32] {'cams'}, use_global_device_ids=true, to_apply=%region_1.2 | all-reduce | flops 2 | bytes 16 | tf_op jit(solution)/shard_map/psum | solution.py:54
  70.6 1.6 %fusion.10 = f32[4,1,288]{2,1,0:T(1,128)S(1)} fusion(f32[4,288,288]{2,1,0:T(8,128)S(1)} %copy-done, f32[4,288,1]{1,0,2:T(4,128)S(1)} %fusion.19), kind=kOutput, calls=%fused_computation.21 | convolution fusion | flops 3981312 | bytes 1336320 | tf_op jit(solution)/shard_map/bij,bj->bi/dot_general | solution.py:50
  72.3 2.1 %collective-permute-start.4 = (f32[4,288]{1,0:T(4,128)S(1)}, f32[4,288]{1,0:T(4,128)S(1)}, u32[]{:S(2)}, u32[]{:S(2)}) collective-permute-start(f32[4,288]{1,0:T(4,128)S(1)} %bitcast.54), channel_id=1, source_target_pairs={{0,31},{1,0},{2,1},{3,2},{4,3},{5,4},{6,5},{7,6},{8,7},{9,8},{10,9... | collective-permute-start | bytes 13832 | tf_op jit(solution)/shard_map/ppermute | solution.py:16
  74.3 2.0 %collective-permute-start.5 = (f32[4,288]{1,0:T(4,128)S(1)}, f32[4,288]{1,0:T(4,128)S(1)}, u32[]{:S(2)}, u32[]{:S(2)}) collective-permute-start(f32[4,288]{1,0:T(4,128)S(1)} %bitcast.55), channel_id=1, source_target_pairs={{0,30},{1,31},{2,0},{3,1},{4,2},{5,3},{6,4},{7,5},{8,6},{9,7},{10,... | collective-permute-start | bytes 13832 | tf_op jit(solution)/shard_map/ppermute | solution.py:16
  76.3 5.7 %fusion.8 = f32[4,1,4,288]{3,1,2,0:T(1,128)S(1)} fusion(f32[4,4,288,288]{3,2,1,0:T(8,128)} %param.6, f32[4,288,1,1]{1,0,2,3:T(4,128)S(1)} %bitcast.56), kind=kOutput, calls=%fused_computation.19 | convolution fusion | flops 15925248 | bytes 5331456 | tf_op jit(solution)/shard_map/bsij,bi->bsj/dot_general | solution.py:34
  82.1 0.3 fusion.2
  82.8 0.6 gather_fusion.1
  83.4 8.2 %fusion.25 = f32[4,4,1,288]{3,2,1,0:T(1,128)S(1)} fusion(f32[4,4,288,1]{2,3,1,0:T(1,128)S(1)} %reshape.96, f32[4,4,288,288]{3,2,1,0:T(8,128)} %param.6), kind=kOutput, calls=%fused_computation.53 | convolution fusion | flops 15925248 | bytes 5345280 | tf_op jit(solution)/shard_map/bsij,bsj->bsi/dot_general | solution.py:32
  91.7 0.7 multiply_reduce_fusion
  92.4 41.6 %all-reduce = (f32[]{:T(128)}, f32[]{:T(128)}) all-reduce(f32[]{:T(128)} %get-tuple-element.3, f32[]{:T(128)} %get-tuple-element.2), channel_id=1, replica_groups=mesh['cams'=32] {'cams'}, use_global_device_ids=true, to_apply=%region_6.7 | all-reduce | flops 2 | bytes 16 | tf_op jit(solution)/shard_map/psum | solution.py:54
  138.5 0.6 multiply_subtract_fusion
  (32 shorter events, 1.1 us)
Async XLA Ops:
  0.6 1.5 %copy-start = (f32[4,288,288]{2,1,0:T(8,128)S(1)}, f32[4,288,288]{2,1,0:T(8,128)}, u32[]{:S(2)}) copy-start(f32[4,288,288]{2,1,0:T(8,128)} %param.9) | copy-start | bytes 3981316
  4.5 16.2 %collective-permute-start = (f32[4,288]{1,0:T(4,128)S(1)}, f32[4,288]{1,0:T(4,128)S(1)}, u32[]{:S(2)}, u32[]{:S(2)}) collective-permute-start(f32[4,288]{1,0:T(4,128)S(1)} %bitcast.50), channel_id=1, source_target_pairs={{0,31},{1,0},{2,1},{3,2},{4,3},{5,4},{6,5},{7,6},{8,7},{9,8},{10,9... | collective-permute-start | bytes 13832 | tf_op jit(solution)/shard_map/ppermute | solution.py:16
  10.9 9.8 %collective-permute-start.1 = (f32[4,288]{1,0:T(4,128)S(1)}, f32[4,288]{1,0:T(4,128)S(1)}, u32[]{:S(2)}, u32[]{:S(2)}) collective-permute-start(f32[4,288]{1,0:T(4,128)S(1)} %bitcast.51), channel_id=1, source_target_pairs={{0,30},{1,31},{2,0},{3,1},{4,2},{5,3},{6,4},{7,5},{8,6},{9,7},{10,... | collective-permute-start | bytes 13832 | tf_op jit(solution)/shard_map/ppermute | solution.py:16
  13.0 16.7 %copy-start.1 = (f32[4,288]{1,0:T(4,128)S(1)}, f32[4,288]{1,0:T(4,128)}, u32[]{:S(2)}) copy-start(f32[4,288]{1,0:T(4,128)} %param.5) | copy-start | bytes 13828
  19.1 10.6 %collective-permute-start.2 = (f32[4,288]{1,0:T(4,128)S(1)}, f32[4,288]{1,0:T(4,128)S(1)}, u32[]{:S(2)}, u32[]{:S(2)}) collective-permute-start(f32[4,288]{1,0:T(4,128)S(1)} %get-tuple-element.16), channel_id=1, source_target_pairs={{0,1},{1,2},{2,3},{3,4},{4,5},{5,6},{6,7},{7,8},{8,9},{9,10},{10,1... | collective-permute-start | bytes 13832 | tf_op jit(solution)/shard_map/ppermute | solution.py:16
  19.3 10.4 %collective-permute-start.3 = (f32[4,288]{1,0:T(4,128)S(1)}, f32[4,288]{1,0:T(4,128)S(1)}, u32[]{:S(2)}, u32[]{:S(2)}) collective-permute-start(f32[4,288]{1,0:T(4,128)S(1)} %get-tuple-element.17), channel_id=1, source_target_pairs={{0,2},{1,3},{2,4},{3,5},{4,6},{5,7},{6,8},{7,9},{8,10},{9,11},{10,... | collective-permute-start | bytes 13832 | tf_op jit(solution)/shard_map/ppermute | solution.py:16
  72.3 10.5 %collective-permute-start.4 = (f32[4,288]{1,0:T(4,128)S(1)}, f32[4,288]{1,0:T(4,128)S(1)}, u32[]{:S(2)}, u32[]{:S(2)}) collective-permute-start(f32[4,288]{1,0:T(4,128)S(1)} %bitcast.54), channel_id=1, source_target_pairs={{0,31},{1,0},{2,1},{3,2},{4,3},{5,4},{6,5},{7,6},{8,7},{9,8},{10,9... | collective-permute-start | bytes 13832 | tf_op jit(solution)/shard_map/ppermute | solution.py:16
  74.3 8.4 %collective-permute-start.5 = (f32[4,288]{1,0:T(4,128)S(1)}, f32[4,288]{1,0:T(4,128)S(1)}, u32[]{:S(2)}, u32[]{:S(2)}) collective-permute-start(f32[4,288]{1,0:T(4,128)S(1)} %bitcast.55), channel_id=1, source_target_pairs={{0,30},{1,31},{2,0},{3,1},{4,2},{5,3},{6,4},{7,5},{8,6},{9,7},{10,... | collective-permute-start | bytes 13832 | tf_op jit(solution)/shard_map/ppermute | solution.py:16
  82.4 9.3 %collective-permute-start.6 = (f32[4,288]{1,0:T(4,128)S(1)}, f32[4,288]{1,0:T(4,128)S(1)}, u32[]{:S(2)}, u32[]{:S(2)}) collective-permute-start(f32[4,288]{1,0:T(4,128)S(1)} %get-tuple-element.14), channel_id=1, source_target_pairs={{0,1},{1,2},{2,3},{3,4},{4,5},{5,6},{6,7},{7,8},{8,9},{9,10},{10,1... | collective-permute-start | bytes 13832 | tf_op jit(solution)/shard_map/ppermute | solution.py:16
  82.6 9.1 %collective-permute-start.7 = (f32[4,288]{1,0:T(4,128)S(1)}, f32[4,288]{1,0:T(4,128)S(1)}, u32[]{:S(2)}, u32[]{:S(2)}) collective-permute-start(f32[4,288]{1,0:T(4,128)S(1)} %get-tuple-element.15), channel_id=1, source_target_pairs={{0,2},{1,3},{2,4},{3,5},{4,6},{5,7},{6,8},{7,9},{8,10},{9,11},{10,... | collective-permute-start | bytes 13832 | tf_op jit(solution)/shard_map/ppermute | solution.py:16
where the time goes:
time: 140 us; the launch traced here: 139 us
  blocking collectives  80.5 us (58%)
  matrix products  32.3 us (23%)
  starting transfers between devices  13 us (9%)
  between operations  6.67 us (5%)
  other arithmetic  3.73 us (3%)
  local copies, waits for them, and re-layouts  2.91 us (2%)
    psum x2, blocking collectives, paired(): lax.psum((jnp.sum(residual * precond), jnp.sum(image * precond)), 'cams')  80.5 us
    dot_general x2, matrix products, apply_schur(): upper = jnp.einsum('bsij,bsj->bsi', schur_tiles, picked, precision=HIGH)  16.4 us
    ppermute x8, starting transfers between devices, shifted(): return lax.ppermute(value, axis, pairs)  13 us
    dot_general x2, matrix products, apply_schur(): lower = jnp.einsum('bsij,bi->bsj', schur_tiles, vector, precision=HIGH)  11.4 us
    dot_general x2, matrix products, apply_precond(): return jnp.einsum('bij,bj->bi', jacobi_inverse, vector, precision=HIGH)  3.95 us
  transfers between devices with their start and end apart: 8, of which 0 were waited for; matrix products, arithmetic and copies ran while one was open for 23% of the time, Pallas kernels for 0%

commit v1 on v0

v1 whole, which is shorter than its diff:
```python
import functools

import jax
import jax.numpy as jnp
from jax import lax
from jax.experimental import pallas as pl
from jax.experimental.pallas import tpu as pltpu
from jax.sharding import PartitionSpec as P

AXIS = "cams"
BAND = 2
F32 = jnp.float32
VMEM_LIMIT = 40 * 2**20
TINY = 1e-30


def padded(width):
    return -(-width // 128) * 128


def iota(shape, dim):
    return lax.broadcasted_iota(jnp.int32, shape, dim)


def total(value):
    return jnp.sum(jnp.sum(value, axis=1, keepdims=True), axis=0, keepdims=True)


def lay_scalars(values, lanes, first):
    lane = iota((1, lanes), 1)
    row = jnp.zeros((1, lanes), F32)
    for i, value in enumerate(values):
        row = jnp.where(lane == first + i, value, row)
    return row


def columns_to_row(columns, width):
    lanes = padded(width)
    skew = iota((8, 128), 1) - iota((8, 128), 0)
    parts = [jnp.zeros((8, 128), F32) for _ in range(lanes // 128)]
    for i, piece in enumerate(columns):
        tile, lane = divmod(8 * i, 128)
        parts[tile] = parts[tile] + jnp.where(skew == lane, piece, 0.0)
    return jnp.sum(jnp.concatenate(parts, axis=1), axis=0, keepdims=True)


def times_row(load, row, width):
    wide = jnp.broadcast_to(row[:, :width], (8, width))
    return [
        jnp.sum(load(i) * wide, axis=1, keepdims=True) for i in range(width // 8)
    ]


def transposed_products(tiles, group, columns, slots, width):
    sums = [jnp.zeros((8, width), F32) for _ in range(slots)]
    for i, piece in enumerate(columns):
        for slot in range(slots):
            sums[slot] = sums[slot] + tiles[group, slot, 8 * i : 8 * i + 8, :] * piece
    return sums


def scatter_products(tiles, place, live, group, columns, slots, width, own, spread):
    products = transposed_products(tiles, group, columns, slots, width)
    own[group, :, :width] = products[0]
    for slot in range(1, slots):
        where = place[group, slot]
        kept = jnp.where(live[group, slot] > 0, products[slot], 0.0)
        spread[where, :, :width] = spread[where, :, :width] + kept


def upper_columns(tiles, place, live, wide, group, slots, width):
    rows = []
    for slot in range(1, slots):
        row = wide[place[group, slot], :, :width]
        rows.append(jnp.where(live[group, slot] > 0, row, 0.0))
    pieces = []
    for i in range(width // 8):
        part = tiles[group, 1, 8 * i : 8 * i + 8, :] * rows[0]
        for slot in range(2, slots):
            part = part + tiles[group, slot, 8 * i : 8 * i + 8, :] * rows[slot - 1]
        pieces.append(jnp.sum(part, axis=1, keepdims=True))
    return pieces


def position():
    me = lax.axis_index(AXIS)
    chip = me // 2
    return chip, (me - 2 * chip) == 1, (chip - 2 * (chip // 2)) == 1


def begin_kernel(blocks, slots, width, count,
                 cols, counts, right, tiles_hbm, jacobi_hbm,
                 tiles, jacobi, place, live, swap, far, near,
                 own, spread, tile_sem, jacobi_sem):
    lanes = padded(width)
    loads = []
    for g in range(blocks):
        first = pltpu.make_async_copy(jacobi_hbm.at[g], jacobi.at[g], jacobi_sem.at[g])
        second = pltpu.make_async_copy(tiles_hbm.at[g], tiles.at[g], tile_sem.at[g])
        first.start()
        second.start()
        loads.append((first, second))
    base = lax.axis_index(AXIS) * blocks
    for g in range(blocks):
        for k in range(slots):
            ahead = cols[g, k] - base
            ahead = jnp.where(ahead < 0, ahead + count * blocks, ahead)
            place[g, k] = jnp.clip(ahead, 0, (BAND + 1) * blocks - 1)
            live[g, k] = (k < counts[g]).astype(jnp.int32)
    spread[...] = jnp.zeros_like(spread)
    own[...] = jnp.zeros_like(own)
    for g in range(blocks):
        loads[g][0].wait()
        columns = times_row(
            lambda i: jacobi[g, 8 * i : 8 * i + 8, :], right[g : g + 1, :], width
        )
        swap[g : g + 1, :] = columns_to_row(columns, width)
        loads[g][1].wait()
        scatter_products(tiles, place, live, g, columns, slots, width, own, spread)
    sums = jnp.sum(spread[...], axis=1)
    swap[blocks : 2 * blocks, :] = sums[blocks : 2 * blocks]
    far[...] = sums[2 * blocks :]
    near[...] = sums[:blocks] + jnp.sum(own[...], axis=1)


def pack_kernel(blocks, swap, swapped, far, odd_out, even_out):
    _, second, odd = position()
    rows, other = swap[...], swapped[...]
    forward = far[...] + jnp.where(second, 0.0, other[blocks:])
    forward = jnp.concatenate([forward, jnp.zeros_like(forward)], axis=0)
    backward = jnp.concatenate([rows[:blocks], other[:blocks]], axis=0)
    odd_out[...] = jnp.where(odd, forward, backward)
    even_out[...] = jnp.where(odd, backward, forward)


def spread_rows(wide, rows, first):
    for i in range(rows.shape[0]):
        wide[first + i, :, :] = jnp.broadcast_to(rows[i : i + 1], wide.shape[1:])


def middle_kernel(blocks, slots, width,
                  place, live, right, tiles, jacobi, swap, swapped, odd_in, even_in, near,
                  image, swap_out, far, near_out, wide, own, spread):
    lanes = padded(width)
    _, second, odd = position()
    rows, other = swap[...], swapped[...]
    ahead = jnp.where(odd, odd_in[...], even_in[...])
    behind = jnp.where(odd, even_in[...], odd_in[...])
    spread_rows(wide, rows[:blocks], 0)
    spread_rows(wide, jnp.where(second, ahead[blocks:], other[:blocks]), blocks)
    spread_rows(wide, ahead[:blocks], 2 * blocks)
    spread[...] = jnp.zeros_like(spread)
    own[...] = jnp.zeros_like(own)
    known = near[...] + behind[:blocks] + jnp.where(second, other[blocks:], 0.0)
    for g in range(blocks):
        columns = upper_columns(tiles, place, live, wide, g, slots, width)
        image[g : g + 1, :] = known[g : g + 1] + columns_to_row(columns, width)
    q = image[...]
    size = jnp.max(jnp.max(jnp.abs(q), axis=1, keepdims=True), axis=0, keepdims=True)
    size = jnp.where(size > TINY, size, 1.0)
    scaled = q * (1.0 / size)
    for g in range(blocks):
        columns = times_row(
            lambda i: jacobi[g, 8 * i : 8 * i + 8, :], scaled[g : g + 1, :], width
        )
        swap_out[g : g + 1, :] = columns_to_row(columns, width)
        scatter_products(tiles, place, live, g, columns, slots, width, own, spread)
    sums = jnp.sum(spread[...], axis=1)
    diagonal = jnp.sum(own[...], axis=1)
    w = swap_out[:blocks, :]
    far[...] = sums[2 * blocks :]
    near_out[...] = sums[:blocks] + diagonal
    z = rows[:blocks]
    r = right[...]
    values = [
        size,
        total(r * z[:, :width]),
        total(z * q),
        total(r * w[:, :width]),
        total(scaled * w),
        total(w * (diagonal + 2.0 * sums[:blocks])),
    ]
    swap_out[blocks : 2 * blocks, :] = sums[blocks : 2 * blocks]
    swap_out[0:1, :] = w[0:1] + lay_scalars(values, lanes, width)


def gather_kernel(blocks, width, swap, swapped, far, out):
    lanes = padded(width)
    _, second, _ = position()
    rows, other = swap[...], swapped[...]

    def at(block, i):
        return block[0:1, width + i : width + i + 1]

    lane = iota((1, lanes), 1)
    mine, theirs = at(rows, 0), at(other, 0)
    scale = jnp.where(second, mine, jnp.maximum(mine, theirs))
    sent = far[...] * (mine / scale) + jnp.where(
        second, 0.0, other[blocks:] * (theirs / scale)
    )
    crossing = total(rows[blocks:, :width] * other[:blocks, :width])
    values = [
        mine,
        scale,
        at(rows, 1) + at(other, 1),
        at(rows, 2) + at(other, 2),
        at(rows, 3),
        at(rows, 4),
        at(rows, 2),
        at(rows, 5),
        jnp.where(second, 0.0, 2.0 * crossing),
        theirs,
    ]
    out[...] = jnp.broadcast_to(
        jnp.concatenate([rows[:blocks], sent], axis=0)[None], out.shape
    )
    first = jnp.where(lane < width, rows[0:1], lay_scalars(values, lanes, width))
    out[:, 0:1, :] = jnp.broadcast_to(first[None], (out.shape[0], 1, lanes))


def scalars_of(gathered, width):
    rows = gathered[:, 0:1, :]
    return lambda i: rows[:, :, width + i : width + i + 1]


def chips_total(value):
    return jnp.sum(value, axis=0)


def sums_kernel(blocks, width, gathered, out):
    chips, _, lanes = gathered.shape
    chip, _, _ = position()
    after = jnp.where(chip == chips - 1, 0, chip + 1)
    at = scalars_of(gathered[...], width)
    alpha = chips_total(at(2)) / chips_total(at(3))
    size = alpha[None] * at(0)
    sent = alpha[None] * at(1)
    paired = alpha[None] * at(9)
    fresh = chips_total(size * size * at(5) - size * at(4) - alpha[None] * at(6))
    diagonal = chips_total(
        size * size * at(7) + size * paired * at(8) - 2.0 * (size * at(0)) * at(5)
    )
    inside = (iota((2 * blocks, lanes), 0) >= blocks) & (iota((2 * blocks, lanes), 1) < width)
    edges = jnp.zeros((2 * blocks, lanes), F32)
    for e in range(chips):
        n = (e + 1) % chips
        turned = pltpu.roll(gathered[n] * size[n], blocks, 0)
        edges = edges + gathered[e] * sent[e] * turned
    edges = total(jnp.where(inside, edges, 0.0))
    ahead = gathered[after, :blocks, :] * (alpha * gathered[after, 0:1, width : width + 1])
    out[...] = jnp.zeros_like(out)
    out[:blocks, :] = ahead
    out[0:1, :] = jnp.where(
        iota((1, lanes), 1) < width,
        ahead[0:1],
        lay_scalars([fresh, diagonal + 2.0 * edges], lanes, width),
    )


def end_kernel(blocks, slots, width,
               place, live, right, tiles, first_swap, image, swap, swapped, near, gathered, last, last_swapped,
               update, residual, wide, product):
    chips, _, lanes = gathered.shape
    chip, second, _ = position()
    after = jnp.where(chip == chips - 1, 0, chip + 1)
    before = jnp.where(chip == 0, chips - 1, chip - 1)
    at = scalars_of(gathered[...], width)
    norm = chips_total(at(2))
    along = chips_total(at(3))
    alpha = norm / along
    mine = alpha * swap[0:1, width : width + 1]
    theirs = alpha * swapped[0:1, width : width + 1]
    keep = iota((blocks, lanes), 1) < width
    w = jnp.where(keep, swap[:blocks, :], 0.0) * mine
    w_other = jnp.where(keep, swapped[:blocks, :], 0.0) * theirs
    ahead = last[:blocks, :]
    spread_rows(wide, w, 0)
    spread_rows(wide, jnp.where(second, last_swapped[:blocks, :], w_other), blocks)
    spread_rows(wide, ahead, 2 * blocks)
    known = near[...] * mine
    known = known + gathered[before, blocks:, :] * (
        alpha * gathered[before, 0:1, width + 1 : width + 2]
    )
    known = known + jnp.where(second, swapped[blocks:, :] * theirs, 0.0)
    for g in range(blocks):
        columns = upper_columns(tiles, place, live, wide, g, slots, width)
        product[g : g + 1, :] = known[g : g + 1] + columns_to_row(columns, width)

    def shared(i):
        return last[0:1, width + i : width + i + 1] + last_swapped[0:1, width + i : width + i + 1]

    fresh = norm + shared(0)
    curved = along + shared(1)
    ratio = fresh / norm
    step = fresh / (curved - ratio * (fresh / alpha))
    z = first_swap[:blocks, :]
    q = image[...]
    z_next = z - w
    update[...] = (alpha * z + step * (z_next + ratio * z))[:, :width]
    r_next = right[...] - (alpha * q)[:, :width]
    residual[...] = r_next - (step * ((q - product[...]) + ratio * q))[:, :width]


def on_device(right_side, schur_tiles, block_cols, tile_counts, jacobi_inverse):
    count = lax.axis_size(AXIS)
    blocks, slots, width, _ = schur_tiles.shape
    lanes = padded(width)
    chips = count // 2
    vmem = pl.BlockSpec(memory_space=pltpu.VMEM)
    smem = pl.BlockSpec(memory_space=pltpu.SMEM)
    hbm = pl.BlockSpec(memory_space=pltpu.HBM)
    params = pltpu.CompilerParams(vmem_limit_bytes=VMEM_LIMIT)
    rows = pltpu.VMEM((2 * blocks, lanes), F32)
    half = pltpu.VMEM((blocks, lanes), F32)
    reach = (BAND + 1) * blocks
    spread = pltpu.VMEM((reach, 8, lanes), F32)
    own = pltpu.VMEM((blocks, 8, lanes), F32)
    index = pltpu.SMEM((blocks, slots), jnp.int32)

    def swap_cores(value):
        return lax.ppermute(value, AXIS, [(i, i ^ 1) for i in range(count)])

    def swap_chips(odd, value):
        pairs = []
        for i in range(count):
            chip, core = divmod(i, 2)
            step = 1 if (chip % 2 == 1) == odd else -1
            pairs.append((i, 2 * ((chip + step) % chips) + core))
        return lax.ppermute(value, AXIS, pairs)

    tiles, jacobi, place, live, swap, far, near = pl.pallas_call(
        functools.partial(begin_kernel, blocks, slots, width, count),
        in_specs=[smem, smem, vmem, hbm, hbm],
        out_specs=[vmem, vmem, smem, smem, vmem, vmem, vmem],
        out_shape=[
            pltpu.VMEM(schur_tiles.shape, F32),
            pltpu.VMEM(jacobi_inverse.shape, F32),
            index, index, rows, half, half,
        ],
        scratch_shapes=[
            own, spread,
            pltpu.SemaphoreType.DMA((blocks,)),
            pltpu.SemaphoreType.DMA((blocks,)),
        ],
        compiler_params=params,
    )(block_cols, tile_counts, right_side, schur_tiles, jacobi_inverse)
    swapped = swap_cores(swap)
    odd_out, even_out = pl.pallas_call(
        functools.partial(pack_kernel, blocks),
        in_specs=[vmem] * 3, out_specs=[vmem] * 2, out_shape=[rows, rows],
        compiler_params=params,
    )(swap, swapped, far)
    odd_in = swap_chips(True, odd_out)
    even_in = swap_chips(False, even_out)
    image, swap2, far2, near2 = pl.pallas_call(
        functools.partial(middle_kernel, blocks, slots, width),
        in_specs=[smem, smem] + [vmem] * 8, out_specs=[vmem] * 4,
        out_shape=[half, rows, half, half],
        scratch_shapes=[spread, own, spread],
        compiler_params=params,
    )(place, live, right_side, tiles, jacobi, swap, swapped, odd_in, even_in, near)
    swapped2 = swap_cores(swap2)
    sent = pl.pallas_call(
        functools.partial(gather_kernel, blocks, width),
        in_specs=[vmem] * 3, out_specs=vmem,
        out_shape=pltpu.VMEM((chips, 2 * blocks, lanes), F32),
        compiler_params=params,
    )(swap2, swapped2, far2)
    groups = [[2 * c + core for c in range(chips)] for core in range(2)]
    gathered = lax.all_to_all(sent, AXIS, 0, 0, axis_index_groups=groups)
    last = pl.pallas_call(
        functools.partial(sums_kernel, blocks, width),
        in_specs=[vmem], out_specs=vmem, out_shape=rows,
        compiler_params=params,
    )(gathered)
    last_swapped = swap_cores(last)
    return pl.pallas_call(
        functools.partial(end_kernel, blocks, slots, width),
        in_specs=[smem, smem] + [vmem] * 10, out_specs=[vmem] * 2,
        out_shape=[jax.ShapeDtypeStruct(right_side.shape, F32)] * 2,
        scratch_shapes=[spread, half],
        compiler_params=params,
    )(place, live, right_side, tiles, swap, image, swap2, swapped2, near2, gathered, last, last_swapped)


def solution(mesh):
    placed = (
        P(AXIS, None),
        P(AXIS, None, None, None),
        P(AXIS, None),
        P(AXIS),
        P(AXIS, None, None),
    )
    return jax.shard_map(
        on_device,
        mesh=mesh,
        in_specs=placed,
        out_specs=(P(AXIS, None), P(AXIS, None)),
        check_vma=False,
    )
```

time: 140 us -> 40.1 us (0.29)
  blocking collectives: 80.5 us -> 13.7 us
  matrix products: 32.3 us -> 0 us
  Pallas kernels: 0 us -> 7.61 us
  waiting for transfers between devices: 0.02 us -> 6.85 us
  between operations: 6.67 us -> 0.68 us
  starting transfers between devices: 13 us -> 7.46 us
  other arithmetic: 3.73 us -> 0 us
    psum x2 -> x0, blocking collectives: 80.5 us -> none  [paired(): lax.psum((jnp.sum(residual * precond), jnp.sum(image * precond)), 'cams')]
    dot_general x8 -> x0, matrix products: 32.3 us -> none  [the longest x2 16.4 us: apply_schur(): upper = jnp.einsum('bsij,bsj->bsi', schur_tiles, picked, precision=HIGH)]
    all_to_all x0 -> x1, blocking collectives: none -> 13.7 us  [on_device(): gathered = lax.all_to_all(sent, AXIS, 0, 0, axis_index_groups=groups)]
    pallas_call x0 -> x6, Pallas kernels: none -> 7.61 us  [the longest x1 4.3 us: on_device(): pl.pallas_call(functools.partial(begin_kernel, blocks, slots, width, coun...]
    ppermute x8 -> x5, waiting for transfers between devices: 0.02 us -> 6.85 us  [the longest x2 3.69 us: swap_chips(): return lax.ppermute(value, AXIS, pairs)]
    ppermute x8 -> x5, starting transfers between devices: 13 us -> 7.46 us  [the longest x2 6.89 us: swap_chips(): return lax.ppermute(value, AXIS, pairs)]
    unnamed x4 -> x10, local copies, waits for them, and re-layouts: 1.48 us -> 3.5 us
    reduce_sum x4 -> x0, other arithmetic: 1.51 us -> none  [the longest x2 1.3 us: paired(): jnp.sum(image * precond)]
  transfers between devices with their start and end apart: 8 -> 5, of which waited for: 0 -> 5; matrix products, arithmetic and copies ran while one was open for 23% -> 0% of each run, Pallas kernels for 0% -> 0%
where the time goes in v1:
time: 40.1 us; the launch traced here: 39.8 us
  blocking collectives  13.7 us (34%)
  Pallas kernels  7.61 us (19%)
  starting transfers between devices  7.46 us (19%)
  waiting for transfers between devices  6.85 us (17%)
  local copies, waits for them, and re-layouts  3.5 us (9%)
  between operations  0.68 us (2%)
    all_to_all x1, blocking collectives, on_device(): gathered = lax.all_to_all(sent, AXIS, 0, 0, axis_index_groups=groups)  13.7 us
    ppermute x2, starting transfers between devices, swap_chips(): return lax.ppermute(value, AXIS, pairs)  6.89 us
    pallas_call x1, Pallas kernels, on_device(): pl.pallas_call(functools.partial(begin_kernel, blocks, slots, width, coun...  4.3 us
    ppermute x2, waiting for transfers between devices, swap_chips(): return lax.ppermute(value, AXIS, pairs)  3.69 us
    unnamed x10, local copies, waits for them, and re-layouts  3.5 us
    ppermute x3, waiting for transfers between devices, swap_cores(): return lax.ppermute(value, AXIS, [(i, i ^ 1) for i in range(count)])  3.16 us
    pallas_call x1, Pallas kernels, on_device(): pl.pallas_call(functools.partial(middle_kernel, blocks, slots, width), in...  1.42 us
    pallas_call x1, Pallas kernels, on_device(): pl.pallas_call(functools.partial(end_kernel, blocks, slots, width), in_sp...  1.29 us
  transfers between devices with their start and end apart: 5, of which 5 were waited for; matrix products, arithmetic and copies ran while one was open for 0% of the time, Pallas kernels for 0%

profile of v1, /device:TPU:0, one launch (start us, length us, event | category | flops | bytes accessed | tf_op | source)
XLA Modules:
  0.0 39.8 jit_solution(5627753878566467985)
XLA Ops:
  0.6 0.0 copy-start
  0.6 1.5 %copy-done = f32[4,288,288]{2,1,0:T(8,128)S(1)} copy-done((f32[4,288,288]{2,1,0:T(8,128)S(1)}, f32[4,288,288]{2,1,0:T(8,128)}, u32[]{:S(2)}) %copy-start) | copy-done | bytes 1327128
  2.1 0.0 copy-start.1
  2.1 0.7 %copy-done.1 = f32[4,288]{1,0:T(4,128)S(1)} copy-done((f32[4,288]{1,0:T(4,128)S(1)}, f32[4,288]{1,0:T(4,128)}, u32[]{:S(2)}) %copy-start.1) | copy-done | bytes 4632
  2.8 0.7 %copy-done.3 = s32[4,4]{1,0:T(4,128)S(1)} copy-done((s32[4,4]{1,0:T(4,128)S(1)}, s32[4,4]{1,0:T(4,128)}, u32[]{:S(2)}) %copy-start.3) | copy-done | bytes 88
  3.5 0.0 copy-start.4
  3.5 0.7 %copy-done.4 = s32[4]{0:T(128)S(1)} copy-done((s32[4]{0:T(128)S(1)}, s32[4]{0:T(128)}, u32[]{:S(2)}) %copy-start.4) | copy-done | bytes 40
  4.1 4.3 %shard_map.68 = (f32[4,4,288,288]{3,2,1,0:T(8,128)S(1)}, f32[4,288,288]{2,1,0:T(8,128)S(1)}, s32[4,4]{1,0:T(4,128)S(4)}, s32[4,4]{1,0:T(4,128)S(4)}, f32[8,384]{...) custom-call(s32[4,4]{1,0:T(4,128)S(1)} %copy-done.3, s32[4]{0:T(128)S(1)} %copy-done.4, ...), custom_call_target="tpu_custom_call" | custom-call | tf_op jit(solution)/shard_map/pallas_call | solution.py:331
  8.4 0.5 %collective-permute-start = (f32[8,384]{1,0:T(8,128)S(1)}, f32[8,384]{1,0:T(8,128)S(1)}, u32[]{:S(2)}, u32[]{:S(2)}) collective-permute-start(f32[8,384]{1,0:T(8,128)S(1)} %get-tuple-element.18.swap.first_swap), channel_id=1, source_target_pairs={{0,1},{1,0},{2,3},{3,2},{4,5},{5,4},{6,7},{7,6},{8,9},{9,8},{10,11... | collective-permute-start | bytes 36872 | tf_op jit(solution)/shard_map/ppermute | solution.py:321
  9.0 0.8 %collective-permute-done.swapped = f32[8,384]{1,0:T(8,128)S(1)} collective-permute-done((f32[8,384]{1,0:T(8,128)S(1)}, f32[8,384]{1,0:T(8,128)S(1)}, u32[]{:S(2)}, u32[]{:S(2)}) %collective-permute-start) | collective-permute-done | bytes 12320 | tf_op jit(solution)/shard_map/ppermute | solution.py:321
  9.8 6.9 %collective-permute-start.1 = (f32[8,384]{1,0:T(8,128)S(1)}, f32[8,384]{1,0:T(8,128)S(1)}, u32[]{:S(2)}, u32[]{:S(2)}) collective-permute-start(f32[8,384]{1,0:T(8,128)S(1)} %get-tuple-element.21), channel_id=1, source_target_pairs={{0,30},{1,31},{2,4},{3,5},{4,2},{5,3},{6,8},{7,9},{8,6},{9,7},{10,... | collective-permute-start | bytes 36872 | tf_op jit(solution)/shard_map/ppermute | solution.py:329
  16.7 0.0 collective-permute-start.2
  16.7 1.7 %collective-permute-done.1.odd_in = f32[8,384]{1,0:T(8,128)S(1)} collective-permute-done((f32[8,384]{1,0:T(8,128)S(1)}, f32[8,384]{1,0:T(8,128)S(1)}, u32[]{:S(2)}, u32[]{:S(2)}) %collective-permute-start.1) | collective-permute-done | bytes 12320 | tf_op jit(solution)/shard_map/ppermute | solution.py:329
  18.4 2.0 %collective-permute-done.2.even_in = f32[8,384]{1,0:T(8,128)S(1)} collective-permute-done((f32[8,384]{1,0:T(8,128)S(1)}, f32[8,384]{1,0:T(8,128)S(1)}, u32[]{:S(2)}, u32[]{:S(2)}) %collective-permute-start.2) | collective-permute-done | bytes 12320 | tf_op jit(solution)/shard_map/ppermute | solution.py:329
  20.4 0.0 copy-done.2
  20.4 1.4 %shard_map.70 = (f32[4,384]{1,0:T(4,128)S(1)}, f32[8,384]{1,0:T(8,128)S(1)}, f32[4,384]{1,0:T(4,128)S(1)}, f32[4,384]{1,0:T(4,128)S(1)}) custom-call(s32[4,4]{1,0:T(4,128)S(4)} %get-tuple-element.15.place, s32[4,4]{1,0:T(4,128)S(4)} %get-tuple-element.16.live, f32[4,288]{1,0:T(4,128)S(1)} %copy-done.2, f32[4,4,288,288]{3,2,1,0:T(8,128)S(1)} %get-tuple-element.17.tiles, ...), custom_call_target="tpu_custom_call" | custom-call | tf_op jit(solution)/shard_map/pallas_call | solution.py:355
  21.8 0.0 collective-permute-start.3
  21.9 1.2 %collective-permute-done.3.swapped = f32[8,384]{1,0:T(8,128)S(1)} collective-permute-done((f32[8,384]{1,0:T(8,128)S(1)}, f32[8,384]{1,0:T(8,128)S(1)}, u32[]{:S(2)}, u32[]{:S(2)}) %collective-permute-start.3) | collective-permute-done | bytes 12320 | tf_op jit(solution)/shard_map/ppermute | solution.py:321
  23.0 0.2 shard_map.71
  23.2 13.7 %all_to_all.5.gathered = f32[16,8,384]{2,1,0:T(8,128)S(1)} all-to-all(f32[16,8,384]{2,1,0:T(8,128)S(1)} %shard_map.71), channel_id=1, replica_groups={{0,2,4,6,8,10,12,14,16,18,20,22,24,26,28,30},{1,3,5,7,9,11,13,15,17,19,..., dimensions={0} | all-to-all | bytes 393216 | tf_op jit(solution)/shard_map/all_to_all | solution.py:370
  37.0 0.4 %shard_map.72.last = f32[8,384]{1,0:T(8,128)S(1)} custom-call(f32[16,8,384]{2,1,0:T(8,128)S(1)} %all_to_all.5.gathered), custom_call_target="tpu_custom_call" | custom-call | tf_op jit(solution)/shard_map/pallas_call | solution.py:371
  37.4 0.0 collective-permute-start.4
  37.4 1.2 %collective-permute-done.4.last_swapped = f32[8,384]{1,0:T(8,128)S(1)} collective-permute-done((f32[8,384]{1,0:T(8,128)S(1)}, f32[8,384]{1,0:T(8,128)S(1)}, u32[]{:S(2)}, u32[]{:S(2)}) %collective-permute-start.4) | collective-permute-done | bytes 12320 | tf_op jit(solution)/shard_map/ppermute | solution.py:321
  38.6 1.3 %shard_map.73 = (f32[4,288]{1,0:T(4,128)}, f32[4,288]{1,0:T(4,128)}) custom-call(s32[4,4]{1,0:T(4,128)S(4)} %get-tuple-element.15.place, s32[4,4]{1,0:T(4,128)S(4)} %get-tuple-element.16.live, f32[4,288]{1,0:T(4,128)S(1)} %copy-done.2, f32[4,4,288,288]{3,2,1,0:T(8,128)S(1)} %get-tuple-element.17.tiles, f32[8,384]{1,0:T(8,128)S(1)} %get-tuple-element.18.swap.first_swap, ...), custom_call_target="tpu_custom_call" | custom-call | tf_op jit(solution)/shard_map/pallas_call | solution.py:377
  (3 shorter events, 0.0 us)
Async XLA Ops:
  0.6 1.5 %copy-start = (f32[4,288,288]{2,1,0:T(8,128)S(1)}, f32[4,288,288]{2,1,0:T(8,128)}, u32[]{:S(2)}) copy-start(f32[4,288,288]{2,1,0:T(8,128)} %jacobi_hbm.1) | copy-start | bytes 3981316
  2.1 0.7 %copy-start.1 = (f32[4,288]{1,0:T(4,128)S(1)}, f32[4,288]{1,0:T(4,128)}, u32[]{:S(2)}) copy-start(f32[4,288]{1,0:T(4,128)} %right.5) | copy-start | bytes 13828
  2.8 0.7 %copy-start.3 = (s32[4,4]{1,0:T(4,128)S(1)}, s32[4,4]{1,0:T(4,128)}, u32[]{:S(2)}) copy-start(s32[4,4]{1,0:T(4,128)} %cols.1) | copy-start | bytes 196
  3.5 0.7 %copy-start.4 = (s32[4]{0:T(128)S(1)}, s32[4]{0:T(128)}, u32[]{:S(2)}) copy-start(s32[4]{0:T(128)} %counts.1) | copy-start | bytes 52
  4.1 16.3 %copy-start.2 = (f32[4,288]{1,0:T(4,128)S(1)}, f32[4,288]{1,0:T(4,128)}, u32[]{:S(2)}) copy-start(f32[4,288]{1,0:T(4,128)} %right.5) | copy-start | bytes 13828
  8.4 1.4 %collective-permute-start = (f32[8,384]{1,0:T(8,128)S(1)}, f32[8,384]{1,0:T(8,128)S(1)}, u32[]{:S(2)}, u32[]{:S(2)}) collective-permute-start(f32[8,384]{1,0:T(8,128)S(1)} %get-tuple-element.18.swap.first_swap), channel_id=1, source_target_pairs={{0,1},{1,0},{2,3},{3,2},{4,5},{5,4},{6,7},{7,6},{8,9},{9,8},{10,11... | collective-permute-start | bytes 36872 | tf_op jit(solution)/shard_map/ppermute | solution.py:321
  9.8 8.6 %collective-permute-start.1 = (f32[8,384]{1,0:T(8,128)S(1)}, f32[8,384]{1,0:T(8,128)S(1)}, u32[]{:S(2)}, u32[]{:S(2)}) collective-permute-start(f32[8,384]{1,0:T(8,128)S(1)} %get-tuple-element.21), channel_id=1, source_target_pairs={{0,30},{1,31},{2,4},{3,5},{4,2},{5,3},{6,8},{7,9},{8,6},{9,7},{10,... | collective-permute-start | bytes 36872 | tf_op jit(solution)/shard_map/ppermute | solution.py:329
  16.7 3.7 %collective-permute-start.2 = (f32[8,384]{1,0:T(8,128)S(1)}, f32[8,384]{1,0:T(8,128)S(1)}, u32[]{:S(2)}, u32[]{:S(2)}) collective-permute-start(f32[8,384]{1,0:T(8,128)S(1)} %get-tuple-element.22), channel_id=1, source_target_pairs={{0,2},{1,3},{2,0},{3,1},{4,6},{5,7},{6,4},{7,5},{8,10},{9,11},{10,... | collective-permute-start | bytes 36872 | tf_op jit(solution)/shard_map/ppermute | solution.py:329
  21.8 1.2 %collective-permute-start.3 = (f32[8,384]{1,0:T(8,128)S(1)}, f32[8,384]{1,0:T(8,128)S(1)}, u32[]{:S(2)}, u32[]{:S(2)}) collective-permute-start(f32[8,384]{1,0:T(8,128)S(1)} %get-tuple-element.25.swap), channel_id=1, source_target_pairs={{0,1},{1,0},{2,3},{3,2},{4,5},{5,4},{6,7},{7,6},{8,9},{9,8},{10,11... | collective-permute-start | bytes 36872 | tf_op jit(solution)/shard_map/ppermute | solution.py:321
  37.4 1.2 %collective-permute-start.4 = (f32[8,384]{1,0:T(8,128)S(1)}, f32[8,384]{1,0:T(8,128)S(1)}, u32[]{:S(2)}, u32[]{:S(2)}) collective-permute-start(f32[8,384]{1,0:T(8,128)S(1)} %shard_map.72.last), channel_id=1, source_target_pairs={{0,1},{1,0},{2,3},{3,2},{4,5},{5,4},{6,7},{7,6},{8,9},{9,8},{10,11... | collective-permute-start | bytes 36872 | tf_op jit(solution)/shard_map/ppermute | solution.py:321

commit v2 on v1

v2 whole, which is shorter than its diff:
```python
import functools

import jax
import jax.numpy as jnp
from jax import lax
from jax.experimental import pallas as pl
from jax.experimental.pallas import tpu as pltpu
from jax.sharding import PartitionSpec as P

AXIS = "cams"
BAND = 2
F32 = jnp.float32
VMEM_LIMIT = 40 * 2**20
TINY = 1e-30


def padded(width):
    return -(-width // 128) * 128


def iota(shape, dim):
    return lax.broadcasted_iota(jnp.int32, shape, dim)


def total(value):
    return jnp.sum(jnp.sum(value, axis=1, keepdims=True), axis=0, keepdims=True)


def lay_scalars(values, lanes, first):
    lane = iota((1, lanes), 1)
    row = jnp.zeros((1, lanes), F32)
    for i, value in enumerate(values):
        row = jnp.where(lane == first + i, value, row)
    return row


def columns_to_row(columns, width):
    lanes = padded(width)
    skew = iota((8, 128), 1) - iota((8, 128), 0)
    parts = [jnp.zeros((8, 128), F32) for _ in range(lanes // 128)]
    for i, piece in enumerate(columns):
        tile, lane = divmod(8 * i, 128)
        parts[tile] = parts[tile] + jnp.where(skew == lane, piece, 0.0)
    return jnp.sum(jnp.concatenate(parts, axis=1), axis=0, keepdims=True)


def times_row(load, row, width):
    wide = jnp.broadcast_to(row[:, :width], (8, width))
    return [
        jnp.sum(load(i) * wide, axis=1, keepdims=True) for i in range(width // 8)
    ]


def scatter_products(tiles, place, live, group, columns, slots, width, spread):
    sums = [jnp.zeros((8, width), F32) for _ in range(1, slots)]
    for i, piece in enumerate(columns):
        for slot in range(1, slots):
            part = tiles[group, slot - 1, 8 * i : 8 * i + 8, :] * piece
            sums[slot - 1] = sums[slot - 1] + part
    for slot in range(1, slots):
        where = place[group, slot]
        kept = jnp.where(live[group, slot] > 0, sums[slot - 1], 0.0)
        spread[where, :, :width] = spread[where, :, :width] + kept


def upper_columns(tiles, place, live, wide, group, slots, width):
    rows = []
    for slot in range(1, slots):
        row = wide[place[group, slot], :, :width]
        rows.append(jnp.where(live[group, slot] > 0, row, 0.0))
    pieces = []
    for i in range(width // 8):
        part = tiles[group, 0, 8 * i : 8 * i + 8, :] * rows[0]
        for slot in range(2, slots):
            part = part + tiles[group, slot - 1, 8 * i : 8 * i + 8, :] * rows[slot - 1]
        pieces.append(jnp.sum(part, axis=1, keepdims=True))
    return pieces


def where_am_i(spot):
    return spot[0], spot[1] == 1, spot[2] == 1


def begin_kernel(blocks, slots, width, count,
                 cols_hbm, counts_hbm, right_hbm, jacobi_hbm, tiles_hbm,
                 jacobi, tiles, right, place, live, spot, z, near, odd_out, even_out,
                 cols, counts, spread, sems, jacobi_sem, tile_sem):
    small = [
        pltpu.make_async_copy(counts_hbm, counts, sems.at[0]),
        pltpu.make_async_copy(cols_hbm, cols, sems.at[1]),
        pltpu.make_async_copy(right_hbm, right, sems.at[2]),
    ]

    def jacobi_copy(g):
        return pltpu.make_async_copy(jacobi_hbm.at[g], jacobi.at[g], jacobi_sem.at[g])

    def tile_copy(g, k):
        return pltpu.make_async_copy(
            tiles_hbm.at[g, k], tiles.at[g, k - 1], tile_sem.at[g, k - 1]
        )

    for copy in small:
        copy.start()
    for g in range(blocks):
        jacobi_copy(g).start()
    small[0].wait()

    @pl.loop(0, blocks)
    def _(g):
        @pl.loop(1, counts[g])
        def _(k):
            tile_copy(g, k).start()

    @pl.loop(0, blocks)
    def _(g):
        @pl.loop(counts[g], slots)
        def _(k):
            tiles[g, k - 1] = jnp.zeros((width, width), F32)

    small[1].wait()
    base = cols[0, 0]
    me = base // blocks
    spot[0] = me // 2
    spot[1] = me % 2
    spot[2] = (me // 2) % 2
    for g in range(blocks):
        for k in range(slots):
            ahead = cols[g, k] - base
            ahead = jnp.where(ahead < 0, ahead + count * blocks, ahead)
            place[g, k] = jnp.clip(ahead, 0, (BAND + 1) * blocks - 1)
            live[g, k] = (k < counts[g]).astype(jnp.int32)
    spread[...] = jnp.zeros_like(spread)
    small[2].wait()

    for g in range(blocks):
        jacobi_copy(g).wait()
        columns = times_row(
            lambda i: jacobi[g, 8 * i : 8 * i + 8, :], right[g : g + 1, :], width
        )
        z[g : g + 1, :] = columns_to_row(columns, width)

        @pl.loop(1, counts[g])
        def _(k):
            tile_copy(g, k).wait()

        scatter_products(tiles, place, live, g, columns, slots, width, spread)
    sums = jnp.sum(spread[...], axis=1)
    near[...] = sums[:blocks]
    one, two = sums[blocks : 2 * blocks], sums[2 * blocks :]
    _, _, odd = where_am_i(spot)
    rows = z[...]
    backward = jnp.concatenate([rows, rows], axis=0)
    forward = jnp.concatenate([two, one], axis=0)
    odd_out[...] = jnp.where(odd, forward, backward)
    even_out[...] = jnp.where(odd, backward, forward)


def diagonal_product(blocks, width, diagonal, rows, out):
    for g in range(blocks):
        columns = times_row(
            lambda i: diagonal[g, 8 * i : 8 * i + 8, :], rows[g : g + 1, :], width
        )
        out[g : g + 1, :] = columns_to_row(columns, width)


def first_diagonal_kernel(blocks, width, tiles_hbm, z, near, diagonal, near_out, sem):
    copies = [
        pltpu.make_async_copy(tiles_hbm.at[g, 0], diagonal.at[g], sem.at[g])
        for g in range(blocks)
    ]
    for copy in copies:
        copy.start()
    for copy in copies:
        copy.wait()
    diagonal_product(blocks, width, diagonal, z, near_out)
    near_out[...] = near_out[...] + near[...]


def relay_kernel(blocks, spot, z, near, odd_out, even_out, odd_in, even_in, out, known):
    _, second, odd = where_am_i(spot)
    forward = jnp.where(odd, odd_out[...], even_out[...])
    ahead = jnp.where(odd, odd_in[...], even_in[...])
    behind = jnp.where(odd, even_in[...], odd_in[...])
    out[:blocks, :] = jnp.where(second, z[...], ahead[:blocks])
    out[blocks:, :] = jnp.where(second, behind[blocks:], forward[blocks:])
    known[...] = near[...] + behind[:blocks]


def spread_rows(wide, rows, first):
    for i in range(rows.shape[0]):
        wide[first + i, :, :] = jnp.broadcast_to(rows[i : i + 1], wide.shape[1:])


def middle_kernel(blocks, slots, width,
                  place, live, spot, tiles, jacobi, z, known_in, odd_in, even_in, relayed, right,
                  image, swap, far, near, wide, spread):
    lanes = padded(width)
    _, _, odd = where_am_i(spot)
    ahead = jnp.where(odd, odd_in[...], even_in[...])
    spread_rows(wide, z[...], 0)
    spread_rows(wide, relayed[:blocks, :], blocks)
    spread_rows(wide, ahead[:blocks], 2 * blocks)
    spread[...] = jnp.zeros_like(spread)
    known = known_in[...] + relayed[blocks:, :]
    for g in range(blocks):
        columns = upper_columns(tiles, place, live, wide, g, slots, width)
        image[g : g + 1, :] = known[g : g + 1, :] + columns_to_row(columns, width)
    q = image[...]
    size = jnp.max(jnp.max(jnp.abs(q), axis=1, keepdims=True), axis=0, keepdims=True)
    size = jnp.where(size > TINY, size, 1.0)
    scaled = q * (1.0 / size)
    for g in range(blocks):
        columns = times_row(
            lambda i: jacobi[g, 8 * i : 8 * i + 8, :], scaled[g : g + 1, :], width
        )
        swap[g : g + 1, :] = columns_to_row(columns, width)
        scatter_products(tiles, place, live, g, columns, slots, width, spread)
    sums = jnp.sum(spread[...], axis=1)
    far[...] = sums[2 * blocks :]
    near[...] = sums[:blocks]
    swap[blocks : 2 * blocks, :] = sums[blocks : 2 * blocks]
    values = [size, total(right[...] * z[:, :width]), total(z[...] * q)]
    swap[0:1, :] = swap[0:1, :] + lay_scalars(values, lanes, width)


def second_diagonal_kernel(blocks, width, right, diagonal_tiles, image, swap, near, near_out, out):
    lanes = padded(width)
    keep = iota((blocks, lanes), 1) < width
    w = jnp.where(keep, swap[:blocks, :], 0.0)
    diagonal_product(blocks, width, diagonal_tiles, swap, near_out)
    diagonal = near_out[...]
    values = [
        total(right[...] * w[:, :width]),
        total(image[...] * w),
        total(w * (diagonal + 2.0 * near[...])),
    ]
    near_out[...] = diagonal + near[...]
    out[...] = lay_scalars(values, 128, 0)


def fold(head, other, width, extra):
    tail = width - 256
    lane = iota((head.shape[0], 128), 1)
    last = jnp.where(lane < tail, head[:, 256:384], pltpu.roll(other[:, 256:384], tail, 1))
    last = jnp.where(lane < 2 * tail, last, extra)
    return head[:, :128], head[:, 128:256], other[:, :128], other[:, 128:256], last


def unfold_first(part, width):
    tail = width - 256
    last = jnp.where(iota(part.shape[1:], 1) < tail, part[4], 0.0)
    return jnp.concatenate([part[0], part[1], last], axis=1)


def unfold_second(part, width):
    tail = width - 256
    last = jnp.where(iota(part.shape[1:], 1) < tail, pltpu.roll(part[4], 128 - tail, 1), 0.0)
    return jnp.concatenate([part[2], part[3], last], axis=1)


def gather_kernel(blocks, width, spot, swap, swapped, far, dots, out):
    _, second, _ = where_am_i(spot)
    rows, other = swap[...], swapped[...]

    def at(block, i):
        return block[0:1, width + i : width + i + 1]

    mine, theirs = at(rows, 0), at(other, 0)
    scale = jnp.where(second, mine, jnp.maximum(mine, theirs))
    sent = far[...] * (mine / scale) + jnp.where(
        second, 0.0, other[blocks:] * (theirs / scale)
    )
    crossing = total(rows[blocks:, :width] * other[:blocks, :width])
    values = [
        mine,
        scale,
        at(rows, 1) + at(other, 1),
        at(rows, 2) + at(other, 2),
        dots[0:1, 0:1],
        dots[0:1, 1:2] / mine,
        at(rows, 2),
        dots[0:1, 2:3],
        jnp.where(second, 0.0, 2.0 * crossing),
        theirs,
    ]
    extra = lay_scalars(values, 128, 2 * (width - 256))
    parts = fold(rows[:blocks], sent, width, extra)
    for e in range(out.shape[0]):
        for i, part in enumerate(parts):
            out[e, i] = part


def after_kernel(spot, gathered, out):
    chips = gathered.shape[0]
    chip, _, _ = where_am_i(spot)
    out[...] = gathered[jnp.where(chip == chips - 1, 0, chip + 1)]


def sums_kernel(blocks, width, gathered, out):
    chips = gathered.shape[0]
    tail = width - 256
    table = jnp.concatenate([gathered[e, 4, 0:1, :] for e in range(chips)], axis=0)
    later = jnp.concatenate([table[1:], table[:1]], axis=0)

    def at(i, rows=table):
        return rows[:, 2 * tail + i : 2 * tail + i + 1]

    def chips_total(value):
        return jnp.sum(value, axis=0, keepdims=True)

    norm = chips_total(at(2))
    along = chips_total(at(3))
    alpha = norm / along
    size = alpha * at(0)
    fresh = chips_total(size * (size * at(5) - at(4)) - alpha * at(6))
    diagonal = chips_total(
        size * (size * at(7) + (alpha * at(9)) * at(8) - 2.0 * at(0) * at(5))
    )
    weight = (alpha * at(1)) * (alpha * at(0, later))
    inside = iota((blocks, 128), 1) < tail
    lines = []
    for e in range(chips):
        n = (e + 1) % chips
        ends = jnp.where(inside, pltpu.roll(gathered[e, 4], 128 - tail, 1) * gathered[n, 4], 0.0)
        pair = gathered[e, 2] * gathered[n, 0] + gathered[e, 3] * gathered[n, 1] + ends
        lines.append(jnp.sum(pair, axis=0, keepdims=True))
    edges = total(jnp.concatenate(lines, axis=0) * weight)
    values = [fresh, diagonal + 2.0 * edges, norm, along]
    out[...] = jnp.broadcast_to(lay_scalars(values, 128, 0), out.shape)


def later_kernel(blocks, slots, width,
                 place, live, spot, tiles, swap, swapped, near, gathered, next_part, next_other, sums,
                 product, scaled, wide):
    chips = gathered.shape[0]
    lanes = padded(width)
    chip, second, _ = where_am_i(spot)
    tail = width - 256
    before = gathered[jnp.where(chip == 0, chips - 1, chip - 1)]
    alpha = sums[0:1, 2:3] / sums[0:1, 3:4]

    def at(part, i):
        return alpha * part[4, 0:1, 2 * tail + i : 2 * tail + i + 1]

    mine = alpha * swap[0:1, width : width + 1]
    theirs = alpha * swapped[0:1, width : width + 1]
    keep = iota((blocks, lanes), 1) < width
    w = jnp.where(keep, swap[:blocks, :], 0.0) * mine
    w_other = jnp.where(keep, swapped[:blocks, :], 0.0) * theirs
    ahead, ahead_other = next_part[...], next_other[...]
    ahead = unfold_first(ahead, width) * at(ahead, 0)
    ahead_other = unfold_first(ahead_other, width) * at(ahead_other, 0)
    scaled[...] = w
    spread_rows(wide, w, 0)
    spread_rows(wide, jnp.where(second, ahead_other, w_other), blocks)
    spread_rows(wide, ahead, 2 * blocks)
    known = near[...] * mine + unfold_second(before, width) * at(before, 1)
    product[...] = known + jnp.where(second, swapped[blocks:, :] * theirs, 0.0)

    for g in range(blocks):
        columns = upper_columns(tiles, place, live, wide, g, slots, width)
        product[g : g + 1, :] = product[g : g + 1, :] + columns_to_row(columns, width)


def end_kernel(blocks, width, right, z_ref, image, product, scaled, sums, sums_other,
               update, residual):
    def shared(i):
        return sums[0:1, i : i + 1] + sums_other[0:1, i : i + 1]

    norm, along = sums[0:1, 2:3], sums[0:1, 3:4]
    alpha = norm / along
    fresh = norm + shared(0)
    curved = along + shared(1)
    ratio = fresh / norm
    step = fresh / (curved - ratio * (fresh / alpha))
    z, q = z_ref[...], image[...]
    z_next = z - scaled[...]
    update[...] = (alpha * z + step * (z_next + ratio * z))[:, :width]
    r_next = right[...] - (alpha * q)[:, :width]
    residual[...] = r_next - (step * ((q - product[...]) + ratio * q))[:, :width]


def on_device(right_side, schur_tiles, block_cols, tile_counts, jacobi_inverse):
    count = lax.axis_size(AXIS)
    blocks, slots, width, _ = schur_tiles.shape
    lanes = padded(width)
    chips = count // 2
    vmem = pl.BlockSpec(memory_space=pltpu.VMEM)
    smem = pl.BlockSpec(memory_space=pltpu.SMEM)
    hbm = pl.BlockSpec(memory_space=pltpu.HBM)
    rows = pltpu.VMEM((2 * blocks, lanes), F32)
    half = pltpu.VMEM((blocks, lanes), F32)
    small = pltpu.VMEM((8, 128), F32)
    spread = pltpu.VMEM(((BAND + 1) * blocks, 8, lanes), F32)
    index = pltpu.SMEM((blocks, slots), jnp.int32)

    def call(kernel, sizes, in_specs, out_shape, scratch=(), work=0):
        single = not isinstance(out_shape, list)
        shapes = [out_shape] if single else out_shape
        specs = [
            smem if getattr(shape, "memory_space", None) == pltpu.SMEM else vmem
            for shape in shapes
        ]
        return pl.pallas_call(
            functools.partial(kernel, *sizes),
            in_specs=in_specs,
            out_specs=specs[0] if single else specs,
            out_shape=out_shape,
            scratch_shapes=list(scratch),
            compiler_params=pltpu.CompilerParams(vmem_limit_bytes=VMEM_LIMIT),
            cost_estimate=pl.CostEstimate(
                flops=2 * work * width * width, bytes_accessed=4 * work * width * width, transcendentals=0
            ),
        )

    def swap_cores(value):
        return lax.ppermute(value, AXIS, [(i, i ^ 1) for i in range(count)])

    def swap_chips(odd, value):
        pairs = []
        for i in range(count):
            chip, core = divmod(i, 2)
            step = 1 if (chip % 2 == 1) == odd else -1
            pairs.append((i, 2 * ((chip + step) % chips) + core))
        return lax.ppermute(value, AXIS, pairs)

    sizes = (blocks, slots, width)
    off_chip = [
        pltpu.with_memory_space_constraint(value, pltpu.HBM)
        for value in (block_cols, tile_counts, right_side, jacobi_inverse, schur_tiles)
    ]
    jacobi, tiles, right, place, live, spot, z, near, odd_out, even_out = call(
        begin_kernel, sizes + (count,), [hbm] * 5,
        [
            pltpu.VMEM(jacobi_inverse.shape, F32),
            pltpu.VMEM((blocks, slots - 1, width, width), F32),
            pltpu.VMEM(right_side.shape, F32),
            index, index, pltpu.SMEM((4,), jnp.int32),
            half, half, rows, rows,
        ],
        [
            pltpu.SMEM(block_cols.shape, jnp.int32),
            pltpu.SMEM(tile_counts.shape, jnp.int32),
            spread,
            pltpu.SemaphoreType.DMA((3,)),
            pltpu.SemaphoreType.DMA((blocks,)),
            pltpu.SemaphoreType.DMA((blocks, slots - 1)),
        ],
        work=blocks * slots,
    )(*off_chip)
    odd_in = swap_chips(True, odd_out)
    even_in = swap_chips(False, even_out)
    diagonal, near1 = call(
        first_diagonal_kernel, (blocks, width), [hbm, vmem, vmem],
        [pltpu.VMEM((blocks, width, width), F32), half],
        [pltpu.SemaphoreType.DMA((blocks,))],
        work=blocks,
    )(off_chip[4], z, near)
    relay, known = call(relay_kernel, (blocks,), [smem] + [vmem] * 6, [rows, half])(
        spot, z, near1, odd_out, even_out, odd_in, even_in
    )
    relayed = swap_cores(relay)
    image, swap, far, near2 = call(
        middle_kernel, sizes, [smem] * 3 + [vmem] * 8, [half, rows, half, half], [spread, spread],
        work=3 * blocks * slots,
    )(place, live, spot, tiles, jacobi, z, known, odd_in, even_in, relayed, right)
    swapped = swap_cores(swap)
    near3, dots = call(
        second_diagonal_kernel, (blocks, width), [vmem] * 5, [half, pltpu.VMEM((1, 128), F32)], work=blocks
    )(right, diagonal, image, swap, near2)
    sent = call(
        gather_kernel, (blocks, width), [smem] + [vmem] * 4, pltpu.VMEM((chips, 5, blocks, 128), F32)
    )(spot, swap, swapped, far, dots)
    groups = [[2 * c + core for c in range(chips)] for core in range(2)]
    gathered = lax.all_to_all(sent, AXIS, 0, 0, axis_index_groups=groups)
    next_part = call(after_kernel, (), [smem, vmem], pltpu.VMEM((5, blocks, 128), F32))(spot, gathered)
    next_other = swap_cores(next_part)
    sums = call(sums_kernel, (blocks, width), [vmem], small, work=chips)(gathered)
    sums_other = swap_cores(sums)
    product, scaled = call(
        later_kernel, sizes, [smem] * 3 + [vmem] * 8, [half, half], [spread], work=blocks * slots,
    )(place, live, spot, tiles, swap, swapped, near3, gathered, next_part, next_other, sums)
    out = jax.ShapeDtypeStruct(right_side.shape, F32)
    return call(end_kernel, (blocks, width), [vmem] * 7, [out, out])(
        right, z, image, product, scaled, sums, sums_other
    )


def solution(mesh):
    placed = (
        P(AXIS, None),
        P(AXIS, None, None, None),
        P(AXIS, None),
        P(AXIS),
        P(AXIS, None, None),
    )
    return jax.shard_map(
        on_device,
        mesh=mesh,
        in_specs=placed,
        out_specs=(P(AXIS, None), P(AXIS, None)),
        check_vma=False,
    )
```

time: 40.1 us -> 34.1 us (0.85)
  local copies, waits for them, and re-layouts: 3.5 us -> 0 us
  waiting for transfers between devices: 6.85 us -> 4.17 us
  Pallas kernels: 7.61 us -> 8.67 us
  blocking collectives: 13.7 us -> 12.9 us
    unnamed x10 -> x0, local copies, waits for them, and re-layouts: 3.5 us -> none
    ppermute x2, waiting for transfers between devices: 3.69 us -> 1.98 us  [swap_chips(): return lax.ppermute(value, AXIS, pairs)]
    pallas_call x6 -> x10, Pallas kernels: 7.61 us -> 8.67 us  [the longest x1 3.37 us: on_device(): call(begin_kernel, sizes + (count,), [hbm] * 5, [pltpu.VMEM(jacobi_invers...]
    ppermute x3 -> x4, waiting for transfers between devices: 3.16 us -> 2.19 us  [swap_cores(): return lax.ppermute(value, AXIS, [(i, i ^ 1) for i in range(count)])]
    all_to_all x1, blocking collectives: 13.7 us -> 12.9 us  [on_device(): gathered = lax.all_to_all(sent, AXIS, 0, 0, axis_index_groups=groups)]
    ppermute x3 -> x4, starting transfers between devices: 0.57 us -> 0.82 us  [swap_cores(): return lax.ppermute(value, AXIS, [(i, i ^ 1) for i in range(count)])]
  transfers between devices with their start and end apart: 5 -> 6, of which waited for: 5 -> 4; matrix products, arithmetic and copies ran while one was open for 0% -> 0% of each run, Pallas kernels for 0% -> 9%
where the time goes in v2:
time: 34.1 us
  blocking collectives  12.9 us (38%)
  Pallas kernels  8.67 us (25%)
  starting transfers between devices  7.65 us (22%)
  waiting for transfers between devices  4.17 us (12%)
  between operations  0.69 us (2%)
    all_to_all x1, blocking collectives, on_device(): gathered = lax.all_to_all(sent, AXIS, 0, 0, axis_index_groups=groups)  12.9 us
    ppermute x2, starting transfers between devices, swap_chips(): return lax.ppermute(value, AXIS, pairs)  6.83 us
    pallas_call x1, Pallas kernels, on_device(): call(begin_kernel, sizes + (count,), [hbm] * 5, [pltpu.VMEM(jacobi_invers...  3.37 us
    ppermute x4, waiting for transfers between devices, swap_cores(): return lax.ppermute(value, AXIS, [(i, i ^ 1) for i in range(count)])  2.19 us
    ppermute x2, waiting for transfers between devices, swap_chips(): return lax.ppermute(value, AXIS, pairs)  1.98 us
    pallas_call x1, Pallas kernels, on_device(): call(first_diagonal_kernel, (blocks, width), [hbm, vmem, vmem], [pltpu.VM...  1.7 us
    pallas_call x1, Pallas kernels, on_device(): call(middle_kernel, sizes, [smem] * 3 + [vmem] * 8, [half, rows, half, ha...  1.17 us
    pallas_call x1, Pallas kernels, on_device(): call(end_kernel, (blocks, width), [vmem] * 7, [out, out])  0.93 us
  transfers between devices with their start and end apart: 6, of which 4 were waited for; matrix products, arithmetic and copies ran while one was open for 0% of the time, Pallas kernels for 9%

profile of v2, /device:TPU:0, one launch (start us, length us, event | category | flops | bytes accessed | tf_op | source)
XLA Modules:
  0.0 34.1 jit_solution(14143726953758760532)
XLA Ops:
  0.6 3.4 %shard_map.68 = (f32[4,288,288]{2,1,0:T(8,128)S(1)}, f32[4,3,288,288]{3,2,1,0:T(8,128)S(1)}, f32[4,288]{1,0:T(4,128)S(1)}, s32[4,4]{1,0:T(4,128)S(4)}, s32[4,4]{...) custom-call(s32[4,4]{1,0:T(4,128)} %cols_hbm.1, ...), custom_call_target="tpu_custom_call" | custom-call | flops 2654208 | bytes 5308416 | tf_op jit(solution)/shard_map/pallas_call | solution.py:432
  4.0 6.8 %collective-permute-start = (f32[8,384]{1,0:T(8,128)S(1)}, f32[8,384]{1,0:T(8,128)S(1)}, u32[]{:S(2)}, u32[]{:S(2)}) collective-permute-start(f32[8,384]{1,0:T(8,128)S(1)} %get-tuple-element.33.odd_out), channel_id=1, source_target_pairs={{0,30},{1,31},{2,4},{3,5},{4,2},{5,3},{6,8},{7,9},{8,6},{9,7},{10,... | collective-permute-start | bytes 36872 | tf_op jit(solution)/shard_map/ppermute | solution.py:425
  10.8 0.0 collective-permute-start.1
  10.8 1.7 %shard_map.69 = (f32[4,288,288]{2,1,0:T(8,128)S(1)}, f32[4,384]{1,0:T(4,128)S(1)}) custom-call(f32[4,4,288,288]{3,2,1,0:T(8,128)} %tiles_hbm.3, f32[4,384]{1,0:T(4,128)S(1)} %get-tuple-element.25.z.z_ref, f32[4,384]{1,0:T(4,128)S(1)} %get-tuple-element.31.near), custom_call_target="tpu_custom_call" | custom-call | flops 663552 | bytes 1327104 | tf_op jit(solution)/shard_map/pallas_call | solution.py:453
  12.5 0.0 collective-permute-done.odd_in
  12.6 2.0 %collective-permute-done.1.even_in = f32[8,384]{1,0:T(8,128)S(1)} collective-permute-done((f32[8,384]{1,0:T(8,128)S(1)}, f32[8,384]{1,0:T(8,128)S(1)}, u32[]{:S(2)}, u32[]{:S(2)}) %collective-permute-start.1) | collective-permute-done | bytes 12320 | tf_op jit(solution)/shard_map/ppermute | solution.py:425
  14.5 0.1 collective-permute-start.2
  14.6 1.2 %collective-permute-done.2.relayed = f32[8,384]{1,0:T(8,128)S(1)} collective-permute-done((f32[8,384]{1,0:T(8,128)S(1)}, f32[8,384]{1,0:T(8,128)S(1)}, u32[]{:S(2)}, u32[]{:S(2)}) %collective-permute-start.2) | collective-permute-done | bytes 12320 | tf_op jit(solution)/shard_map/ppermute | solution.py:417
  15.8 1.2 %shard_map.71 = (f32[4,384]{1,0:T(4,128)S(1)}, f32[8,384]{1,0:T(8,128)S(1)}, f32[4,384]{1,0:T(4,128)S(1)}, f32[4,384]{1,0:T(4,128)S(1)}) custom-call(s32[4,4]{1,0:T(4,128)S(4)} %get-tuple-element.26.place, s32[4,4]{1,0:T(4,128)S(4)} %get-tuple-element.27.live, s32[4]{0:T(128)S(4)} %get-tuple-element.28.spot, f32[4,3,288,288]{3,2,1,0:T(8,128)S(1)} %get-tuple-element.29.tiles, ...), custom_call_target="tpu_custom_call" | custom-call | flops 7962624 | bytes 15925248 | tf_op jit(solution)/shard_map/pallas_call | solution.py:463
  17.0 0.2 collective-permute-start.3
  17.2 0.3 shard_map.72
  17.5 0.7 %collective-permute-done.3.swapped = f32[8,384]{1,0:T(8,128)S(1)} collective-permute-done((f32[8,384]{1,0:T(8,128)S(1)}, f32[8,384]{1,0:T(8,128)S(1)}, u32[]{:S(2)}, u32[]{:S(2)}) %collective-permute-start.3) | collective-permute-done | bytes 12320 | tf_op jit(solution)/shard_map/ppermute | solution.py:417
  18.2 0.2 shard_map.73
  18.4 12.9 %all_to_all.5.gathered = f32[16,5,4,128]{3,2,1,0:T(4,128)S(1)} all-to-all(f32[16,5,4,128]{3,2,1,0:T(4,128)S(1)} %shard_map.73), channel_id=1, replica_groups={{0,2,4,6,8,10,12,14,16,18,20,22,24,26,28,30},{1,3,5,7,9,11,13,15,17,19,..., dimensions={0} | all-to-all | bytes 327680 | tf_op jit(solution)/shard_map/all_to_all | solution.py:475
  31.3 0.0 collective-permute-start.4
  31.3 0.3 shard_map.75.sums
  31.7 0.5 %collective-permute-start.5 = (f32[8,128]{1,0:T(8,128)S(1)}, f32[8,128]{1,0:T(8,128)S(1)}, u32[]{:S(2)}, u32[]{:S(2)}) collective-permute-start(f32[8,128]{1,0:T(8,128)S(1)} %shard_map.75.sums), channel_id=1, source_target_pairs={{0,1},{1,0},{2,3},{3,2},{4,5},{5,4},{6,7},{7,6},{8,9},{9,8},{10,11... | collective-permute-start | bytes 12296 | tf_op jit(solution)/shard_map/ppermute | solution.py:417
  32.2 0.3 collective-permute-done.4.next_other
  32.5 0.7 %shard_map.76 = (f32[4,384]{1,0:T(4,128)S(1)}, f32[4,384]{1,0:T(4,128)S(1)}) custom-call(s32[4,4]{1,0:T(4,128)S(4)} %get-tuple-element.26.place, s32[4,4]{1,0:T(4,128)S(4)} %get-tuple-element.27.live, s32[4]{0:T(128)S(4)} %get-tuple-element.28.spot, f32[4,3,288,288]{3,2,1,0:T(8,128)S(1)} %get-tuple-element.29.tiles, f32[8,384]{1,0:T(8,128)S(1)} %get-tuple-element.38.swap, ...), custom_call_target="tpu_custom_call" | custom-call | flops 2654208 | bytes 5308416 | tf_op jit(solution)/shard_map/pallas_call | solution.py:480
  33.2 0.0 collective-permute-done.5.sums_other
  33.2 0.9 %shard_map.77 = (f32[4,288]{1,0:T(4,128)}, f32[4,288]{1,0:T(4,128)}) custom-call(f32[4,288]{1,0:T(4,128)S(1)} %get-tuple-element.24.right, f32[4,384]{1,0:T(4,128)S(1)} %get-tuple-element.25.z.z_ref, f32[4,384]{1,0:T(4,128)S(1)} %get-tuple-element.37.image, f32[4,384]{1,0:T(4,128)S(1)} %get-tuple-element.44.product, f32[4,384]{1,0:T(4,128)S(1)} %get-tuple-element.45.scaled, ...), custom_call_target="tpu_custom_call" | custom-call | tf_op jit(solution)/shard_map/pallas_call | solution.py:484
  (2 shorter events, 0.0 us)
Async XLA Ops:
  4.0 8.5 %collective-permute-start = (f32[8,384]{1,0:T(8,128)S(1)}, f32[8,384]{1,0:T(8,128)S(1)}, u32[]{:S(2)}, u32[]{:S(2)}) collective-permute-start(f32[8,384]{1,0:T(8,128)S(1)} %get-tuple-element.33.odd_out), channel_id=1, source_target_pairs={{0,30},{1,31},{2,4},{3,5},{4,2},{5,3},{6,8},{7,9},{8,6},{9,7},{10,... | collective-permute-start | bytes 36872 | tf_op jit(solution)/shard_map/ppermute | solution.py:425
  10.8 3.7 %collective-permute-start.1 = (f32[8,384]{1,0:T(8,128)S(1)}, f32[8,384]{1,0:T(8,128)S(1)}, u32[]{:S(2)}, u32[]{:S(2)}) collective-permute-start(f32[8,384]{1,0:T(8,128)S(1)} %get-tuple-element.34.even_out), channel_id=1, source_target_pairs={{0,2},{1,3},{2,0},{3,1},{4,6},{5,7},{6,4},{7,5},{8,10},{9,11},{10,... | collective-permute-start | bytes 36872 | tf_op jit(solution)/shard_map/ppermute | solution.py:425
  14.5 1.2 %collective-permute-start.2 = (f32[8,384]{1,0:T(8,128)S(1)}, f32[8,384]{1,0:T(8,128)S(1)}, u32[]{:S(2)}, u32[]{:S(2)}) collective-permute-start(f32[8,384]{1,0:T(8,128)S(1)} %get-tuple-element.36), channel_id=1, source_target_pairs={{0,1},{1,0},{2,3},{3,2},{4,5},{5,4},{6,7},{7,6},{8,9},{9,8},{10,11... | collective-permute-start | bytes 36872 | tf_op jit(solution)/shard_map/ppermute | solution.py:417
  17.0 1.2 %collective-permute-start.3 = (f32[8,384]{1,0:T(8,128)S(1)}, f32[8,384]{1,0:T(8,128)S(1)}, u32[]{:S(2)}, u32[]{:S(2)}) collective-permute-start(f32[8,384]{1,0:T(8,128)S(1)} %get-tuple-element.38.swap), channel_id=1, source_target_pairs={{0,1},{1,0},{2,3},{3,2},{4,5},{5,4},{6,7},{7,6},{8,9},{9,8},{10,11... | collective-permute-start | bytes 36872 | tf_op jit(solution)/shard_map/ppermute | solution.py:417
  31.3 1.2 %collective-permute-start.4 = (f32[5,4,128]{2,1,0:T(4,128)S(1)}, f32[5,4,128]{2,1,0:T(4,128)S(1)}, u32[]{:S(2)}, u32[]{:S(2)}) collective-permute-start(f32[5,4,128]{2,1,0:T(4,128)S(1)} %shard_map.74.next_part), channel_id=1, source_target_pairs={{0,1},{1,0},{2,3},{3,2},{4,5},{5,4},{6,7},{7,6},{8,9},{9,8},{10,11... | collective-permute-start | bytes 30728 | tf_op jit(solution)/shard_map/ppermute | solution.py:417
  31.7 1.5 %collective-permute-start.5 = (f32[8,128]{1,0:T(8,128)S(1)}, f32[8,128]{1,0:T(8,128)S(1)}, u32[]{:S(2)}, u32[]{:S(2)}) collective-permute-start(f32[8,128]{1,0:T(8,128)S(1)} %shard_map.75.sums), channel_id=1, source_target_pairs={{0,1},{1,0},{2,3},{3,2},{4,5},{5,4},{6,7},{7,6},{8,9},{9,8},{10,11... | collective-permute-start | bytes 12296 | tf_op jit(solution)/shard_map/ppermute | solution.py:417

commit v3 on v2

--- a/solution.py
+++ b/solution.py
@@ -83,7 +83,7 @@
 
 def begin_kernel(blocks, slots, width, count,
                  cols_hbm, counts_hbm, right_hbm, jacobi_hbm, tiles_hbm,
-                 jacobi, tiles, right, place, live, spot, z, near, odd_out, even_out,
+                 jacobi, tiles, right, place, live, spot, z, near, one_out, odd_out, back_out, even_out,
                  cols, counts, spread, sems, jacobi_sem, tile_sem):
     small = [
         pltpu.make_async_copy(counts_hbm, counts, sems.at[0]),
@@ -149,10 +149,10 @@
     one, two = sums[blocks : 2 * blocks], sums[2 * blocks :]
     _, _, odd = where_am_i(spot)
     rows = z[...]
-    backward = jnp.concatenate([rows, rows], axis=0)
-    forward = jnp.concatenate([two, one], axis=0)
-    odd_out[...] = jnp.where(odd, forward, backward)
-    even_out[...] = jnp.where(odd, backward, forward)
+    one_out[...] = one
+    back_out[...] = rows
+    odd_out[...] = jnp.where(odd, two, rows)
+    even_out[...] = jnp.where(odd, rows, two)
 
 
 def diagonal_product(blocks, width, diagonal, rows, out):
@@ -176,14 +176,11 @@
     near_out[...] = near_out[...] + near[...]
 
 
-def relay_kernel(blocks, spot, z, near, odd_out, even_out, odd_in, even_in, out, known):
-    _, second, odd = where_am_i(spot)
-    forward = jnp.where(odd, odd_out[...], even_out[...])
-    ahead = jnp.where(odd, odd_in[...], even_in[...])
-    behind = jnp.where(odd, even_in[...], odd_in[...])
-    out[:blocks, :] = jnp.where(second, z[...], ahead[:blocks])
-    out[blocks:, :] = jnp.where(second, behind[blocks:], forward[blocks:])
-    known[...] = near[...] + behind[:blocks]
+def join_kernel(spot, near, forward_in, odd_in, back_in, even_in, known, one, two):
+    _, _, odd = where_am_i(spot)
+    one[...] = back_in[...]
+    two[...] = jnp.where(odd, odd_in[...], even_in[...])
+    known[...] = near[...] + forward_in[...] + jnp.where(odd, even_in[...], odd_in[...])
 
 
 def spread_rows(wide, rows, first):
@@ -192,16 +189,13 @@
 
 
 def middle_kernel(blocks, slots, width,
-                  place, live, spot, tiles, jacobi, z, known_in, odd_in, even_in, relayed, right,
+                  place, live, tiles, jacobi, z, known, one, two, right,
                   image, swap, far, near, wide, spread):
     lanes = padded(width)
-    _, _, odd = where_am_i(spot)
-    ahead = jnp.where(odd, odd_in[...], even_in[...])
     spread_rows(wide, z[...], 0)
-    spread_rows(wide, relayed[:blocks, :], blocks)
-    spread_rows(wide, ahead[:blocks], 2 * blocks)
+    spread_rows(wide, one[...], blocks)
+    spread_rows(wide, two[...], 2 * blocks)
     spread[...] = jnp.zeros_like(spread)
-    known = known_in[...] + relayed[blocks:, :]
     for g in range(blocks):
         columns = upper_columns(tiles, place, live, wide, g, slots, width)
         image[g : g + 1, :] = known[g : g + 1, :] + columns_to_row(columns, width)
@@ -429,14 +423,14 @@
         pltpu.with_memory_space_constraint(value, pltpu.HBM)
         for value in (block_cols, tile_counts, right_side, jacobi_inverse, schur_tiles)
     ]
-    jacobi, tiles, right, place, live, spot, z, near, odd_out, even_out = call(
+    jacobi, tiles, right, place, live, spot, z, near, one_out, odd_out, back_out, even_out = call(
         begin_kernel, sizes + (count,), [hbm] * 5,
         [
             pltpu.VMEM(jacobi_inverse.shape, F32),
             pltpu.VMEM((blocks, slots - 1, width, width), F32),
             pltpu.VMEM(right_side.shape, F32),
             index, index, pltpu.SMEM((4,), jnp.int32),
-            half, half, rows, rows,
+            half, half, half, half, half, half,
         ],
         [
             pltpu.SMEM(block_cols.shape, jnp.int32),
@@ -448,7 +442,9 @@
         ],
         work=blocks * slots,
     )(*off_chip)
+    forward_in = lax.ppermute(one_out, AXIS, [(i, (i + 1) % count) for i in range(count)])
     odd_in = swap_chips(True, odd_out)
+    back_in = lax.ppermute(back_out, AXIS, [((i + 1) % count, i) for i in range(count)])
     even_in = swap_chips(False, even_out)
     diagonal, near1 = call(
         first_diagonal_kernel, (blocks, width), [hbm, vmem, vmem],
@@ -456,14 +452,13 @@
         [pltpu.SemaphoreType.DMA((blocks,))],
         work=blocks,
     )(off_chip[4], z, near)
-    relay, known = call(relay_kernel, (blocks,), [smem] + [vmem] * 6, [rows, half])(
-        spot, z, near1, odd_out, even_out, odd_in, even_in
-    )
-    relayed = swap_cores(relay)
+    known, one, two = call(join_kernel, (), [smem] + [vmem] * 5, [half, half, half])(
+        spot, near1, forward_in, odd_in, back_in, even_in
+    )
     image, swap, far, near2 = call(
-        middle_kernel, sizes, [smem] * 3 + [vmem] * 8, [half, rows, half, half], [spread, spread],
+        middle_kernel, sizes, [smem] * 2 + [vmem] * 7, [half, rows, half, half], [spread, spread],
         work=3 * blocks * slots,
-    )(place, live, spot, tiles, jacobi, z, known, odd_in, even_in, relayed, right)
+    )(place, live, tiles, jacobi, z, known, one, two, right)
     swapped = swap_cores(swap)
     near3, dots = call(
         second_diagonal_kernel, (blocks, width), [vmem] * 5, [half, pltpu.VMEM((1, 128), F32)], work=blocks

time: 34.1 us -> 33.3 us (0.977)
  starting transfers between devices: 7.65 us -> 9.1 us
  waiting for transfers between devices: 4.17 us -> 2.73 us
  Pallas kernels: 8.67 us -> 8.11 us
    ppermute x0 -> x2, starting transfers between devices: none -> 1.46 us  [the longest x1 0.74 us: on_device(): lax.ppermute(back_out, AXIS, [((i + 1) % count, i) for i in range(count)])]
    ppermute x4 -> x3, waiting for transfers between devices: 2.19 us -> 1.17 us  [swap_cores(): return lax.ppermute(value, AXIS, [(i, i ^ 1) for i in range(count)])]
    pallas_call x1, Pallas kernels: 3.37 us -> 2.81 us  [on_device(): call(begin_kernel, sizes + (count,), [hbm] * 5, [pltpu.VMEM(jacobi_invers...]
    ppermute x2, waiting for transfers between devices: 1.98 us -> 1.56 us  [swap_chips(): return lax.ppermute(value, AXIS, pairs)]
    all_to_all x1, blocking collectives: 12.9 us -> 12.6 us  [on_device(): gathered = lax.all_to_all(sent, AXIS, 0, 0, axis_index_groups=groups)]
    ppermute x4 -> x3, starting transfers between devices: 0.82 us -> 0.59 us  [swap_cores(): return lax.ppermute(value, AXIS, [(i, i ^ 1) for i in range(count)])]
  transfers between devices with their start and end apart: 6 -> 7, of which waited for: 4 -> 3; matrix products, arithmetic and copies ran while one was open for 0% -> 0% of each run, Pallas kernels for 9% -> 9%
where the time goes in v3:
time: 33.3 us; the launch traced here: 33.2 us
  blocking collectives  12.6 us (38%)
  starting transfers between devices  9.1 us (27%)
  Pallas kernels  8.11 us (24%)
  waiting for transfers between devices  2.73 us (8%)
  between operations  0.7 us (2%)
    all_to_all x1, blocking collectives, on_device(): gathered = lax.all_to_all(sent, AXIS, 0, 0, axis_index_groups=groups)  12.6 us
    ppermute x2, starting transfers between devices, swap_chips(): return lax.ppermute(value, AXIS, pairs)  7.05 us
    pallas_call x1, Pallas kernels, on_device(): call(begin_kernel, sizes + (count,), [hbm] * 5, [pltpu.VMEM(jacobi_invers...  2.81 us
    pallas_call x1, Pallas kernels, on_device(): call(first_diagonal_kernel, (blocks, width), [hbm, vmem, vmem], [pltpu.VM...  1.7 us
    ppermute x2, waiting for transfers between devices, swap_chips(): return lax.ppermute(value, AXIS, pairs)  1.56 us
    ppermute x3, waiting for transfers between devices, swap_cores(): return lax.ppermute(value, AXIS, [(i, i ^ 1) for i in range(count)])  1.17 us
    pallas_call x1, Pallas kernels, on_device(): call(middle_kernel, sizes, [smem] * 2 + [vmem] * 7, [half, rows, half, ha...  1.16 us
    pallas_call x1, Pallas kernels, on_device(): call(end_kernel, (blocks, width), [vmem] * 7, [out, out])  0.93 us
  transfers between devices with their start and end apart: 7, of which 3 were waited for; matrix products, arithmetic and copies ran while one was open for 0% of the time, Pallas kernels for 9%

profile of v3, /device:TPU:0, one launch (start us, length us, event | category | flops | bytes accessed | tf_op | source)
XLA Modules:
  0.0 33.2 jit_solution(8396411785863085949)
XLA Ops:
  0.6 2.8 %shard_map.68 = (f32[4,288,288]{2,1,0:T(8,128)S(1)}, f32[4,3,288,288]{3,2,1,0:T(8,128)S(1)}, f32[4,288]{1,0:T(4,128)S(1)}, s32[4,4]{1,0:T(4,128)S(4)}, s32[4,4]{...) custom-call(s32[4,4]{1,0:T(4,128)} %cols_hbm.1, ...), custom_call_target="tpu_custom_call" | custom-call | flops 2654208 | bytes 5308416 | tf_op jit(solution)/shard_map/pallas_call | solution.py:426
  3.5 0.7 %collective-permute-start = (f32[4,384]{1,0:T(4,128)S(1)}, f32[4,384]{1,0:T(4,128)S(1)}, u32[]{:S(2)}, u32[]{:S(2)}) collective-permute-start(f32[4,384]{1,0:T(4,128)S(1)} %get-tuple-element.36), channel_id=1, source_target_pairs={{0,1},{1,2},{2,3},{3,4},{4,5},{5,6},{6,7},{7,8},{8,9},{9,10},{10,1... | collective-permute-start | bytes 18440 | tf_op jit(solution)/shard_map/ppermute | solution.py:445
  4.2 6.7 %collective-permute-start.1 = (f32[4,384]{1,0:T(4,128)S(1)}, f32[4,384]{1,0:T(4,128)S(1)}, u32[]{:S(2)}, u32[]{:S(2)}) collective-permute-start(f32[4,384]{1,0:T(4,128)S(1)} %get-tuple-element.37), channel_id=1, source_target_pairs={{0,30},{1,31},{2,4},{3,5},{4,2},{5,3},{6,8},{7,9},{8,6},{9,7},{10,... | collective-permute-start | bytes 18440 | tf_op jit(solution)/shard_map/ppermute | solution.py:419
  10.9 0.7 %collective-permute-start.2 = (f32[4,384]{1,0:T(4,128)S(1)}, f32[4,384]{1,0:T(4,128)S(1)}, u32[]{:S(2)}, u32[]{:S(2)}) collective-permute-start(f32[4,384]{1,0:T(4,128)S(1)} %get-tuple-element.38), channel_id=1, source_target_pairs={{1,0},{2,1},{3,2},{4,3},{5,4},{6,5},{7,6},{8,7},{9,8},{10,9},{11,1... | collective-permute-start | bytes 18440 | tf_op jit(solution)/shard_map/ppermute | solution.py:447
  11.6 0.3 %collective-permute-start.3 = (f32[4,384]{1,0:T(4,128)S(1)}, f32[4,384]{1,0:T(4,128)S(1)}, u32[]{:S(2)}, u32[]{:S(2)}) collective-permute-start(f32[4,384]{1,0:T(4,128)S(1)} %get-tuple-element.39), channel_id=1, source_target_pairs={{0,2},{1,3},{2,0},{3,1},{4,6},{5,7},{6,4},{7,5},{8,10},{9,11},{10,... | collective-permute-start | bytes 18440 | tf_op jit(solution)/shard_map/ppermute | solution.py:419
  12.0 1.7 %shard_map.69 = (f32[4,288,288]{2,1,0:T(8,128)S(1)}, f32[4,384]{1,0:T(4,128)S(1)}) custom-call(f32[4,4,288,288]{3,2,1,0:T(8,128)} %tiles_hbm.3, f32[4,384]{1,0:T(4,128)S(1)} %get-tuple-element.28.z.z_ref, f32[4,384]{1,0:T(4,128)S(1)} %get-tuple-element.34.near), custom_call_target="tpu_custom_call" | custom-call | flops 663552 | bytes 1327104 | tf_op jit(solution)/shard_map/pallas_call | solution.py:449
  13.7 0.0 collective-permute-done.forward_in
  13.7 0.0 collective-permute-done.1.odd_in
  13.7 0.0 collective-permute-done.2.back_in
  13.7 1.6 %collective-permute-done.3.even_in = f32[4,384]{1,0:T(4,128)S(1)} collective-permute-done((f32[4,384]{1,0:T(4,128)S(1)}, f32[4,384]{1,0:T(4,128)S(1)}, u32[]{:S(2)}, u32[]{:S(2)}) %collective-permute-start.3) | collective-permute-done | bytes 6176 | tf_op jit(solution)/shard_map/ppermute | solution.py:419
  15.3 1.2 %shard_map.71 = (f32[4,384]{1,0:T(4,128)S(1)}, f32[8,384]{1,0:T(8,128)S(1)}, f32[4,384]{1,0:T(4,128)S(1)}, f32[4,384]{1,0:T(4,128)S(1)}) custom-call(s32[4,4]{1,0:T(4,128)S(4)} %get-tuple-element.29.place, s32[4,4]{1,0:T(4,128)S(4)} %get-tuple-element.30.live, f32[4,3,288,288]{3,2,1,0:T(8,128)S(1)} %get-tuple-element.31.tiles, ...), custom_call_target="tpu_custom_call" | custom-call | flops 7962624 | bytes 15925248 | tf_op jit(solution)/shard_map/pallas_call | solution.py:458
  16.4 0.1 collective-permute-start.4
  16.5 0.3 %shard_map.72 = (f32[4,384]{1,0:T(4,128)S(1)}, f32[1,128]{1,0:T(1,128)S(1)}) custom-call(f32[4,288]{1,0:T(4,128)S(1)} %get-tuple-element.27.right, f32[4,288,288]{2,1,0:T(8,128)S(1)} %get-tuple-element.45.diagonal_tiles, f32[4,384]{1,0:T(4,128)S(1)} %get-tuple-element.43.image, f32[8,384]{1,0:T(8,128)S(1)} %get-tuple-element.44.swap, ...), custom_call_target="tpu_custom_call" | custom-call | flops 663552 | bytes 1327104 | tf_op jit(solution)/shard_map/pallas_call | solution.py:463
  16.8 0.8 %collective-permute-done.4.swapped = f32[8,384]{1,0:T(8,128)S(1)} collective-permute-done((f32[8,384]{1,0:T(8,128)S(1)}, f32[8,384]{1,0:T(8,128)S(1)}, u32[]{:S(2)}, u32[]{:S(2)}) %collective-permute-start.4) | collective-permute-done | bytes 12320 | tf_op jit(solution)/shard_map/ppermute | solution.py:411
  17.7 0.2 shard_map.73
  17.9 12.6 %all_to_all.5.gathered = f32[16,5,4,128]{3,2,1,0:T(4,128)S(1)} all-to-all(f32[16,5,4,128]{3,2,1,0:T(4,128)S(1)} %shard_map.73), channel_id=1, replica_groups={{0,2,4,6,8,10,12,14,16,18,20,22,24,26,28,30},{1,3,5,7,9,11,13,15,17,19,..., dimensions={0} | all-to-all | bytes 327680 | tf_op jit(solution)/shard_map/all_to_all | solution.py:470
  30.5 0.0 collective-permute-start.5
  30.5 0.3 shard_map.75.sums
  30.8 0.5 %collective-permute-start.6 = (f32[8,128]{1,0:T(8,128)S(1)}, f32[8,128]{1,0:T(8,128)S(1)}, u32[]{:S(2)}, u32[]{:S(2)}) collective-permute-start(f32[8,128]{1,0:T(8,128)S(1)} %shard_map.75.sums), channel_id=1, source_target_pairs={{0,1},{1,0},{2,3},{3,2},{4,5},{5,4},{6,7},{7,6},{8,9},{9,8},{10,11... | collective-permute-start | bytes 12296 | tf_op jit(solution)/shard_map/ppermute | solution.py:411
  31.3 0.3 %collective-permute-done.5.next_other = f32[5,4,128]{2,1,0:T(4,128)S(1)} collective-permute-done((f32[5,4,128]{2,1,0:T(4,128)S(1)}, f32[5,4,128]{2,1,0:T(4,128)S(1)}, u32[]{:S(2)}, u32[]{:S(2)}) %collective-permute-start.5) | collective-permute-done | bytes 10272 | tf_op jit(solution)/shard_map/ppermute | solution.py:411
  31.6 0.7 %shard_map.76 = (f32[4,384]{1,0:T(4,128)S(1)}, f32[4,384]{1,0:T(4,128)S(1)}) custom-call(s32[4,4]{1,0:T(4,128)S(4)} %get-tuple-element.29.place, s32[4,4]{1,0:T(4,128)S(4)} %get-tuple-element.30.live, s32[4]{0:T(128)S(4)} %get-tuple-element.33.spot, f32[4,3,288,288]{3,2,1,0:T(8,128)S(1)} %get-tuple-element.31.tiles, f32[8,384]{1,0:T(8,128)S(1)} %get-tuple-element.44.swap, ...), custom_call_target="tpu_custom_call" | custom-call | flops 2654208 | bytes 5308416 | tf_op jit(solution)/shard_map/pallas_call | solution.py:475
  32.3 0.0 collective-permute-done.6.sums_other
  32.3 0.9 %shard_map.77 = (f32[4,288]{1,0:T(4,128)}, f32[4,288]{1,0:T(4,128)}) custom-call(f32[4,288]{1,0:T(4,128)S(1)} %get-tuple-element.27.right, f32[4,384]{1,0:T(4,128)S(1)} %get-tuple-element.28.z.z_ref, f32[4,384]{1,0:T(4,128)S(1)} %get-tuple-element.43.image, f32[4,384]{1,0:T(4,128)S(1)} %get-tuple-element.50.product, f32[4,384]{1,0:T(4,128)S(1)} %get-tuple-element.51.scaled, ...), custom_call_target="tpu_custom_call" | custom-call | tf_op jit(solution)/shard_map/pallas_call | solution.py:479
  (2 shorter events, 0.0 us)
Async XLA Ops:
  3.5 10.2 %collective-permute-start = (f32[4,384]{1,0:T(4,128)S(1)}, f32[4,384]{1,0:T(4,128)S(1)}, u32[]{:S(2)}, u32[]{:S(2)}) collective-permute-start(f32[4,384]{1,0:T(4,128)S(1)} %get-tuple-element.36), channel_id=1, source_target_pairs={{0,1},{1,2},{2,3},{3,4},{4,5},{5,6},{6,7},{7,8},{8,9},{9,10},{10,1... | collective-permute-start | bytes 18440 | tf_op jit(solution)/shard_map/ppermute | solution.py:445
  4.2 9.5 %collective-permute-start.1 = (f32[4,384]{1,0:T(4,128)S(1)}, f32[4,384]{1,0:T(4,128)S(1)}, u32[]{:S(2)}, u32[]{:S(2)}) collective-permute-start(f32[4,384]{1,0:T(4,128)S(1)} %get-tuple-element.37), channel_id=1, source_target_pairs={{0,30},{1,31},{2,4},{3,5},{4,2},{5,3},{6,8},{7,9},{8,6},{9,7},{10,... | collective-permute-start | bytes 18440 | tf_op jit(solution)/shard_map/ppermute | solution.py:419
  10.9 2.8 %collective-permute-start.2 = (f32[4,384]{1,0:T(4,128)S(1)}, f32[4,384]{1,0:T(4,128)S(1)}, u32[]{:S(2)}, u32[]{:S(2)}) collective-permute-start(f32[4,384]{1,0:T(4,128)S(1)} %get-tuple-element.38), channel_id=1, source_target_pairs={{1,0},{2,1},{3,2},{4,3},{5,4},{6,5},{7,6},{8,7},{9,8},{10,9},{11,1... | collective-permute-start | bytes 18440 | tf_op jit(solution)/shard_map/ppermute | solution.py:447
  11.6 3.6 %collective-permute-start.3 = (f32[4,384]{1,0:T(4,128)S(1)}, f32[4,384]{1,0:T(4,128)S(1)}, u32[]{:S(2)}, u32[]{:S(2)}) collective-permute-start(f32[4,384]{1,0:T(4,128)S(1)} %get-tuple-element.39), channel_id=1, source_target_pairs={{0,2},{1,3},{2,0},{3,1},{4,6},{5,7},{6,4},{7,5},{8,10},{9,11},{10,... | collective-permute-start | bytes 18440 | tf_op jit(solution)/shard_map/ppermute | solution.py:419
  16.4 1.2 %collective-permute-start.4 = (f32[8,384]{1,0:T(8,128)S(1)}, f32[8,384]{1,0:T(8,128)S(1)}, u32[]{:S(2)}, u32[]{:S(2)}) collective-permute-start(f32[8,384]{1,0:T(8,128)S(1)} %get-tuple-element.44.swap), channel_id=1, source_target_pairs={{0,1},{1,0},{2,3},{3,2},{4,5},{5,4},{6,7},{7,6},{8,9},{9,8},{10,11... | collective-permute-start | bytes 36872 | tf_op jit(solution)/shard_map/ppermute | solution.py:411
  30.5 1.2 %collective-permute-start.5 = (f32[5,4,128]{2,1,0:T(4,128)S(1)}, f32[5,4,128]{2,1,0:T(4,128)S(1)}, u32[]{:S(2)}, u32[]{:S(2)}) collective-permute-start(f32[5,4,128]{2,1,0:T(4,128)S(1)} %shard_map.74.next_part), channel_id=1, source_target_pairs={{0,1},{1,0},{2,3},{3,2},{4,5},{5,4},{6,7},{7,6},{8,9},{9,8},{10,11... | collective-permute-start | bytes 30728 | tf_op jit(solution)/shard_map/ppermute | solution.py:411
  30.8 1.5 %collective-permute-start.6 = (f32[8,128]{1,0:T(8,128)S(1)}, f32[8,128]{1,0:T(8,128)S(1)}, u32[]{:S(2)}, u32[]{:S(2)}) collective-permute-start(f32[8,128]{1,0:T(8,128)S(1)} %shard_map.75.sums), channel_id=1, source_target_pairs={{0,1},{1,0},{2,3},{3,2},{4,5},{5,4},{6,7},{7,6},{8,9},{9,8},{10,11... | collective-permute-start | bytes 12296 | tf_op jit(solution)/shard_map/ppermute | solution.py:411

commit v4 on v3

--- a/solution.py
+++ b/solution.py
@@ -214,13 +214,12 @@
     near[...] = sums[:blocks]
     swap[blocks : 2 * blocks, :] = sums[blocks : 2 * blocks]
     values = [size, total(right[...] * z[:, :width]), total(z[...] * q)]
-    swap[0:1, :] = swap[0:1, :] + lay_scalars(values, lanes, width)
+    for i, value in enumerate(values):
+        swap[2 * blocks + i : 2 * blocks + i + 1, :] = jnp.broadcast_to(value, (1, lanes))
 
 
 def second_diagonal_kernel(blocks, width, right, diagonal_tiles, image, swap, near, near_out, out):
-    lanes = padded(width)
-    keep = iota((blocks, lanes), 1) < width
-    w = jnp.where(keep, swap[:blocks, :], 0.0)
+    w = swap[:blocks, :]
     diagonal_product(blocks, width, diagonal_tiles, swap, near_out)
     diagonal = near_out[...]
     values = [
@@ -257,25 +256,25 @@
     rows, other = swap[...], swapped[...]
 
     def at(block, i):
-        return block[0:1, width + i : width + i + 1]
+        return block[2 * blocks + i : 2 * blocks + i + 1]
 
     mine, theirs = at(rows, 0), at(other, 0)
     scale = jnp.where(second, mine, jnp.maximum(mine, theirs))
     sent = far[...] * (mine / scale) + jnp.where(
-        second, 0.0, other[blocks:] * (theirs / scale)
+        second, 0.0, other[blocks : 2 * blocks] * (theirs / scale)
     )
-    crossing = total(rows[blocks:, :width] * other[:blocks, :width])
+    crossing = total(rows[blocks : 2 * blocks] * other[:blocks])
     values = [
-        mine,
-        scale,
-        at(rows, 1) + at(other, 1),
-        at(rows, 2) + at(other, 2),
+        mine[:, :128],
+        scale[:, :128],
+        (at(rows, 1) + at(other, 1))[:, :128],
+        (at(rows, 2) + at(other, 2))[:, :128],
         dots[0:1, 0:1],
-        dots[0:1, 1:2] / mine,
-        at(rows, 2),
+        dots[0:1, 1:2] / mine[:, :1],
+        at(rows, 2)[:, :128],
         dots[0:1, 2:3],
         jnp.where(second, 0.0, 2.0 * crossing),
-        theirs,
+        theirs[:, :128],
     ]
     extra = lay_scalars(values, 128, 2 * (width - 256))
     parts = fold(rows[:blocks], sent, width, extra)
@@ -319,54 +318,58 @@
         pair = gathered[e, 2] * gathered[n, 0] + gathered[e, 3] * gathered[n, 1] + ends
         lines.append(jnp.sum(pair, axis=0, keepdims=True))
     edges = total(jnp.concatenate(lines, axis=0) * weight)
-    values = [fresh, diagonal + 2.0 * edges, norm, along]
-    out[...] = jnp.broadcast_to(lay_scalars(values, 128, 0), out.shape)
-
-
-def later_kernel(blocks, slots, width,
-                 place, live, spot, tiles, swap, swapped, near, gathered, next_part, next_other, sums,
-                 product, scaled, wide):
+    values = [fresh, diagonal + 2.0 * edges, norm, along, alpha, 1.0 / norm, along / norm]
+    for i, value in enumerate(values):
+        out[i : i + 1, :] = jnp.broadcast_to(value, (1, out.shape[1]))
+
+
+def prepare_kernel(blocks, width, spot, swap, swapped, near, gathered, next_part, sums,
+                   known, scaled, factor, wide):
     chips = gathered.shape[0]
-    lanes = padded(width)
     chip, second, _ = where_am_i(spot)
     tail = width - 256
     before = gathered[jnp.where(chip == 0, chips - 1, chip - 1)]
-    alpha = sums[0:1, 2:3] / sums[0:1, 3:4]
+    ahead = next_part[...]
+    alpha = sums[4:5, :]
 
     def at(part, i):
         return alpha * part[4, 0:1, 2 * tail + i : 2 * tail + i + 1]
 
-    mine = alpha * swap[0:1, width : width + 1]
-    theirs = alpha * swapped[0:1, width : width + 1]
-    keep = iota((blocks, lanes), 1) < width
-    w = jnp.where(keep, swap[:blocks, :], 0.0) * mine
-    w_other = jnp.where(keep, swapped[:blocks, :], 0.0) * theirs
-    ahead, ahead_other = next_part[...], next_other[...]
-    ahead = unfold_first(ahead, width) * at(ahead, 0)
-    ahead_other = unfold_first(ahead_other, width) * at(ahead_other, 0)
+    mine = alpha * swap[2 * blocks : 2 * blocks + 1, :]
+    theirs = alpha * swapped[2 * blocks : 2 * blocks + 1, :]
+    w = swap[:blocks, :] * mine
     scaled[...] = w
+    factor[...] = at(ahead, 9)
     spread_rows(wide, w, 0)
-    spread_rows(wide, jnp.where(second, ahead_other, w_other), blocks)
-    spread_rows(wide, ahead, 2 * blocks)
-    known = near[...] * mine + unfold_second(before, width) * at(before, 1)
-    product[...] = known + jnp.where(second, swapped[blocks:, :] * theirs, 0.0)
+    spread_rows(wide, swapped[:blocks, :] * theirs, blocks)
+    spread_rows(wide, unfold_first(ahead, width) * at(ahead, 0), 2 * blocks)
+    here = near[...] * mine + unfold_second(before, width) * at(before, 1)
+    known[...] = here + jnp.where(second, swapped[blocks : 2 * blocks, :] * theirs, 0.0)
+
+
+def later_kernel(blocks, slots, width,
+                 place, live, spot, tiles, known, factor, ready, next_other,
+                 product, wide):
+    _, second, _ = where_am_i(spot)
+    wide[...] = ready[...]
+
+    @pl.when(second)
+    def _():
+        spread_rows(wide, unfold_first(next_other[...], width) * factor[...], blocks)
 
     for g in range(blocks):
         columns = upper_columns(tiles, place, live, wide, g, slots, width)
-        product[g : g + 1, :] = product[g : g + 1, :] + columns_to_row(columns, width)
+        product[g : g + 1, :] = known[g : g + 1, :] + columns_to_row(columns, width)
 
 
 def end_kernel(blocks, width, right, z_ref, image, product, scaled, sums, sums_other,
                update, residual):
-    def shared(i):
-        return sums[0:1, i : i + 1] + sums_other[0:1, i : i + 1]
-
-    norm, along = sums[0:1, 2:3], sums[0:1, 3:4]
-    alpha = norm / along
-    fresh = norm + shared(0)
-    curved = along + shared(1)
-    ratio = fresh / norm
-    step = fresh / (curved - ratio * (fresh / alpha))
+    norm, along = sums[2:3, :], sums[3:4, :]
+    alpha = sums[4:5, :]
+    fresh = norm + (sums[0:1, :] + sums_other[0:1, :])
+    curved = along + (sums[1:2, :] + sums_other[1:2, :])
+    ratio = fresh * sums[5:6, :]
+    step = fresh / (curved - ratio * (fresh * sums[6:7, :]))
     z, q = z_ref[...], image[...]
     z_next = z - scaled[...]
     update[...] = (alpha * z + step * (z_next + ratio * z))[:, :width]
@@ -384,7 +387,8 @@
     hbm = pl.BlockSpec(memory_space=pltpu.HBM)
     rows = pltpu.VMEM((2 * blocks, lanes), F32)
     half = pltpu.VMEM((blocks, lanes), F32)
-    small = pltpu.VMEM((8, 128), F32)
+    small = pltpu.VMEM((8, lanes), F32)
+    more = pltpu.VMEM((4 * blocks, lanes), F32)
     spread = pltpu.VMEM(((BAND + 1) * blocks, 8, lanes), F32)
     index = pltpu.SMEM((blocks, slots), jnp.int32)
 
@@ -456,7 +460,7 @@
         spot, near1, forward_in, odd_in, back_in, even_in
     )
     image, swap, far, near2 = call(
-        middle_kernel, sizes, [smem] * 2 + [vmem] * 7, [half, rows, half, half], [spread, spread],
+        middle_kernel, sizes, [smem] * 2 + [vmem] * 7, [half, more, half, half], [spread, spread],
         work=3 * blocks * slots,
     )(place, live, tiles, jacobi, z, known, one, two, right)
     swapped = swap_cores(swap)
@@ -472,9 +476,13 @@
     next_other = swap_cores(next_part)
     sums = call(sums_kernel, (blocks, width), [vmem], small, work=chips)(gathered)
     sums_other = swap_cores(sums)
-    product, scaled = call(
-        later_kernel, sizes, [smem] * 3 + [vmem] * 8, [half, half], [spread], work=blocks * slots,
-    )(place, live, spot, tiles, swap, swapped, near3, gathered, next_part, next_other, sums)
+    known2, scaled, factor, ready = call(
+        prepare_kernel, (blocks, width), [smem] + [vmem] * 6,
+        [half, half, pltpu.VMEM((1, lanes), F32), spread],
+    )(spot, swap, swapped, near3, gathered, next_part, sums)
+    product = call(
+        later_kernel, sizes, [smem] * 3 + [vmem] * 5, half, [spread], work=100 * blocks * slots,
+    )(place, live, spot, tiles, known2, factor, ready, next_other)
     out = jax.ShapeDtypeStruct(right_side.shape, F32)
     return call(end_kernel, (blocks, width), [vmem] * 7, [out, out])(
         right, z, image, product, scaled, sums, sums_other

time: 33.3 us -> 32.8 us (0.985)
    pallas_call x2 -> x3, Pallas kernels: 1.82 us -> 1.74 us  [the longest x1 1.17 us: on_device(): call(middle_kernel, sizes, [smem] * 2 + [vmem] * 7, [half, more, half, ha...]
where the time goes in v4:
time: 32.8 us; the launch traced here: 32.9 us
  blocking collectives  12.6 us (38%)
  starting transfers between devices  9.07 us (28%)
  Pallas kernels  7.88 us (24%)
  waiting for transfers between devices  2.63 us (8%)
  between operations  0.71 us (2%)
    all_to_all x1, blocking collectives, on_device(): gathered = lax.all_to_all(sent, AXIS, 0, 0, axis_index_groups=groups)  12.6 us
    ppermute x2, starting transfers between devices, swap_chips(): return lax.ppermute(value, AXIS, pairs)  6.86 us
    pallas_call x1, Pallas kernels, on_device(): call(begin_kernel, sizes + (count,), [hbm] * 5, [pltpu.VMEM(jacobi_invers...  3.01 us
    pallas_call x1, Pallas kernels, on_device(): call(first_diagonal_kernel, (blocks, width), [hbm, vmem, vmem], [pltpu.VM...  1.69 us
    ppermute x2, waiting for transfers between devices, swap_chips(): return lax.ppermute(value, AXIS, pairs)  1.53 us
    pallas_call x1, Pallas kernels, on_device(): call(middle_kernel, sizes, [smem] * 2 + [vmem] * 7, [half, more, half, ha...  1.17 us
    ppermute x3, waiting for transfers between devices, swap_cores(): return lax.ppermute(value, AXIS, [(i, i ^ 1) for i in range(count)])  1.1 us
    ppermute x1, starting transfers between devices, on_device(): lax.ppermute(back_out, AXIS, [((i + 1) % count, i) for i in range(count)])  1.06 us
  transfers between devices with their start and end apart: 7, of which 3 were waited for; matrix products, arithmetic and copies ran while one was open for 0% of the time, Pallas kernels for 9%

profile of v4, /device:TPU:0, one launch (start us, length us, event | category | flops | bytes accessed | tf_op | source)
XLA Modules:
  0.0 32.9 jit_solution(6437723429071686747)
XLA Ops:
  0.6 3.0 %shard_map.68 = (f32[4,288,288]{2,1,0:T(8,128)S(1)}, f32[4,3,288,288]{3,2,1,0:T(8,128)S(1)}, f32[4,288]{1,0:T(4,128)S(1)}, s32[4,4]{1,0:T(4,128)S(4)}, s32[4,4]{...) custom-call(s32[4,4]{1,0:T(4,128)} %cols_hbm.1, ...), custom_call_target="tpu_custom_call" | custom-call | flops 2654208 | bytes 5308416 | tf_op jit(solution)/shard_map/pallas_call | solution.py:430
  3.7 0.6 %collective-permute-start = (f32[4,384]{1,0:T(4,128)S(1)}, f32[4,384]{1,0:T(4,128)S(1)}, u32[]{:S(2)}, u32[]{:S(2)}) collective-permute-start(f32[4,384]{1,0:T(4,128)S(1)} %get-tuple-element.38), channel_id=1, source_target_pairs={{0,1},{1,2},{2,3},{3,4},{4,5},{5,6},{6,7},{7,8},{8,9},{9,10},{10,1... | collective-permute-start | bytes 18440 | tf_op jit(solution)/shard_map/ppermute | solution.py:449
  4.2 6.5 %collective-permute-start.1 = (f32[4,384]{1,0:T(4,128)S(1)}, f32[4,384]{1,0:T(4,128)S(1)}, u32[]{:S(2)}, u32[]{:S(2)}) collective-permute-start(f32[4,384]{1,0:T(4,128)S(1)} %get-tuple-element.39), channel_id=1, source_target_pairs={{0,30},{1,31},{2,4},{3,5},{4,2},{5,3},{6,8},{7,9},{8,6},{9,7},{10,... | collective-permute-start | bytes 18440 | tf_op jit(solution)/shard_map/ppermute | solution.py:423
  10.7 1.1 %collective-permute-start.2 = (f32[4,384]{1,0:T(4,128)S(1)}, f32[4,384]{1,0:T(4,128)S(1)}, u32[]{:S(2)}, u32[]{:S(2)}) collective-permute-start(f32[4,384]{1,0:T(4,128)S(1)} %get-tuple-element.40), channel_id=1, source_target_pairs={{1,0},{2,1},{3,2},{4,3},{5,4},{6,5},{7,6},{8,7},{9,8},{10,9},{11,1... | collective-permute-start | bytes 18440 | tf_op jit(solution)/shard_map/ppermute | solution.py:451
  11.8 0.4 %collective-permute-start.3 = (f32[4,384]{1,0:T(4,128)S(1)}, f32[4,384]{1,0:T(4,128)S(1)}, u32[]{:S(2)}, u32[]{:S(2)}) collective-permute-start(f32[4,384]{1,0:T(4,128)S(1)} %get-tuple-element.41), channel_id=1, source_target_pairs={{0,2},{1,3},{2,0},{3,1},{4,6},{5,7},{6,4},{7,5},{8,10},{9,11},{10,... | collective-permute-start | bytes 18440 | tf_op jit(solution)/shard_map/ppermute | solution.py:423
  12.1 1.7 %shard_map.69 = (f32[4,288,288]{2,1,0:T(8,128)S(1)}, f32[4,384]{1,0:T(4,128)S(1)}) custom-call(f32[4,4,288,288]{3,2,1,0:T(8,128)} %tiles_hbm.3, f32[4,384]{1,0:T(4,128)S(1)} %get-tuple-element.30.z.z_ref, f32[4,384]{1,0:T(4,128)S(1)} %get-tuple-element.36.near), custom_call_target="tpu_custom_call" | custom-call | flops 663552 | bytes 1327104 | tf_op jit(solution)/shard_map/pallas_call | solution.py:453
  13.8 0.0 collective-permute-done.forward_in
  13.8 0.0 collective-permute-done.1.odd_in
  13.9 0.0 collective-permute-done.2.back_in
  13.9 1.5 %collective-permute-done.3.even_in = f32[4,384]{1,0:T(4,128)S(1)} collective-permute-done((f32[4,384]{1,0:T(4,128)S(1)}, f32[4,384]{1,0:T(4,128)S(1)}, u32[]{:S(2)}, u32[]{:S(2)}) %collective-permute-start.3) | collective-permute-done | bytes 6176 | tf_op jit(solution)/shard_map/ppermute | solution.py:423
  15.4 1.2 %shard_map.71 = (f32[4,384]{1,0:T(4,128)S(1)}, f32[16,384]{1,0:T(8,128)S(1)}, f32[4,384]{1,0:T(4,128)S(1)}, f32[4,384]{1,0:T(4,128)S(1)}) custom-call(s32[4,4]{1,0:T(4,128)S(4)} %get-tuple-element.31.place, s32[4,4]{1,0:T(4,128)S(4)} %get-tuple-element.32.live, f32[4,3,288,288]{3,2,1,0:T(8,128)S(1)} %get-tuple-element.33.tiles, ...), custom_call_target="tpu_custom_call" | custom-call | flops 7962624 | bytes 15925248 | tf_op jit(solution)/shard_map/pallas_call | solution.py:462
  16.6 0.1 collective-permute-start.4
  16.7 0.3 %shard_map.72 = (f32[4,384]{1,0:T(4,128)S(1)}, f32[1,128]{1,0:T(1,128)S(1)}) custom-call(f32[4,288]{1,0:T(4,128)S(1)} %get-tuple-element.29.right, f32[4,288,288]{2,1,0:T(8,128)S(1)} %get-tuple-element.47.diagonal_tiles, f32[4,384]{1,0:T(4,128)S(1)} %get-tuple-element.45.image, f32[16,384]{1,0:T(8,128)S(1)} %get-tuple-element.46.swap, ...), custom_call_target="tpu_custom_call" | custom-call | flops 663552 | bytes 1327104 | tf_op jit(solution)/shard_map/pallas_call | solution.py:467
  17.0 0.8 %collective-permute-done.4.swapped = f32[16,384]{1,0:T(8,128)S(1)} collective-permute-done((f32[16,384]{1,0:T(8,128)S(1)}, f32[16,384]{1,0:T(8,128)S(1)}, u32[]{:S(2)}, u32[]{:S(2)}) %collective-permute-start.4) | collective-permute-done | bytes 24608 | tf_op jit(solution)/shard_map/ppermute | solution.py:415
  17.8 0.2 shard_map.73
  18.0 12.6 %all_to_all.5.gathered = f32[16,5,4,128]{3,2,1,0:T(4,128)S(1)} all-to-all(f32[16,5,4,128]{3,2,1,0:T(4,128)S(1)} %shard_map.73), channel_id=1, replica_groups={{0,2,4,6,8,10,12,14,16,18,20,22,24,26,28,30},{1,3,5,7,9,11,13,15,17,19,..., dimensions={0} | all-to-all | bytes 327680 | tf_op jit(solution)/shard_map/all_to_all | solution.py:474
  30.6 0.0 collective-permute-start.5
  30.6 0.3 shard_map.75.sums
  30.9 0.5 %collective-permute-start.6 = (f32[8,384]{1,0:T(8,128)S(1)}, f32[8,384]{1,0:T(8,128)S(1)}, u32[]{:S(2)}, u32[]{:S(2)}) collective-permute-start(f32[8,384]{1,0:T(8,128)S(1)} %shard_map.75.sums), channel_id=1, source_target_pairs={{0,1},{1,0},{2,3},{3,2},{4,5},{5,4},{6,7},{7,6},{8,9},{9,8},{10,11... | collective-permute-start | bytes 36872 | tf_op jit(solution)/shard_map/ppermute | solution.py:415
  31.4 0.1 shard_map.76
  31.5 0.2 collective-permute-done.5.next_other
  31.8 0.5 %shard_map.77.product = f32[4,384]{1,0:T(4,128)S(1)} custom-call(s32[4,4]{1,0:T(4,128)S(4)} %get-tuple-element.31.place, s32[4,4]{1,0:T(4,128)S(4)} %get-tuple-element.32.live, s32[4]{0:T(128)S(4)} %get-tuple-element.35.spot, f32[4,3,288,288]{3,2,1,0:T(8,128)S(1)} %get-tuple-element.33.tiles, f32[4,384]{1,0:T(4,128)S(1)} %get-tuple-element.52.known, ...), custom_call_target="tpu_custom_call" | custom-call | flops 265420800 | bytes 530841600 | tf_op jit(solution)/shard_map/pallas_call | solution.py:483
  32.3 0.0 collective-permute-done.6.sums_other
  32.3 0.6 %shard_map.78 = (f32[4,288]{1,0:T(4,128)}, f32[4,288]{1,0:T(4,128)}) custom-call(f32[4,288]{1,0:T(4,128)S(1)} %get-tuple-element.29.right, f32[4,384]{1,0:T(4,128)S(1)} %get-tuple-element.30.z.z_ref, f32[4,384]{1,0:T(4,128)S(1)} %get-tuple-element.45.image, f32[4,384]{1,0:T(4,128)S(1)} %shard_map.77.product, f32[4,384]{1,0:T(4,128)S(1)} %get-tuple-element.55.scaled, ...), custom_call_target="tpu_custom_call" | custom-call | tf_op jit(solution)/shard_map/pallas_call | solution.py:487
  (2 shorter events, 0.0 us)
Async XLA Ops:
  3.7 10.2 %collective-permute-start = (f32[4,384]{1,0:T(4,128)S(1)}, f32[4,384]{1,0:T(4,128)S(1)}, u32[]{:S(2)}, u32[]{:S(2)}) collective-permute-start(f32[4,384]{1,0:T(4,128)S(1)} %get-tuple-element.38), channel_id=1, source_target_pairs={{0,1},{1,2},{2,3},{3,4},{4,5},{5,6},{6,7},{7,8},{8,9},{9,10},{10,1... | collective-permute-start | bytes 18440 | tf_op jit(solution)/shard_map/ppermute | solution.py:449
  4.2 9.6 %collective-permute-start.1 = (f32[4,384]{1,0:T(4,128)S(1)}, f32[4,384]{1,0:T(4,128)S(1)}, u32[]{:S(2)}, u32[]{:S(2)}) collective-permute-start(f32[4,384]{1,0:T(4,128)S(1)} %get-tuple-element.39), channel_id=1, source_target_pairs={{0,30},{1,31},{2,4},{3,5},{4,2},{5,3},{6,8},{7,9},{8,6},{9,7},{10,... | collective-permute-start | bytes 18440 | tf_op jit(solution)/shard_map/ppermute | solution.py:423
  10.7 3.2 %collective-permute-start.2 = (f32[4,384]{1,0:T(4,128)S(1)}, f32[4,384]{1,0:T(4,128)S(1)}, u32[]{:S(2)}, u32[]{:S(2)}) collective-permute-start(f32[4,384]{1,0:T(4,128)S(1)} %get-tuple-element.40), channel_id=1, source_target_pairs={{1,0},{2,1},{3,2},{4,3},{5,4},{6,5},{7,6},{8,7},{9,8},{10,9},{11,1... | collective-permute-start | bytes 18440 | tf_op jit(solution)/shard_map/ppermute | solution.py:451
  11.8 3.6 %collective-permute-start.3 = (f32[4,384]{1,0:T(4,128)S(1)}, f32[4,384]{1,0:T(4,128)S(1)}, u32[]{:S(2)}, u32[]{:S(2)}) collective-permute-start(f32[4,384]{1,0:T(4,128)S(1)} %get-tuple-element.41), channel_id=1, source_target_pairs={{0,2},{1,3},{2,0},{3,1},{4,6},{5,7},{6,4},{7,5},{8,10},{9,11},{10,... | collective-permute-start | bytes 18440 | tf_op jit(solution)/shard_map/ppermute | solution.py:423
  16.6 1.3 %collective-permute-start.4 = (f32[16,384]{1,0:T(8,128)S(1)}, f32[16,384]{1,0:T(8,128)S(1)}, u32[]{:S(2)}, u32[]{:S(2)}) collective-permute-start(f32[16,384]{1,0:T(8,128)S(1)} %get-tuple-element.46.swap), channel_id=1, source_target_pairs={{0,1},{1,0},{2,3},{3,2},{4,5},{5,4},{6,7},{7,6},{8,9},{9,8},{10,11... | collective-permute-start | bytes 73736 | tf_op jit(solution)/shard_map/ppermute | solution.py:415
  30.6 1.2 %collective-permute-start.5 = (f32[5,4,128]{2,1,0:T(4,128)S(1)}, f32[5,4,128]{2,1,0:T(4,128)S(1)}, u32[]{:S(2)}, u32[]{:S(2)}) collective-permute-start(f32[5,4,128]{2,1,0:T(4,128)S(1)} %shard_map.74.next_part), channel_id=1, source_target_pairs={{0,1},{1,0},{2,3},{3,2},{4,5},{5,4},{6,7},{7,6},{8,9},{9,8},{10,11... | collective-permute-start | bytes 30728 | tf_op jit(solution)/shard_map/ppermute | solution.py:415
  30.9 1.4 %collective-permute-start.6 = (f32[8,384]{1,0:T(8,128)S(1)}, f32[8,384]{1,0:T(8,128)S(1)}, u32[]{:S(2)}, u32[]{:S(2)}) collective-permute-start(f32[8,384]{1,0:T(8,128)S(1)} %shard_map.75.sums), channel_id=1, source_target_pairs={{0,1},{1,0},{2,3},{3,2},{4,5},{5,4},{6,7},{7,6},{8,9},{9,8},{10,11... | collective-permute-start | bytes 36872 | tf_op jit(solution)/shard_map/ppermute | solution.py:415

commit v5 on v4

--- a/solution.py
+++ b/solution.py
@@ -132,21 +132,25 @@
     spread[...] = jnp.zeros_like(spread)
     small[2].wait()
 
+    every = []
     for g in range(blocks):
         jacobi_copy(g).wait()
         columns = times_row(
             lambda i: jacobi[g, 8 * i : 8 * i + 8, :], right[g : g + 1, :], width
         )
         z[g : g + 1, :] = columns_to_row(columns, width)
+        every.append(columns)
+    for g in range(blocks):
+        columns = every[g]
 
         @pl.loop(1, counts[g])
         def _(k):
             tile_copy(g, k).wait()
 
         scatter_products(tiles, place, live, g, columns, slots, width, spread)
-    sums = jnp.sum(spread[...], axis=1)
-    near[...] = sums[:blocks]
-    one, two = sums[blocks : 2 * blocks], sums[2 * blocks :]
+    near[...] = spread[:blocks]
+    sums = jnp.sum(spread[blocks:], axis=1)
+    one, two = sums[:blocks], sums[blocks:]
     _, _, odd = where_am_i(spot)
     rows = z[...]
     one_out[...] = one
@@ -173,7 +177,7 @@
     for copy in copies:
         copy.wait()
     diagonal_product(blocks, width, diagonal, z, near_out)
-    near_out[...] = near_out[...] + near[...]
+    near_out[...] = near_out[...] + jnp.sum(near[...], axis=1)
 
 
 def join_kernel(spot, near, forward_in, odd_in, back_in, even_in, known, one, two):
@@ -391,6 +395,7 @@
     more = pltpu.VMEM((4 * blocks, lanes), F32)
     spread = pltpu.VMEM(((BAND + 1) * blocks, 8, lanes), F32)
     index = pltpu.SMEM((blocks, slots), jnp.int32)
+    late = pltpu.VMEM((blocks, 8, lanes), F32)
 
     def call(kernel, sizes, in_specs, out_shape, scratch=(), work=0):
         single = not isinstance(out_shape, list)
@@ -434,7 +439,7 @@
             pltpu.VMEM((blocks, slots - 1, width, width), F32),
             pltpu.VMEM(right_side.shape, F32),
             index, index, pltpu.SMEM((4,), jnp.int32),
-            half, half, half, half, half, half,
+            half, late, half, half, half, half,
         ],
         [
             pltpu.SMEM(block_cols.shape, jnp.int32),

time: 32.8 us -> 33.1 us (level); the launches traced: 32.9 us -> 32.7 us
  starting transfers between devices: 9.07 us -> 8.65 us
  waiting for transfers between devices: 2.63 us -> 3.01 us
    ppermute x2, starting transfers between devices: 6.86 us -> 6.19 us  [swap_chips(): return lax.ppermute(value, AXIS, pairs)]
    ppermute x2, waiting for transfers between devices: 1.53 us -> 1.9 us  [swap_chips(): return lax.ppermute(value, AXIS, pairs)]
where the time goes in v5:
time: 33.1 us; the launch traced here: 32.7 us
  blocking collectives  12.6 us (38%)
  starting transfers between devices  8.65 us (26%)
  Pallas kernels  7.74 us (23%)
  waiting for transfers between devices  3.01 us (9%)
  between operations  0.71 us (2%)
    all_to_all x1, blocking collectives, on_device(): gathered = lax.all_to_all(sent, AXIS, 0, 0, axis_index_groups=groups)  12.6 us
    ppermute x2, starting transfers between devices, swap_chips(): return lax.ppermute(value, AXIS, pairs)  6.19 us
    pallas_call x1, Pallas kernels, on_device(): call(begin_kernel, sizes + (count,), [hbm] * 5, [pltpu.VMEM(jacobi_invers...  2.91 us
    ppermute x2, waiting for transfers between devices, swap_chips(): return lax.ppermute(value, AXIS, pairs)  1.9 us
    pallas_call x1, Pallas kernels, on_device(): call(first_diagonal_kernel, (blocks, width), [hbm, vmem, vmem], [pltpu.VM...  1.69 us
    pallas_call x1, Pallas kernels, on_device(): call(middle_kernel, sizes, [smem] * 2 + [vmem] * 7, [half, more, half, ha...  1.14 us
    ppermute x3, waiting for transfers between devices, swap_cores(): return lax.ppermute(value, AXIS, [(i, i ^ 1) for i in range(count)])  1.11 us
    ppermute x1, starting transfers between devices, on_device(): lax.ppermute(back_out, AXIS, [((i + 1) % count, i) for i in range(count)])  1.09 us
  transfers between devices with their start and end apart: 7, of which 3 were waited for; matrix products, arithmetic and copies ran while one was open for 0% of the time, Pallas kernels for 9%

profile of v5, /device:TPU:0, one launch (start us, length us, event | category | flops | bytes accessed | tf_op | source)
XLA Modules:
  0.0 32.7 jit_solution(18134222095552783803)
XLA Ops:
  0.6 2.9 %shard_map.68 = (f32[4,288,288]{2,1,0:T(8,128)S(1)}, f32[4,3,288,288]{3,2,1,0:T(8,128)S(1)}, f32[4,288]{1,0:T(4,128)S(1)}, s32[4,4]{1,0:T(4,128)S(4)}, s32[4,4]{...) custom-call(s32[4,4]{1,0:T(4,128)} %cols_hbm.1, ...), custom_call_target="tpu_custom_call" | custom-call | flops 2654208 | bytes 5308416 | tf_op jit(solution)/shard_map/pallas_call | solution.py:435
  3.5 0.8 %collective-permute-start = (f32[4,384]{1,0:T(4,128)S(1)}, f32[4,384]{1,0:T(4,128)S(1)}, u32[]{:S(2)}, u32[]{:S(2)}) collective-permute-start(f32[4,384]{1,0:T(4,128)S(1)} %get-tuple-element.38), channel_id=1, source_target_pairs={{0,1},{1,2},{2,3},{3,4},{4,5},{5,6},{6,7},{7,8},{8,9},{9,10},{10,1... | collective-permute-start | bytes 18440 | tf_op jit(solution)/shard_map/ppermute | solution.py:454
  4.3 6.2 %collective-permute-start.1 = (f32[4,384]{1,0:T(4,128)S(1)}, f32[4,384]{1,0:T(4,128)S(1)}, u32[]{:S(2)}, u32[]{:S(2)}) collective-permute-start(f32[4,384]{1,0:T(4,128)S(1)} %get-tuple-element.39), channel_id=1, source_target_pairs={{0,30},{1,31},{2,4},{3,5},{4,2},{5,3},{6,8},{7,9},{8,6},{9,7},{10,... | collective-permute-start | bytes 18440 | tf_op jit(solution)/shard_map/ppermute | solution.py:428
  10.5 1.1 %collective-permute-start.2 = (f32[4,384]{1,0:T(4,128)S(1)}, f32[4,384]{1,0:T(4,128)S(1)}, u32[]{:S(2)}, u32[]{:S(2)}) collective-permute-start(f32[4,384]{1,0:T(4,128)S(1)} %get-tuple-element.40), channel_id=1, source_target_pairs={{1,0},{2,1},{3,2},{4,3},{5,4},{6,5},{7,6},{8,7},{9,8},{10,9},{11,1... | collective-permute-start | bytes 18440 | tf_op jit(solution)/shard_map/ppermute | solution.py:456
  11.6 0.0 collective-permute-start.3
  11.6 1.7 %shard_map.69 = (f32[4,288,288]{2,1,0:T(8,128)S(1)}, f32[4,384]{1,0:T(4,128)S(1)}) custom-call(f32[4,4,288,288]{3,2,1,0:T(8,128)} %tiles_hbm.3, f32[4,384]{1,0:T(4,128)S(1)} %get-tuple-element.30.z.z_ref, f32[4,8,384]{2,1,0:T(8,128)S(1)} %get-tuple-element.36.near), custom_call_target="tpu_custom_call" | custom-call | flops 663552 | bytes 1327104 | tf_op jit(solution)/shard_map/pallas_call | solution.py:458
  13.3 0.0 collective-permute-done.forward_in
  13.3 0.0 collective-permute-done.1.odd_in
  13.3 0.0 collective-permute-done.2.back_in
  13.3 1.9 %collective-permute-done.3.even_in = f32[4,384]{1,0:T(4,128)S(1)} collective-permute-done((f32[4,384]{1,0:T(4,128)S(1)}, f32[4,384]{1,0:T(4,128)S(1)}, u32[]{:S(2)}, u32[]{:S(2)}) %collective-permute-start.3) | collective-permute-done | bytes 6176 | tf_op jit(solution)/shard_map/ppermute | solution.py:428
  15.2 1.1 %shard_map.71 = (f32[4,384]{1,0:T(4,128)S(1)}, f32[16,384]{1,0:T(8,128)S(1)}, f32[4,384]{1,0:T(4,128)S(1)}, f32[4,384]{1,0:T(4,128)S(1)}) custom-call(s32[4,4]{1,0:T(4,128)S(4)} %get-tuple-element.31.place, s32[4,4]{1,0:T(4,128)S(4)} %get-tuple-element.32.live, f32[4,3,288,288]{3,2,1,0:T(8,128)S(1)} %get-tuple-element.33.tiles, ...), custom_call_target="tpu_custom_call" | custom-call | flops 7962624 | bytes 15925248 | tf_op jit(solution)/shard_map/pallas_call | solution.py:467
  16.4 0.1 collective-permute-start.4
  16.5 0.3 %shard_map.72 = (f32[4,384]{1,0:T(4,128)S(1)}, f32[1,128]{1,0:T(1,128)S(1)}) custom-call(f32[4,288]{1,0:T(4,128)S(1)} %get-tuple-element.29.right, f32[4,288,288]{2,1,0:T(8,128)S(1)} %get-tuple-element.47.diagonal_tiles, f32[4,384]{1,0:T(4,128)S(1)} %get-tuple-element.45.image, f32[16,384]{1,0:T(8,128)S(1)} %get-tuple-element.46.swap, ...), custom_call_target="tpu_custom_call" | custom-call | flops 663552 | bytes 1327104 | tf_op jit(solution)/shard_map/pallas_call | solution.py:472
  16.8 0.8 %collective-permute-done.4.swapped = f32[16,384]{1,0:T(8,128)S(1)} collective-permute-done((f32[16,384]{1,0:T(8,128)S(1)}, f32[16,384]{1,0:T(8,128)S(1)}, u32[]{:S(2)}, u32[]{:S(2)}) %collective-permute-start.4) | collective-permute-done | bytes 24608 | tf_op jit(solution)/shard_map/ppermute | solution.py:420
  17.6 0.2 shard_map.73
  17.8 12.6 %all_to_all.5.gathered = f32[16,5,4,128]{3,2,1,0:T(4,128)S(1)} all-to-all(f32[16,5,4,128]{3,2,1,0:T(4,128)S(1)} %shard_map.73), channel_id=1, replica_groups={{0,2,4,6,8,10,12,14,16,18,20,22,24,26,28,30},{1,3,5,7,9,11,13,15,17,19,..., dimensions={0} | all-to-all | bytes 327680 | tf_op jit(solution)/shard_map/all_to_all | solution.py:479
  30.4 0.0 collective-permute-start.5
  30.4 0.3 shard_map.75.sums
  30.7 0.5 %collective-permute-start.6 = (f32[8,384]{1,0:T(8,128)S(1)}, f32[8,384]{1,0:T(8,128)S(1)}, u32[]{:S(2)}, u32[]{:S(2)}) collective-permute-start(f32[8,384]{1,0:T(8,128)S(1)} %shard_map.75.sums), channel_id=1, source_target_pairs={{0,1},{1,0},{2,3},{3,2},{4,5},{5,4},{6,7},{7,6},{8,9},{9,8},{10,11... | collective-permute-start | bytes 36872 | tf_op jit(solution)/shard_map/ppermute | solution.py:420
  31.2 0.1 shard_map.76
  31.3 0.2 collective-permute-done.5.next_other
  31.6 0.5 %shard_map.77.product = f32[4,384]{1,0:T(4,128)S(1)} custom-call(s32[4,4]{1,0:T(4,128)S(4)} %get-tuple-element.31.place, s32[4,4]{1,0:T(4,128)S(4)} %get-tuple-element.32.live, s32[4]{0:T(128)S(4)} %get-tuple-element.35.spot, f32[4,3,288,288]{3,2,1,0:T(8,128)S(1)} %get-tuple-element.33.tiles, f32[4,384]{1,0:T(4,128)S(1)} %get-tuple-element.52.known, ...), custom_call_target="tpu_custom_call" | custom-call | flops 265420800 | bytes 530841600 | tf_op jit(solution)/shard_map/pallas_call | solution.py:488
  32.1 0.0 collective-permute-done.6.sums_other
  32.1 0.6 %shard_map.78 = (f32[4,288]{1,0:T(4,128)}, f32[4,288]{1,0:T(4,128)}) custom-call(f32[4,288]{1,0:T(4,128)S(1)} %get-tuple-element.29.right, f32[4,384]{1,0:T(4,128)S(1)} %get-tuple-element.30.z.z_ref, f32[4,384]{1,0:T(4,128)S(1)} %get-tuple-element.45.image, f32[4,384]{1,0:T(4,128)S(1)} %shard_map.77.product, f32[4,384]{1,0:T(4,128)S(1)} %get-tuple-element.55.scaled, ...), custom_call_target="tpu_custom_call" | custom-call | tf_op jit(solution)/shard_map/pallas_call | solution.py:492
  (2 shorter events, 0.0 us)
Async XLA Ops:
  3.5 9.8 %collective-permute-start = (f32[4,384]{1,0:T(4,128)S(1)}, f32[4,384]{1,0:T(4,128)S(1)}, u32[]{:S(2)}, u32[]{:S(2)}) collective-permute-start(f32[4,384]{1,0:T(4,128)S(1)} %get-tuple-element.38), channel_id=1, source_target_pairs={{0,1},{1,2},{2,3},{3,4},{4,5},{5,6},{6,7},{7,8},{8,9},{9,10},{10,1... | collective-permute-start | bytes 18440 | tf_op jit(solution)/shard_map/ppermute | solution.py:454
  4.3 9.0 %collective-permute-start.1 = (f32[4,384]{1,0:T(4,128)S(1)}, f32[4,384]{1,0:T(4,128)S(1)}, u32[]{:S(2)}, u32[]{:S(2)}) collective-permute-start(f32[4,384]{1,0:T(4,128)S(1)} %get-tuple-element.39), channel_id=1, source_target_pairs={{0,30},{1,31},{2,4},{3,5},{4,2},{5,3},{6,8},{7,9},{8,6},{9,7},{10,... | collective-permute-start | bytes 18440 | tf_op jit(solution)/shard_map/ppermute | solution.py:428
  10.5 2.8 %collective-permute-start.2 = (f32[4,384]{1,0:T(4,128)S(1)}, f32[4,384]{1,0:T(4,128)S(1)}, u32[]{:S(2)}, u32[]{:S(2)}) collective-permute-start(f32[4,384]{1,0:T(4,128)S(1)} %get-tuple-element.40), channel_id=1, source_target_pairs={{1,0},{2,1},{3,2},{4,3},{5,4},{6,5},{7,6},{8,7},{9,8},{10,9},{11,1... | collective-permute-start | bytes 18440 | tf_op jit(solution)/shard_map/ppermute | solution.py:456
  11.6 3.6 %collective-permute-start.3 = (f32[4,384]{1,0:T(4,128)S(1)}, f32[4,384]{1,0:T(4,128)S(1)}, u32[]{:S(2)}, u32[]{:S(2)}) collective-permute-start(f32[4,384]{1,0:T(4,128)S(1)} %get-tuple-element.41), channel_id=1, source_target_pairs={{0,2},{1,3},{2,0},{3,1},{4,6},{5,7},{6,4},{7,5},{8,10},{9,11},{10,... | collective-permute-start | bytes 18440 | tf_op jit(solution)/shard_map/ppermute | solution.py:428
  16.4 1.3 %collective-permute-start.4 = (f32[16,384]{1,0:T(8,128)S(1)}, f32[16,384]{1,0:T(8,128)S(1)}, u32[]{:S(2)}, u32[]{:S(2)}) collective-permute-start(f32[16,384]{1,0:T(8,128)S(1)} %get-tuple-element.46.swap), channel_id=1, source_target_pairs={{0,1},{1,0},{2,3},{3,2},{4,5},{5,4},{6,7},{7,6},{8,9},{9,8},{10,11... | collective-permute-start | bytes 73736 | tf_op jit(solution)/shard_map/ppermute | solution.py:420
  30.4 1.2 %collective-permute-start.5 = (f32[5,4,128]{2,1,0:T(4,128)S(1)}, f32[5,4,128]{2,1,0:T(4,128)S(1)}, u32[]{:S(2)}, u32[]{:S(2)}) collective-permute-start(f32[5,4,128]{2,1,0:T(4,128)S(1)} %shard_map.74.next_part), channel_id=1, source_target_pairs={{0,1},{1,0},{2,3},{3,2},{4,5},{5,4},{6,7},{7,6},{8,9},{9,8},{10,11... | collective-permute-start | bytes 30728 | tf_op jit(solution)/shard_map/ppermute | solution.py:420
  30.7 1.4 %collective-permute-start.6 = (f32[8,384]{1,0:T(8,128)S(1)}, f32[8,384]{1,0:T(8,128)S(1)}, u32[]{:S(2)}, u32[]{:S(2)}) collective-permute-start(f32[8,384]{1,0:T(8,128)S(1)} %shard_map.75.sums), channel_id=1, source_target_pairs={{0,1},{1,0},{2,3},{3,2},{4,5},{5,4},{6,7},{7,6},{8,9},{9,8},{10,11... | collective-permute-start | bytes 36872 | tf_op jit(solution)/shard_map/ppermute | solution.py:420

commit v6 on v5

--- a/solution.py
+++ b/solution.py
@@ -287,16 +287,30 @@
             out[e, i] = part
 
 
+def gather_order(chips):
+    low, high = chips // 4, chips - chips // 4
+    return [*range(high - 1, low - 1, -1), *range(chips - 1, high - 1, -1), *range(low - 1, -1, -1)]
+
+
+def gather_place(chip, chips):
+    low, high = chips // 4, chips - chips // 4
+    last = high - low + chips - 1 - chip
+    middle = jnp.where(chip >= low, high - 1 - chip, chips - 1 - chip)
+    return jnp.where(chip >= high, last, middle)
+
+
 def after_kernel(spot, gathered, out):
     chips = gathered.shape[0]
     chip, _, _ = where_am_i(spot)
-    out[...] = gathered[jnp.where(chip == chips - 1, 0, chip + 1)]
+    out[...] = gathered[gather_place(jnp.where(chip == chips - 1, 0, chip + 1), chips)]
 
 
 def sums_kernel(blocks, width, gathered, out):
     chips = gathered.shape[0]
     tail = width - 256
-    table = jnp.concatenate([gathered[e, 4, 0:1, :] for e in range(chips)], axis=0)
+    order = gather_order(chips)
+    places = [order.index(c) for c in range(chips)]
+    table = jnp.concatenate([gathered[e, 4, 0:1, :] for e in places], axis=0)
     later = jnp.concatenate([table[1:], table[:1]], axis=0)
 
     def at(i, rows=table):
@@ -318,8 +332,9 @@
     lines = []
     for e in range(chips):
         n = (e + 1) % chips
-        ends = jnp.where(inside, pltpu.roll(gathered[e, 4], 128 - tail, 1) * gathered[n, 4], 0.0)
-        pair = gathered[e, 2] * gathered[n, 0] + gathered[e, 3] * gathered[n, 1] + ends
+        here, there = gathered[places[e]], gathered[places[n]]
+        ends = jnp.where(inside, pltpu.roll(here[4], 128 - tail, 1) * there[4], 0.0)
+        pair = here[2] * there[0] + here[3] * there[1] + ends
         lines.append(jnp.sum(pair, axis=0, keepdims=True))
     edges = total(jnp.concatenate(lines, axis=0) * weight)
     values = [fresh, diagonal + 2.0 * edges, norm, along, alpha, 1.0 / norm, along / norm]
@@ -332,7 +347,7 @@
     chips = gathered.shape[0]
     chip, second, _ = where_am_i(spot)
     tail = width - 256
-    before = gathered[jnp.where(chip == 0, chips - 1, chip - 1)]
+    before = gathered[gather_place(jnp.where(chip == 0, chips - 1, chip - 1), chips)]
     ahead = next_part[...]
     alpha = sums[4:5, :]
 
@@ -475,7 +490,7 @@
     sent = call(
         gather_kernel, (blocks, width), [smem] + [vmem] * 4, pltpu.VMEM((chips, 5, blocks, 128), F32)
     )(spot, swap, swapped, far, dots)
-    groups = [[2 * c + core for c in range(chips)] for core in range(2)]
+    groups = [[2 * c + core for c in gather_order(chips)] for core in range(2)]
     gathered = lax.all_to_all(sent, AXIS, 0, 0, axis_index_groups=groups)
     next_part = call(after_kernel, (), [smem, vmem], pltpu.VMEM((5, blocks, 128), F32))(spot, gathered)
     next_other = swap_cores(next_part)

time: 33.1 us -> 30.3 us (0.915); the launches traced: 32.7 us -> 30.3 us
  blocking collectives: 12.6 us -> 10.2 us
  Pallas kernels: 7.74 us -> 8.15 us
    all_to_all x1, blocking collectives: 12.6 us -> 10.2 us  [on_device(): gathered = lax.all_to_all(sent, AXIS, 0, 0, axis_index_groups=groups)]
    ppermute x2, starting transfers between devices: 6.19 us -> 6.97 us  [swap_chips(): return lax.ppermute(value, AXIS, pairs)]
    ppermute x1, starting transfers between devices: 0.77 us -> 0.06 us  [on_device(): lax.ppermute(one_out, AXIS, [(i, (i + 1) % count) for i in range(count)])]
    pallas_call x1, Pallas kernels: 2.91 us -> 3.3 us  [on_device(): call(begin_kernel, sizes + (count,), [hbm] * 5, [pltpu.VMEM(jacobi_invers...]
  transfers between devices with their start and end apart: 7 -> 7, of which waited for: 3 -> 3; matrix products, arithmetic and copies ran while one was open for 0% -> 0% of each run, Pallas kernels for 9% -> 10%
where the time goes in v6:
time: 30.3 us
  blocking collectives  10.2 us (34%)
  starting transfers between devices  8.44 us (28%)
  Pallas kernels  8.15 us (27%)
  waiting for transfers between devices  2.76 us (9%)
  between operations  0.72 us (2%)
    all_to_all x1, blocking collectives, on_device(): gathered = lax.all_to_all(sent, AXIS, 0, 0, axis_index_groups=groups)  10.2 us
    ppermute x2, starting transfers between devices, swap_chips(): return lax.ppermute(value, AXIS, pairs)  6.97 us
    pallas_call x1, Pallas kernels, on_device(): call(begin_kernel, sizes + (count,), [hbm] * 5, [pltpu.VMEM(jacobi_invers...  3.3 us
    pallas_call x1, Pallas kernels, on_device(): call(first_diagonal_kernel, (blocks, width), [hbm, vmem, vmem], [pltpu.VM...  1.69 us
    ppermute x2, waiting for transfers between devices, swap_chips(): return lax.ppermute(value, AXIS, pairs)  1.66 us
    pallas_call x1, Pallas kernels, on_device(): call(middle_kernel, sizes, [smem] * 2 + [vmem] * 7, [half, more, half, ha...  1.15 us
    ppermute x3, waiting for transfers between devices, swap_cores(): return lax.ppermute(value, AXIS, [(i, i ^ 1) for i in range(count)])  1.1 us
    ppermute x1, starting transfers between devices, on_device(): lax.ppermute(back_out, AXIS, [((i + 1) % count, i) for i in range(count)])  0.82 us
  transfers between devices with their start and end apart: 7, of which 3 were waited for; matrix products, arithmetic and copies ran while one was open for 0% of the time, Pallas kernels for 10%

profile of v6, /device:TPU:0, one launch (start us, length us, event | category | flops | bytes accessed | tf_op | source)
XLA Modules:
  0.0 30.3 jit_solution(15012176575137485787)
XLA Ops:
  0.6 3.3 %shard_map.68 = (f32[4,288,288]{2,1,0:T(8,128)S(1)}, f32[4,3,288,288]{3,2,1,0:T(8,128)S(1)}, f32[4,288]{1,0:T(4,128)S(1)}, s32[4,4]{1,0:T(4,128)S(4)}, s32[4,4]{...) custom-call(s32[4,4]{1,0:T(4,128)} %cols_hbm.1, ...), custom_call_target="tpu_custom_call" | custom-call | flops 2654208 | bytes 5308416 | tf_op jit(solution)/shard_map/pallas_call | solution.py:450
  3.9 0.1 collective-permute-start
  4.0 6.7 %collective-permute-start.1 = (f32[4,384]{1,0:T(4,128)S(1)}, f32[4,384]{1,0:T(4,128)S(1)}, u32[]{:S(2)}, u32[]{:S(2)}) collective-permute-start(f32[4,384]{1,0:T(4,128)S(1)} %get-tuple-element.39), channel_id=1, source_target_pairs={{0,30},{1,31},{2,4},{3,5},{4,2},{5,3},{6,8},{7,9},{8,6},{9,7},{10,... | collective-permute-start | bytes 18440 | tf_op jit(solution)/shard_map/ppermute | solution.py:443
  10.7 0.8 %collective-permute-start.2 = (f32[4,384]{1,0:T(4,128)S(1)}, f32[4,384]{1,0:T(4,128)S(1)}, u32[]{:S(2)}, u32[]{:S(2)}) collective-permute-start(f32[4,384]{1,0:T(4,128)S(1)} %get-tuple-element.40), channel_id=1, source_target_pairs={{1,0},{2,1},{3,2},{4,3},{5,4},{6,5},{7,6},{8,7},{9,8},{10,9},{11,1... | collective-permute-start | bytes 18440 | tf_op jit(solution)/shard_map/ppermute | solution.py:471
  11.6 0.2 collective-permute-start.3
  11.8 1.7 %shard_map.69 = (f32[4,288,288]{2,1,0:T(8,128)S(1)}, f32[4,384]{1,0:T(4,128)S(1)}) custom-call(f32[4,4,288,288]{3,2,1,0:T(8,128)} %tiles_hbm.3, f32[4,384]{1,0:T(4,128)S(1)} %get-tuple-element.30.z.z_ref, f32[4,8,384]{2,1,0:T(8,128)S(1)} %get-tuple-element.36.near), custom_call_target="tpu_custom_call" | custom-call | flops 663552 | bytes 1327104 | tf_op jit(solution)/shard_map/pallas_call | solution.py:473
  13.5 0.0 collective-permute-done.forward_in
  13.5 0.0 collective-permute-done.1.odd_in
  13.5 0.0 collective-permute-done.2.back_in
  13.5 1.7 %collective-permute-done.3.even_in = f32[4,384]{1,0:T(4,128)S(1)} collective-permute-done((f32[4,384]{1,0:T(4,128)S(1)}, f32[4,384]{1,0:T(4,128)S(1)}, u32[]{:S(2)}, u32[]{:S(2)}) %collective-permute-start.3) | collective-permute-done | bytes 6176 | tf_op jit(solution)/shard_map/ppermute | solution.py:443
  15.2 1.1 %shard_map.71 = (f32[4,384]{1,0:T(4,128)S(1)}, f32[16,384]{1,0:T(8,128)S(1)}, f32[4,384]{1,0:T(4,128)S(1)}, f32[4,384]{1,0:T(4,128)S(1)}) custom-call(s32[4,4]{1,0:T(4,128)S(4)} %get-tuple-element.31.place, s32[4,4]{1,0:T(4,128)S(4)} %get-tuple-element.32.live, f32[4,3,288,288]{3,2,1,0:T(8,128)S(1)} %get-tuple-element.33.tiles, ...), custom_call_target="tpu_custom_call" | custom-call | flops 7962624 | bytes 15925248 | tf_op jit(solution)/shard_map/pallas_call | solution.py:482
  16.4 0.1 collective-permute-start.4
  16.4 0.3 %shard_map.72 = (f32[4,384]{1,0:T(4,128)S(1)}, f32[1,128]{1,0:T(1,128)S(1)}) custom-call(f32[4,288]{1,0:T(4,128)S(1)} %get-tuple-element.29.right, f32[4,288,288]{2,1,0:T(8,128)S(1)} %get-tuple-element.47.diagonal_tiles, f32[4,384]{1,0:T(4,128)S(1)} %get-tuple-element.45.image, f32[16,384]{1,0:T(8,128)S(1)} %get-tuple-element.46.swap, ...), custom_call_target="tpu_custom_call" | custom-call | flops 663552 | bytes 1327104 | tf_op jit(solution)/shard_map/pallas_call | solution.py:487
  16.8 0.8 %collective-permute-done.4.swapped = f32[16,384]{1,0:T(8,128)S(1)} collective-permute-done((f32[16,384]{1,0:T(8,128)S(1)}, f32[16,384]{1,0:T(8,128)S(1)}, u32[]{:S(2)}, u32[]{:S(2)}) %collective-permute-start.4) | collective-permute-done | bytes 24608 | tf_op jit(solution)/shard_map/ppermute | solution.py:435
  17.6 0.2 shard_map.73
  17.8 10.2 %all_to_all.5.gathered = f32[16,5,4,128]{3,2,1,0:T(4,128)S(1)} all-to-all(f32[16,5,4,128]{3,2,1,0:T(4,128)S(1)} %shard_map.73), channel_id=1, replica_groups={{22,20,18,16,14,12,10,8,30,28,26,24,6,4,2,0},{23,21,19,17,15,13,11,9,31..., dimensions={0} | all-to-all | bytes 327680 | tf_op jit(solution)/shard_map/all_to_all | solution.py:494
  28.0 0.0 collective-permute-start.5
  28.0 0.3 %shard_map.75.sums = f32[8,384]{1,0:T(8,128)S(1)} custom-call(f32[16,5,4,128]{3,2,1,0:T(4,128)S(1)} %all_to_all.5.gathered), custom_call_target="tpu_custom_call" | custom-call | flops 2654208 | bytes 5308416 | tf_op jit(solution)/shard_map/pallas_call | solution.py:497
  28.3 0.5 %collective-permute-start.6 = (f32[8,384]{1,0:T(8,128)S(1)}, f32[8,384]{1,0:T(8,128)S(1)}, u32[]{:S(2)}, u32[]{:S(2)}) collective-permute-start(f32[8,384]{1,0:T(8,128)S(1)} %shard_map.75.sums), channel_id=1, source_target_pairs={{0,1},{1,0},{2,3},{3,2},{4,5},{5,4},{6,7},{7,6},{8,9},{9,8},{10,11... | collective-permute-start | bytes 36872 | tf_op jit(solution)/shard_map/ppermute | solution.py:435
  28.8 0.1 shard_map.76
  28.9 0.2 collective-permute-done.5.next_other
  29.1 0.5 %shard_map.77.product = f32[4,384]{1,0:T(4,128)S(1)} custom-call(s32[4,4]{1,0:T(4,128)S(4)} %get-tuple-element.31.place, s32[4,4]{1,0:T(4,128)S(4)} %get-tuple-element.32.live, s32[4]{0:T(128)S(4)} %get-tuple-element.35.spot, f32[4,3,288,288]{3,2,1,0:T(8,128)S(1)} %get-tuple-element.33.tiles, f32[4,384]{1,0:T(4,128)S(1)} %get-tuple-element.52.known, ...), custom_call_target="tpu_custom_call" | custom-call | flops 265420800 | bytes 530841600 | tf_op jit(solution)/shard_map/pallas_call | solution.py:503
  29.6 0.0 collective-permute-done.6.sums_other
  29.6 0.6 %shard_map.78 = (f32[4,288]{1,0:T(4,128)}, f32[4,288]{1,0:T(4,128)}) custom-call(f32[4,288]{1,0:T(4,128)S(1)} %get-tuple-element.29.right, f32[4,384]{1,0:T(4,128)S(1)} %get-tuple-element.30.z.z_ref, f32[4,384]{1,0:T(4,128)S(1)} %get-tuple-element.45.image, f32[4,384]{1,0:T(4,128)S(1)} %shard_map.77.product, f32[4,384]{1,0:T(4,128)S(1)} %get-tuple-element.55.scaled, ...), custom_call_target="tpu_custom_call" | custom-call | tf_op jit(solution)/shard_map/pallas_call | solution.py:507
  (2 shorter events, 0.0 us)
Async XLA Ops:
  3.9 9.6 %collective-permute-start = (f32[4,384]{1,0:T(4,128)S(1)}, f32[4,384]{1,0:T(4,128)S(1)}, u32[]{:S(2)}, u32[]{:S(2)}) collective-permute-start(f32[4,384]{1,0:T(4,128)S(1)} %get-tuple-element.38), channel_id=1, source_target_pairs={{0,1},{1,2},{2,3},{3,4},{4,5},{5,6},{6,7},{7,8},{8,9},{9,10},{10,1... | collective-permute-start | bytes 18440 | tf_op jit(solution)/shard_map/ppermute | solution.py:469
  4.0 9.5 %collective-permute-start.1 = (f32[4,384]{1,0:T(4,128)S(1)}, f32[4,384]{1,0:T(4,128)S(1)}, u32[]{:S(2)}, u32[]{:S(2)}) collective-permute-start(f32[4,384]{1,0:T(4,128)S(1)} %get-tuple-element.39), channel_id=1, source_target_pairs={{0,30},{1,31},{2,4},{3,5},{4,2},{5,3},{6,8},{7,9},{8,6},{9,7},{10,... | collective-permute-start | bytes 18440 | tf_op jit(solution)/shard_map/ppermute | solution.py:443
  10.7 2.8 %collective-permute-start.2 = (f32[4,384]{1,0:T(4,128)S(1)}, f32[4,384]{1,0:T(4,128)S(1)}, u32[]{:S(2)}, u32[]{:S(2)}) collective-permute-start(f32[4,384]{1,0:T(4,128)S(1)} %get-tuple-element.40), channel_id=1, source_target_pairs={{1,0},{2,1},{3,2},{4,3},{5,4},{6,5},{7,6},{8,7},{9,8},{10,9},{11,1... | collective-permute-start | bytes 18440 | tf_op jit(solution)/shard_map/ppermute | solution.py:471
  11.6 3.6 %collective-permute-start.3 = (f32[4,384]{1,0:T(4,128)S(1)}, f32[4,384]{1,0:T(4,128)S(1)}, u32[]{:S(2)}, u32[]{:S(2)}) collective-permute-start(f32[4,384]{1,0:T(4,128)S(1)} %get-tuple-element.41), channel_id=1, source_target_pairs={{0,2},{1,3},{2,0},{3,1},{4,6},{5,7},{6,4},{7,5},{8,10},{9,11},{10,... | collective-permute-start | bytes 18440 | tf_op jit(solution)/shard_map/ppermute | solution.py:443
  16.4 1.3 %collective-permute-start.4 = (f32[16,384]{1,0:T(8,128)S(1)}, f32[16,384]{1,0:T(8,128)S(1)}, u32[]{:S(2)}, u32[]{:S(2)}) collective-permute-start(f32[16,384]{1,0:T(8,128)S(1)} %get-tuple-element.46.swap), channel_id=1, source_target_pairs={{0,1},{1,0},{2,3},{3,2},{4,5},{5,4},{6,7},{7,6},{8,9},{9,8},{10,11... | collective-permute-start | bytes 73736 | tf_op jit(solution)/shard_map/ppermute | solution.py:435
  28.0 1.2 %collective-permute-start.5 = (f32[5,4,128]{2,1,0:T(4,128)S(1)}, f32[5,4,128]{2,1,0:T(4,128)S(1)}, u32[]{:S(2)}, u32[]{:S(2)}) collective-permute-start(f32[5,4,128]{2,1,0:T(4,128)S(1)} %shard_map.74.next_part), channel_id=1, source_target_pairs={{0,1},{1,0},{2,3},{3,2},{4,5},{5,4},{6,7},{7,6},{8,9},{9,8},{10,11... | collective-permute-start | bytes 30728 | tf_op jit(solution)/shard_map/ppermute | solution.py:435
  28.3 1.4 %collective-permute-start.6 = (f32[8,384]{1,0:T(8,128)S(1)}, f32[8,384]{1,0:T(8,128)S(1)}, u32[]{:S(2)}, u32[]{:S(2)}) collective-permute-start(f32[8,384]{1,0:T(8,128)S(1)} %shard_map.75.sums), channel_id=1, source_target_pairs={{0,1},{1,0},{2,3},{3,2},{4,5},{5,4},{6,7},{7,6},{8,9},{9,8},{10,11... | collective-permute-start | bytes 36872 | tf_op jit(solution)/shard_map/ppermute | solution.py:435

commit v7 on v6

--- a/solution.py
+++ b/solution.py
@@ -109,7 +109,7 @@
     def _(g):
         @pl.loop(1, counts[g])
         def _(k):
-            tile_copy(g, k).start()
+            tile_copy(g, k).start(priority=1)
 
     @pl.loop(0, blocks)
     def _(g):

time: 30.3 us -> 29.9 us (0.987)
  Pallas kernels: 8.15 us -> 7.49 us
  starting transfers between devices: 8.44 us -> 8.84 us
  waiting for transfers between devices: 2.76 us -> 2.43 us
    ppermute x1, starting transfers between devices: 0.06 us -> 0.86 us  [on_device(): lax.ppermute(one_out, AXIS, [(i, (i + 1) % count) for i in range(count)])]
    pallas_call x1, Pallas kernels: 3.3 us -> 2.66 us  [on_device(): call(begin_kernel, sizes + (count,), [hbm] * 5, [pltpu.VMEM(jacobi_invers...]
    ppermute x1, starting transfers between devices: 0.82 us -> 0.21 us  [on_device(): lax.ppermute(back_out, AXIS, [((i + 1) % count, i) for i in range(count)])]
    ppermute x2, waiting for transfers between devices: 1.66 us -> 1.32 us  [swap_chips(): return lax.ppermute(value, AXIS, pairs)]
where the time goes in v7:
time: 29.9 us; the launch traced here: 29.7 us
  blocking collectives  10.2 us (34%)
  starting transfers between devices  8.84 us (30%)
  Pallas kernels  7.49 us (25%)
  waiting for transfers between devices  2.43 us (8%)
  between operations  0.71 us (2%)
    all_to_all x1, blocking collectives, on_device(): gathered = lax.all_to_all(sent, AXIS, 0, 0, axis_index_groups=groups)  10.2 us
    ppermute x2, starting transfers between devices, swap_chips(): return lax.ppermute(value, AXIS, pairs)  7.18 us
    pallas_call x1, Pallas kernels, on_device(): call(begin_kernel, sizes + (count,), [hbm] * 5, [pltpu.VMEM(jacobi_invers...  2.66 us
    pallas_call x1, Pallas kernels, on_device(): call(first_diagonal_kernel, (blocks, width), [hbm, vmem, vmem], [pltpu.VM...  1.69 us
    ppermute x2, waiting for transfers between devices, swap_chips(): return lax.ppermute(value, AXIS, pairs)  1.32 us
    pallas_call x1, Pallas kernels, on_device(): call(middle_kernel, sizes, [smem] * 2 + [vmem] * 7, [half, more, half, ha...  1.13 us
    ppermute x3, waiting for transfers between devices, swap_cores(): return lax.ppermute(value, AXIS, [(i, i ^ 1) for i in range(count)])  1.1 us
    ppermute x1, starting transfers between devices, on_device(): lax.ppermute(one_out, AXIS, [(i, (i + 1) % count) for i in range(count)])  0.86 us
  transfers between devices with their start and end apart: 7, of which 3 were waited for; matrix products, arithmetic and copies ran while one was open for 0% of the time, Pallas kernels for 10%

profile of v7, /device:TPU:0, one launch (start us, length us, event | category | flops | bytes accessed | tf_op | source)
XLA Modules:
  0.0 29.7 jit_solution(16233304677530918660)
XLA Ops:
  0.6 2.7 %shard_map.68 = (f32[4,288,288]{2,1,0:T(8,128)S(1)}, f32[4,3,288,288]{3,2,1,0:T(8,128)S(1)}, f32[4,288]{1,0:T(4,128)S(1)}, s32[4,4]{1,0:T(4,128)S(4)}, s32[4,4]{...) custom-call(s32[4,4]{1,0:T(4,128)} %cols_hbm.1, ...), custom_call_target="tpu_custom_call" | custom-call | flops 2654208 | bytes 5308416 | tf_op jit(solution)/shard_map/pallas_call | solution.py:450
  3.3 0.9 %collective-permute-start = (f32[4,384]{1,0:T(4,128)S(1)}, f32[4,384]{1,0:T(4,128)S(1)}, u32[]{:S(2)}, u32[]{:S(2)}) collective-permute-start(f32[4,384]{1,0:T(4,128)S(1)} %get-tuple-element.38), channel_id=1, source_target_pairs={{0,1},{1,2},{2,3},{3,4},{4,5},{5,6},{6,7},{7,8},{8,9},{9,10},{10,1... | collective-permute-start | bytes 18440 | tf_op jit(solution)/shard_map/ppermute | solution.py:469
  4.2 6.6 %collective-permute-start.1 = (f32[4,384]{1,0:T(4,128)S(1)}, f32[4,384]{1,0:T(4,128)S(1)}, u32[]{:S(2)}, u32[]{:S(2)}) collective-permute-start(f32[4,384]{1,0:T(4,128)S(1)} %get-tuple-element.39), channel_id=1, source_target_pairs={{0,30},{1,31},{2,4},{3,5},{4,2},{5,3},{6,8},{7,9},{8,6},{9,7},{10,... | collective-permute-start | bytes 18440 | tf_op jit(solution)/shard_map/ppermute | solution.py:443
  10.8 0.2 collective-permute-start.2
  11.0 0.6 %collective-permute-start.3 = (f32[4,384]{1,0:T(4,128)S(1)}, f32[4,384]{1,0:T(4,128)S(1)}, u32[]{:S(2)}, u32[]{:S(2)}) collective-permute-start(f32[4,384]{1,0:T(4,128)S(1)} %get-tuple-element.41), channel_id=1, source_target_pairs={{0,2},{1,3},{2,0},{3,1},{4,6},{5,7},{6,4},{7,5},{8,10},{9,11},{10,... | collective-permute-start | bytes 18440 | tf_op jit(solution)/shard_map/ppermute | solution.py:443
  11.6 1.7 %shard_map.69 = (f32[4,288,288]{2,1,0:T(8,128)S(1)}, f32[4,384]{1,0:T(4,128)S(1)}) custom-call(f32[4,4,288,288]{3,2,1,0:T(8,128)} %tiles_hbm.3, f32[4,384]{1,0:T(4,128)S(1)} %get-tuple-element.30.z.z_ref, f32[4,8,384]{2,1,0:T(8,128)S(1)} %get-tuple-element.36.near), custom_call_target="tpu_custom_call" | custom-call | flops 663552 | bytes 1327104 | tf_op jit(solution)/shard_map/pallas_call | solution.py:473
  13.3 0.0 collective-permute-done.forward_in
  13.3 0.0 collective-permute-done.1.odd_in
  13.3 0.0 collective-permute-done.2.back_in
  13.3 1.3 %collective-permute-done.3.even_in = f32[4,384]{1,0:T(4,128)S(1)} collective-permute-done((f32[4,384]{1,0:T(4,128)S(1)}, f32[4,384]{1,0:T(4,128)S(1)}, u32[]{:S(2)}, u32[]{:S(2)}) %collective-permute-start.3) | collective-permute-done | bytes 6176 | tf_op jit(solution)/shard_map/ppermute | solution.py:443
  14.6 1.1 %shard_map.71 = (f32[4,384]{1,0:T(4,128)S(1)}, f32[16,384]{1,0:T(8,128)S(1)}, f32[4,384]{1,0:T(4,128)S(1)}, f32[4,384]{1,0:T(4,128)S(1)}) custom-call(s32[4,4]{1,0:T(4,128)S(4)} %get-tuple-element.31.place, s32[4,4]{1,0:T(4,128)S(4)} %get-tuple-element.32.live, f32[4,3,288,288]{3,2,1,0:T(8,128)S(1)} %get-tuple-element.33.tiles, ...), custom_call_target="tpu_custom_call" | custom-call | flops 7962624 | bytes 15925248 | tf_op jit(solution)/shard_map/pallas_call | solution.py:482
  15.8 0.1 collective-permute-start.4
  15.8 0.3 %shard_map.72 = (f32[4,384]{1,0:T(4,128)S(1)}, f32[1,128]{1,0:T(1,128)S(1)}) custom-call(f32[4,288]{1,0:T(4,128)S(1)} %get-tuple-element.29.right, f32[4,288,288]{2,1,0:T(8,128)S(1)} %get-tuple-element.47.diagonal_tiles, f32[4,384]{1,0:T(4,128)S(1)} %get-tuple-element.45.image, f32[16,384]{1,0:T(8,128)S(1)} %get-tuple-element.46.swap, ...), custom_call_target="tpu_custom_call" | custom-call | flops 663552 | bytes 1327104 | tf_op jit(solution)/shard_map/pallas_call | solution.py:487
  16.2 0.8 %collective-permute-done.4.swapped = f32[16,384]{1,0:T(8,128)S(1)} collective-permute-done((f32[16,384]{1,0:T(8,128)S(1)}, f32[16,384]{1,0:T(8,128)S(1)}, u32[]{:S(2)}, u32[]{:S(2)}) %collective-permute-start.4) | collective-permute-done | bytes 24608 | tf_op jit(solution)/shard_map/ppermute | solution.py:435
  17.0 0.2 shard_map.73
  17.2 10.2 %all_to_all.5.gathered = f32[16,5,4,128]{3,2,1,0:T(4,128)S(1)} all-to-all(f32[16,5,4,128]{3,2,1,0:T(4,128)S(1)} %shard_map.73), channel_id=1, replica_groups={{22,20,18,16,14,12,10,8,30,28,26,24,6,4,2,0},{23,21,19,17,15,13,11,9,31..., dimensions={0} | all-to-all | bytes 327680 | tf_op jit(solution)/shard_map/all_to_all | solution.py:494
  27.4 0.0 collective-permute-start.5
  27.4 0.3 %shard_map.75.sums = f32[8,384]{1,0:T(8,128)S(1)} custom-call(f32[16,5,4,128]{3,2,1,0:T(4,128)S(1)} %all_to_all.5.gathered), custom_call_target="tpu_custom_call" | custom-call | flops 2654208 | bytes 5308416 | tf_op jit(solution)/shard_map/pallas_call | solution.py:497
  27.7 0.5 %collective-permute-start.6 = (f32[8,384]{1,0:T(8,128)S(1)}, f32[8,384]{1,0:T(8,128)S(1)}, u32[]{:S(2)}, u32[]{:S(2)}) collective-permute-start(f32[8,384]{1,0:T(8,128)S(1)} %shard_map.75.sums), channel_id=1, source_target_pairs={{0,1},{1,0},{2,3},{3,2},{4,5},{5,4},{6,7},{7,6},{8,9},{9,8},{10,11... | collective-permute-start | bytes 36872 | tf_op jit(solution)/shard_map/ppermute | solution.py:435
  28.2 0.1 shard_map.76
  28.3 0.2 collective-permute-done.5.next_other
  28.5 0.5 %shard_map.77.product = f32[4,384]{1,0:T(4,128)S(1)} custom-call(s32[4,4]{1,0:T(4,128)S(4)} %get-tuple-element.31.place, s32[4,4]{1,0:T(4,128)S(4)} %get-tuple-element.32.live, s32[4]{0:T(128)S(4)} %get-tuple-element.35.spot, f32[4,3,288,288]{3,2,1,0:T(8,128)S(1)} %get-tuple-element.33.tiles, f32[4,384]{1,0:T(4,128)S(1)} %get-tuple-element.52.known, ...), custom_call_target="tpu_custom_call" | custom-call | flops 265420800 | bytes 530841600 | tf_op jit(solution)/shard_map/pallas_call | solution.py:503
  29.0 0.0 collective-permute-done.6.sums_other
  29.0 0.6 %shard_map.78 = (f32[4,288]{1,0:T(4,128)}, f32[4,288]{1,0:T(4,128)}) custom-call(f32[4,288]{1,0:T(4,128)S(1)} %get-tuple-element.29.right, f32[4,384]{1,0:T(4,128)S(1)} %get-tuple-element.30.z.z_ref, f32[4,384]{1,0:T(4,128)S(1)} %get-tuple-element.45.image, f32[4,384]{1,0:T(4,128)S(1)} %shard_map.77.product, f32[4,384]{1,0:T(4,128)S(1)} %get-tuple-element.55.scaled, ...), custom_call_target="tpu_custom_call" | custom-call | tf_op jit(solution)/shard_map/pallas_call | solution.py:507
  (2 shorter events, 0.0 us)
Async XLA Ops:
  3.3 10.0 %collective-permute-start = (f32[4,384]{1,0:T(4,128)S(1)}, f32[4,384]{1,0:T(4,128)S(1)}, u32[]{:S(2)}, u32[]{:S(2)}) collective-permute-start(f32[4,384]{1,0:T(4,128)S(1)} %get-tuple-element.38), channel_id=1, source_target_pairs={{0,1},{1,2},{2,3},{3,4},{4,5},{5,6},{6,7},{7,8},{8,9},{9,10},{10,1... | collective-permute-start | bytes 18440 | tf_op jit(solution)/shard_map/ppermute | solution.py:469
  4.2 9.1 %collective-permute-start.1 = (f32[4,384]{1,0:T(4,128)S(1)}, f32[4,384]{1,0:T(4,128)S(1)}, u32[]{:S(2)}, u32[]{:S(2)}) collective-permute-start(f32[4,384]{1,0:T(4,128)S(1)} %get-tuple-element.39), channel_id=1, source_target_pairs={{0,30},{1,31},{2,4},{3,5},{4,2},{5,3},{6,8},{7,9},{8,6},{9,7},{10,... | collective-permute-start | bytes 18440 | tf_op jit(solution)/shard_map/ppermute | solution.py:443
  10.8 2.5 %collective-permute-start.2 = (f32[4,384]{1,0:T(4,128)S(1)}, f32[4,384]{1,0:T(4,128)S(1)}, u32[]{:S(2)}, u32[]{:S(2)}) collective-permute-start(f32[4,384]{1,0:T(4,128)S(1)} %get-tuple-element.40), channel_id=1, source_target_pairs={{1,0},{2,1},{3,2},{4,3},{5,4},{6,5},{7,6},{8,7},{9,8},{10,9},{11,1... | collective-permute-start | bytes 18440 | tf_op jit(solution)/shard_map/ppermute | solution.py:471
  11.0 3.6 %collective-permute-start.3 = (f32[4,384]{1,0:T(4,128)S(1)}, f32[4,384]{1,0:T(4,128)S(1)}, u32[]{:S(2)}, u32[]{:S(2)}) collective-permute-start(f32[4,384]{1,0:T(4,128)S(1)} %get-tuple-element.41), channel_id=1, source_target_pairs={{0,2},{1,3},{2,0},{3,1},{4,6},{5,7},{6,4},{7,5},{8,10},{9,11},{10,... | collective-permute-start | bytes 18440 | tf_op jit(solution)/shard_map/ppermute | solution.py:443
  15.8 1.3 %collective-permute-start.4 = (f32[16,384]{1,0:T(8,128)S(1)}, f32[16,384]{1,0:T(8,128)S(1)}, u32[]{:S(2)}, u32[]{:S(2)}) collective-permute-start(f32[16,384]{1,0:T(8,128)S(1)} %get-tuple-element.46.swap), channel_id=1, source_target_pairs={{0,1},{1,0},{2,3},{3,2},{4,5},{5,4},{6,7},{7,6},{8,9},{9,8},{10,11... | collective-permute-start | bytes 73736 | tf_op jit(solution)/shard_map/ppermute | solution.py:435
  27.4 1.2 %collective-permute-start.5 = (f32[5,4,128]{2,1,0:T(4,128)S(1)}, f32[5,4,128]{2,1,0:T(4,128)S(1)}, u32[]{:S(2)}, u32[]{:S(2)}) collective-permute-start(f32[5,4,128]{2,1,0:T(4,128)S(1)} %shard_map.74.next_part), channel_id=1, source_target_pairs={{0,1},{1,0},{2,3},{3,2},{4,5},{5,4},{6,7},{7,6},{8,9},{9,8},{10,11... | collective-permute-start | bytes 30728 | tf_op jit(solution)/shard_map/ppermute | solution.py:435
  27.7 1.4 %collective-permute-start.6 = (f32[8,384]{1,0:T(8,128)S(1)}, f32[8,384]{1,0:T(8,128)S(1)}, u32[]{:S(2)}, u32[]{:S(2)}) collective-permute-start(f32[8,384]{1,0:T(8,128)S(1)} %shard_map.75.sums), channel_id=1, source_target_pairs={{0,1},{1,0},{2,3},{3,2},{4,5},{5,4},{6,7},{7,6},{8,9},{9,8},{10,11... | collective-permute-start | bytes 36872 | tf_op jit(solution)/shard_map/ppermute | solution.py:435

commit v8 on v7

--- a/solution.py
+++ b/solution.py
@@ -289,14 +289,21 @@
 
 def gather_order(chips):
     low, high = chips // 4, chips - chips // 4
-    return [*range(high - 1, low - 1, -1), *range(chips - 1, high - 1, -1), *range(low - 1, -1, -1)]
+    half = chips // 2
+    return [
+        *range(high - 1, half - 1, -1),
+        *range(chips - 1, high - 1, -1),
+        *range(low - 1, -1, -1),
+        *range(half - 1, low - 1, -1),
+    ]
 
 
 def gather_place(chip, chips):
     low, high = chips // 4, chips - chips // 4
-    last = high - low + chips - 1 - chip
-    middle = jnp.where(chip >= low, high - 1 - chip, chips - 1 - chip)
-    return jnp.where(chip >= high, last, middle)
+    half = chips // 2
+    upper = jnp.where(chip >= high, high - half + chips - 1 - chip, high - 1 - chip)
+    lower = jnp.where(chip >= low, chips - 1 - chip + low, chips - half + low - 1 - chip)
+    return jnp.where(chip >= half, upper, lower)
 
 
 def after_kernel(spot, gathered, out):

time: 29.9 us -> 30.1 us (level)
    ppermute x1, starting transfers between devices: 0.86 us -> 0.1 us  [on_device(): lax.ppermute(one_out, AXIS, [(i, (i + 1) % count) for i in range(count)])]
    ppermute x1, starting transfers between devices: 0.21 us -> 0.61 us  [on_device(): lax.ppermute(back_out, AXIS, [((i + 1) % count, i) for i in range(count)])]
where the time goes in v8:
time: 30.1 us; the launch traced here: 29.9 us
  blocking collectives  10.1 us (34%)
  starting transfers between devices  8.57 us (28%)
  Pallas kernels  7.76 us (26%)
  waiting for transfers between devices  2.7 us (9%)
  between operations  0.71 us (2%)
    all_to_all x1, blocking collectives, on_device(): gathered = lax.all_to_all(sent, AXIS, 0, 0, axis_index_groups=groups)  10.1 us
    ppermute x2, starting transfers between devices, swap_chips(): return lax.ppermute(value, AXIS, pairs)  7.27 us
    pallas_call x1, Pallas kernels, on_device(): call(begin_kernel, sizes + (count,), [hbm] * 5, [pltpu.VMEM(jacobi_invers...  2.93 us
    pallas_call x1, Pallas kernels, on_device(): call(first_diagonal_kernel, (blocks, width), [hbm, vmem, vmem], [pltpu.VM...  1.69 us
    ppermute x2, waiting for transfers between devices, swap_chips(): return lax.ppermute(value, AXIS, pairs)  1.59 us
    pallas_call x1, Pallas kernels, on_device(): call(middle_kernel, sizes, [smem] * 2 + [vmem] * 7, [half, more, half, ha...  1.14 us
    ppermute x3, waiting for transfers between devices, swap_cores(): return lax.ppermute(value, AXIS, [(i, i ^ 1) for i in range(count)])  1.1 us
    pallas_call x1, Pallas kernels, on_device(): call(end_kernel, (blocks, width), [vmem] * 7, [out, out])  0.62 us
  transfers between devices with their start and end apart: 7, of which 3 were waited for; matrix products, arithmetic and copies ran while one was open for 0% of the time, Pallas kernels for 10%

profile of v8, /device:TPU:0, one launch (start us, length us, event | category | flops | bytes accessed | tf_op | source)
XLA Modules:
  0.0 29.9 jit_solution(16690817747397399498)
XLA Ops:
  0.6 2.9 %shard_map.68 = (f32[4,288,288]{2,1,0:T(8,128)S(1)}, f32[4,3,288,288]{3,2,1,0:T(8,128)S(1)}, f32[4,288]{1,0:T(4,128)S(1)}, s32[4,4]{1,0:T(4,128)S(4)}, s32[4,4]{...) custom-call(s32[4,4]{1,0:T(4,128)} %cols_hbm.1, ...), custom_call_target="tpu_custom_call" | custom-call | flops 2654208 | bytes 5308416 | tf_op jit(solution)/shard_map/pallas_call | solution.py:457
  3.6 0.1 collective-permute-start
  3.7 7.0 %collective-permute-start.1 = (f32[4,384]{1,0:T(4,128)S(1)}, f32[4,384]{1,0:T(4,128)S(1)}, u32[]{:S(2)}, u32[]{:S(2)}) collective-permute-start(f32[4,384]{1,0:T(4,128)S(1)} %get-tuple-element.39), channel_id=1, source_target_pairs={{0,30},{1,31},{2,4},{3,5},{4,2},{5,3},{6,8},{7,9},{8,6},{9,7},{10,... | collective-permute-start | bytes 18440 | tf_op jit(solution)/shard_map/ppermute | solution.py:450
  10.6 0.6 %collective-permute-start.2 = (f32[4,384]{1,0:T(4,128)S(1)}, f32[4,384]{1,0:T(4,128)S(1)}, u32[]{:S(2)}, u32[]{:S(2)}) collective-permute-start(f32[4,384]{1,0:T(4,128)S(1)} %get-tuple-element.40), channel_id=1, source_target_pairs={{1,0},{2,1},{3,2},{4,3},{5,4},{6,5},{7,6},{8,7},{9,8},{10,9},{11,1... | collective-permute-start | bytes 18440 | tf_op jit(solution)/shard_map/ppermute | solution.py:478
  11.2 0.3 %collective-permute-start.3 = (f32[4,384]{1,0:T(4,128)S(1)}, f32[4,384]{1,0:T(4,128)S(1)}, u32[]{:S(2)}, u32[]{:S(2)}) collective-permute-start(f32[4,384]{1,0:T(4,128)S(1)} %get-tuple-element.41), channel_id=1, source_target_pairs={{0,2},{1,3},{2,0},{3,1},{4,6},{5,7},{6,4},{7,5},{8,10},{9,11},{10,... | collective-permute-start | bytes 18440 | tf_op jit(solution)/shard_map/ppermute | solution.py:450
  11.6 1.7 %shard_map.69 = (f32[4,288,288]{2,1,0:T(8,128)S(1)}, f32[4,384]{1,0:T(4,128)S(1)}) custom-call(f32[4,4,288,288]{3,2,1,0:T(8,128)} %tiles_hbm.3, f32[4,384]{1,0:T(4,128)S(1)} %get-tuple-element.30.z.z_ref, f32[4,8,384]{2,1,0:T(8,128)S(1)} %get-tuple-element.36.near), custom_call_target="tpu_custom_call" | custom-call | flops 663552 | bytes 1327104 | tf_op jit(solution)/shard_map/pallas_call | solution.py:480
  13.3 0.0 collective-permute-done.forward_in
  13.3 0.0 collective-permute-done.1.odd_in
  13.3 0.0 collective-permute-done.2.back_in
  13.3 1.6 %collective-permute-done.3.even_in = f32[4,384]{1,0:T(4,128)S(1)} collective-permute-done((f32[4,384]{1,0:T(4,128)S(1)}, f32[4,384]{1,0:T(4,128)S(1)}, u32[]{:S(2)}, u32[]{:S(2)}) %collective-permute-start.3) | collective-permute-done | bytes 6176 | tf_op jit(solution)/shard_map/ppermute | solution.py:450
  14.9 1.1 %shard_map.71 = (f32[4,384]{1,0:T(4,128)S(1)}, f32[16,384]{1,0:T(8,128)S(1)}, f32[4,384]{1,0:T(4,128)S(1)}, f32[4,384]{1,0:T(4,128)S(1)}) custom-call(s32[4,4]{1,0:T(4,128)S(4)} %get-tuple-element.31.place, s32[4,4]{1,0:T(4,128)S(4)} %get-tuple-element.32.live, f32[4,3,288,288]{3,2,1,0:T(8,128)S(1)} %get-tuple-element.33.tiles, ...), custom_call_target="tpu_custom_call" | custom-call | flops 7962624 | bytes 15925248 | tf_op jit(solution)/shard_map/pallas_call | solution.py:489
  16.0 0.1 collective-permute-start.4
  16.1 0.3 %shard_map.72 = (f32[4,384]{1,0:T(4,128)S(1)}, f32[1,128]{1,0:T(1,128)S(1)}) custom-call(f32[4,288]{1,0:T(4,128)S(1)} %get-tuple-element.29.right, f32[4,288,288]{2,1,0:T(8,128)S(1)} %get-tuple-element.47.diagonal_tiles, f32[4,384]{1,0:T(4,128)S(1)} %get-tuple-element.45.image, f32[16,384]{1,0:T(8,128)S(1)} %get-tuple-element.46.swap, ...), custom_call_target="tpu_custom_call" | custom-call | flops 663552 | bytes 1327104 | tf_op jit(solution)/shard_map/pallas_call | solution.py:494
  16.4 0.8 %collective-permute-done.4.swapped = f32[16,384]{1,0:T(8,128)S(1)} collective-permute-done((f32[16,384]{1,0:T(8,128)S(1)}, f32[16,384]{1,0:T(8,128)S(1)}, u32[]{:S(2)}, u32[]{:S(2)}) %collective-permute-start.4) | collective-permute-done | bytes 24608 | tf_op jit(solution)/shard_map/ppermute | solution.py:442
  17.3 0.2 shard_map.73
  17.4 10.1 %all_to_all.5.gathered = f32[16,5,4,128]{3,2,1,0:T(4,128)S(1)} all-to-all(f32[16,5,4,128]{3,2,1,0:T(4,128)S(1)} %shard_map.73), channel_id=1, replica_groups={{22,20,18,16,30,28,26,24,6,4,2,0,14,12,10,8},{23,21,19,17,31,29,27,25,7..., dimensions={0} | all-to-all | bytes 327680 | tf_op jit(solution)/shard_map/all_to_all | solution.py:501
  27.6 0.0 collective-permute-start.5
  27.6 0.3 %shard_map.75.sums = f32[8,384]{1,0:T(8,128)S(1)} custom-call(f32[16,5,4,128]{3,2,1,0:T(4,128)S(1)} %all_to_all.5.gathered), custom_call_target="tpu_custom_call" | custom-call | flops 2654208 | bytes 5308416 | tf_op jit(solution)/shard_map/pallas_call | solution.py:504
  27.9 0.5 %collective-permute-start.6 = (f32[8,384]{1,0:T(8,128)S(1)}, f32[8,384]{1,0:T(8,128)S(1)}, u32[]{:S(2)}, u32[]{:S(2)}) collective-permute-start(f32[8,384]{1,0:T(8,128)S(1)} %shard_map.75.sums), channel_id=1, source_target_pairs={{0,1},{1,0},{2,3},{3,2},{4,5},{5,4},{6,7},{7,6},{8,9},{9,8},{10,11... | collective-permute-start | bytes 36872 | tf_op jit(solution)/shard_map/ppermute | solution.py:442
  28.4 0.1 shard_map.76
  28.5 0.2 collective-permute-done.5.next_other
  28.7 0.5 %shard_map.77.product = f32[4,384]{1,0:T(4,128)S(1)} custom-call(s32[4,4]{1,0:T(4,128)S(4)} %get-tuple-element.31.place, s32[4,4]{1,0:T(4,128)S(4)} %get-tuple-element.32.live, s32[4]{0:T(128)S(4)} %get-tuple-element.35.spot, f32[4,3,288,288]{3,2,1,0:T(8,128)S(1)} %get-tuple-element.33.tiles, f32[4,384]{1,0:T(4,128)S(1)} %get-tuple-element.52.known, ...), custom_call_target="tpu_custom_call" | custom-call | flops 265420800 | bytes 530841600 | tf_op jit(solution)/shard_map/pallas_call | solution.py:510
  29.2 0.0 collective-permute-done.6.sums_other
  29.2 0.6 %shard_map.78 = (f32[4,288]{1,0:T(4,128)}, f32[4,288]{1,0:T(4,128)}) custom-call(f32[4,288]{1,0:T(4,128)S(1)} %get-tuple-element.29.right, f32[4,384]{1,0:T(4,128)S(1)} %get-tuple-element.30.z.z_ref, f32[4,384]{1,0:T(4,128)S(1)} %get-tuple-element.45.image, f32[4,384]{1,0:T(4,128)S(1)} %shard_map.77.product, f32[4,384]{1,0:T(4,128)S(1)} %get-tuple-element.55.scaled, ...), custom_call_target="tpu_custom_call" | custom-call | tf_op jit(solution)/shard_map/pallas_call | solution.py:514
  (2 shorter events, 0.0 us)
Async XLA Ops:
  3.6 9.7 %collective-permute-start = (f32[4,384]{1,0:T(4,128)S(1)}, f32[4,384]{1,0:T(4,128)S(1)}, u32[]{:S(2)}, u32[]{:S(2)}) collective-permute-start(f32[4,384]{1,0:T(4,128)S(1)} %get-tuple-element.38), channel_id=1, source_target_pairs={{0,1},{1,2},{2,3},{3,4},{4,5},{5,6},{6,7},{7,8},{8,9},{9,10},{10,1... | collective-permute-start | bytes 18440 | tf_op jit(solution)/shard_map/ppermute | solution.py:476
  3.7 9.6 %collective-permute-start.1 = (f32[4,384]{1,0:T(4,128)S(1)}, f32[4,384]{1,0:T(4,128)S(1)}, u32[]{:S(2)}, u32[]{:S(2)}) collective-permute-start(f32[4,384]{1,0:T(4,128)S(1)} %get-tuple-element.39), channel_id=1, source_target_pairs={{0,30},{1,31},{2,4},{3,5},{4,2},{5,3},{6,8},{7,9},{8,6},{9,7},{10,... | collective-permute-start | bytes 18440 | tf_op jit(solution)/shard_map/ppermute | solution.py:450
  10.6 2.6 %collective-permute-start.2 = (f32[4,384]{1,0:T(4,128)S(1)}, f32[4,384]{1,0:T(4,128)S(1)}, u32[]{:S(2)}, u32[]{:S(2)}) collective-permute-start(f32[4,384]{1,0:T(4,128)S(1)} %get-tuple-element.40), channel_id=1, source_target_pairs={{1,0},{2,1},{3,2},{4,3},{5,4},{6,5},{7,6},{8,7},{9,8},{10,9},{11,1... | collective-permute-start | bytes 18440 | tf_op jit(solution)/shard_map/ppermute | solution.py:478
  11.2 3.6 %collective-permute-start.3 = (f32[4,384]{1,0:T(4,128)S(1)}, f32[4,384]{1,0:T(4,128)S(1)}, u32[]{:S(2)}, u32[]{:S(2)}) collective-permute-start(f32[4,384]{1,0:T(4,128)S(1)} %get-tuple-element.41), channel_id=1, source_target_pairs={{0,2},{1,3},{2,0},{3,1},{4,6},{5,7},{6,4},{7,5},{8,10},{9,11},{10,... | collective-permute-start | bytes 18440 | tf_op jit(solution)/shard_map/ppermute | solution.py:450
  16.0 1.3 %collective-permute-start.4 = (f32[16,384]{1,0:T(8,128)S(1)}, f32[16,384]{1,0:T(8,128)S(1)}, u32[]{:S(2)}, u32[]{:S(2)}) collective-permute-start(f32[16,384]{1,0:T(8,128)S(1)} %get-tuple-element.46.swap), channel_id=1, source_target_pairs={{0,1},{1,0},{2,3},{3,2},{4,5},{5,4},{6,7},{7,6},{8,9},{9,8},{10,11... | collective-permute-start | bytes 73736 | tf_op jit(solution)/shard_map/ppermute | solution.py:442
  27.6 1.2 %collective-permute-start.5 = (f32[5,4,128]{2,1,0:T(4,128)S(1)}, f32[5,4,128]{2,1,0:T(4,128)S(1)}, u32[]{:S(2)}, u32[]{:S(2)}) collective-permute-start(f32[5,4,128]{2,1,0:T(4,128)S(1)} %shard_map.74.next_part), channel_id=1, source_target_pairs={{0,1},{1,0},{2,3},{3,2},{4,5},{5,4},{6,7},{7,6},{8,9},{9,8},{10,11... | collective-permute-start | bytes 30728 | tf_op jit(solution)/shard_map/ppermute | solution.py:442
  27.9 1.4 %collective-permute-start.6 = (f32[8,384]{1,0:T(8,128)S(1)}, f32[8,384]{1,0:T(8,128)S(1)}, u32[]{:S(2)}, u32[]{:S(2)}) collective-permute-start(f32[8,384]{1,0:T(8,128)S(1)} %shard_map.75.sums), channel_id=1, source_target_pairs={{0,1},{1,0},{2,3},{3,2},{4,5},{5,4},{6,7},{7,6},{8,9},{9,8},{10,11... | collective-permute-start | bytes 36872 | tf_op jit(solution)/shard_map/ppermute | solution.py:442
